TPU v7x, 32 devices: a whole 2x2x4 slice. The times are simulated.
32 devices in a mesh: depth: 8 (over z, x), row: 4 (over y, core).
Axes of the slice: x: 2, y: 2, z: 4, core: 2. Of those that a mesh axis runs over, the one named last changes fastest.
Arguments:
- fields: bfloat16 [4, 64, 128, 256], P(None, 'depth', 'row'), may hold values from -48 to 48
- w_in: float32 [32, 12], replicated, may hold values from -1.75 to 1.75
- b_in: float32 [32], replicated, may hold values from -3 to 3
- w_out: float32 [4, 32], replicated, may hold values from -1 to 1
- b_out: float32 [4], replicated, may hold values from -6 to 6
Outputs:
- image: float32 [4, 128, 256], P(None, 'row')
All inputs are finite; a program needn't handle non-finite values.
Results may differ from a plain program's by a relative error of at most 0.00035.
Values may be sent and summed in bfloat16 or wider, within the bound.
No kernel may reach another device: no remote copies, remote signals or barrier semaphores. Data moves between devices by JAX's collectives and lax.ppermute only.
A program may use at most 64 MiB of HBM per device.

v0:
```python
import jax
import jax.numpy as jnp
import numpy as np
from jax import lax
from jax.sharding import PartitionSpec as P

smooth_taps = (1.0 / 64, 6.0 / 64, 15.0 / 64, 20.0 / 64, 15.0 / 64, 6.0 / 64, 1.0 / 64)
slope_taps = (-1.0 / 60, 9.0 / 60, -45.0 / 60, 0.0, 45.0 / 60, -9.0 / 60, 1.0 / 60)
depth_scale = 2.0


def with_halo(block, sides, width):
    for axis, dim in sides:
        count = lax.axis_size(axis)
        forward = [(i, i + 1) for i in range(count - 1)]
        backward = [(target, source) for source, target in forward]
        low = lax.ppermute(
            lax.slice_in_dim(block, block.shape[dim] - width, None, axis=dim), axis, forward
        )
        high = lax.ppermute(lax.slice_in_dim(block, 0, width, axis=dim), axis, backward)
        block = jnp.concatenate([low, block, high], axis=dim)
    return block


def swapped(x, axis, distance):
    return lax.ppermute(x, axis, [(i, i ^ 1 << distance) for i in range(lax.axis_size(axis))])


def filter_axis(values, taps, axis):
    count = values.shape[axis] - 6
    total = taps[0] * lax.slice_in_dim(values, 0, count, axis=axis)
    for place in range(1, 7):
        total = total + taps[place] * lax.slice_in_dim(values, place, place + count, axis=axis)
    return total


def smooth_block(block):
    along_z = filter_axis(block, smooth_taps, 1)
    along_y = filter_axis(along_z, smooth_taps, 2)
    padded = jnp.pad(along_y, ((0, 0), (0, 0), (0, 0), (3, 3)))
    return filter_axis(padded, smooth_taps, 3)


def shade(center, slope_y, slope_z, w_in, b_in, w_out, b_out, total_depth):
    depth_n = center.shape[1]
    features = jnp.concatenate([center, slope_y, slope_z], 0).reshape(12, -1)
    hidden = jnp.tanh(
        jnp.dot(w_in, features, precision=lax.Precision.HIGHEST, preferred_element_type=jnp.float32)
        + b_in[:, None]
    )
    out = (
        jnp.dot(w_out, hidden, precision=lax.Precision.HIGHEST, preferred_element_type=jnp.float32)
        + b_out[:, None]
    )
    rgb = jax.nn.sigmoid(out[0:3]).reshape(3, depth_n, -1)
    optical = (jax.nn.softplus(out[3]) * (depth_scale / total_depth)).reshape(depth_n, -1)
    alpha = 1.0 - jnp.exp(-optical)
    before = jnp.cumsum(optical, axis=0) - optical
    weight = jnp.exp(-before) * alpha
    color = jnp.sum(weight[None] * rgb, axis=1)
    through = jnp.exp(-jnp.sum(optical, axis=0))
    return jnp.concatenate([color, through[None]], 0)


def combine(front, back):
    color = front[..., 0:3, :] + front[..., 3:4, :] * back[..., 0:3, :]
    return jnp.concatenate([color, front[..., 3:4, :] * back[..., 3:4, :]], -2)


def local(fields, w_in, b_in, w_out, b_out):
    slab_depth = fields.shape[1]
    band_rows = fields.shape[2]
    columns = fields.shape[3]
    slabs = lax.axis_size("depth")
    total_depth = slab_depth * slabs
    total_rows = band_rows * lax.axis_size("row")
    extended = with_halo(fields, (("depth", 1), ("row", 2)), 6).astype(jnp.float32)
    smoothed = smooth_block(extended)
    zpos = lax.axis_index("depth") * slab_depth - 3 + lax.iota(jnp.int32, slab_depth + 6)
    ypos = lax.axis_index("row") * band_rows - 3 + lax.iota(jnp.int32, band_rows + 6)
    inside = ((zpos >= 0) & (zpos < total_depth))[:, None, None] & (
        (ypos >= 0) & (ypos < total_rows)
    )[None, :, None]
    smoothed = jnp.where(inside[None], smoothed, 0.0)
    center = smoothed[:, 3:-3, 3:-3, :]
    slope_z = filter_axis(smoothed[:, :, 3:-3, :], slope_taps, 1)
    slope_y = filter_axis(smoothed[:, 3:-3, :, :], slope_taps, 2)
    partial_image = shade(center, slope_y, slope_z, w_in, b_in, w_out, b_out, total_depth)
    levels = slabs.bit_length() - 1
    pixels = band_rows * columns
    segment = pixels // slabs
    myself = lax.axis_index("depth")
    current = partial_image
    for bit in range(levels):
        half = current.shape[1] // 2
        lower_half = current[:, :half]
        upper_half = current[:, half:]
        behind = jnp.right_shift(myself, bit) & 1 == 1
        keeping = jnp.where(behind, upper_half, lower_half)
        giving = jnp.where(behind, lower_half, upper_half)
        received = swapped(giving, "depth", bit)
        front = jnp.where(behind, received, keeping)
        back = jnp.where(behind, keeping, received)
        current = combine(front, back)
    order_list = []
    for place in range(slabs):
        reversed_index = 0
        for bit in range(levels):
            reversed_index = reversed_index + ((place >> bit & 1) << levels - 1 - bit)
        order_list.append(reversed_index)
    order = np.array(order_list, dtype=np.int32)
    whole = lax.all_gather(current, "depth", axis=1, tiled=True)
    arranged = whole.reshape(4, slabs, segment)[:, order, :].reshape(4, pixels)
    image = jnp.concatenate([arranged[0:3], 1.0 - arranged[3:4]], 0)
    return image.reshape(4, band_rows, columns)


def solution(mesh):
    return jax.shard_map(
        local,
        mesh=mesh,
        in_specs=(P(None, "depth", "row", None), P(), P(), P(), P()),
        out_specs=P(None, "row", None),
        check_vma=False,
    )
```

profile of v0, /device:TPU:4, one launch (start us, length us, event | category | flops | bytes accessed | tf_op | source)
XLA Modules:
  0.0 108.3 jit_solution(15603889699609578604)
XLA Ops:
  0.0 1.2 %fusion.54 = (bf16[4,6,32,256]{3,2,1,0:T(8,128)(2,1)S(1)}, bf16[4,6,32,256]{3,2,1,0:T(8,128)(2,1)S(1)}) fusion(bf16[4,8,32,256]{3,2,1,0:T(8,128)(2,1)} %param.7), kind=kLoop, calls=%fused_computation.134 | loop fusion | bytes 1572864 | tf_op jit(solution)/shard_map/slice | solution.py:20
  1.2 3.4 %collective-permute-start = (bf16[4,6,32,256]{3,2,1,0:T(8,128)(2,1)S(1)}, bf16[4,6,32,256]{3,2,1,0:T(8,128)(2,1)S(1)}, u32[]{:S(2)}, u32[]{:S(2)}) collective-permute-start(bf16[4,6,32,256]{3,2,1,0:T(8,128)(2,1)S(1)} %get-tuple-element.17), channel_id=1, source_target_pairs={{0,4},{4,8},{8,12},{12,16},{16,20},{20,24},{24,28},{1,5},{5,9},{9,... | collective-permute-start | bytes 1179656 | tf_op jit(solution)/shard_map/ppermute | solution.py:17
  4.7 1.3 %collective-permute-start.1 = (bf16[4,6,32,256]{3,2,1,0:T(8,128)(2,1)S(1)}, bf16[4,6,32,256]{3,2,1,0:T(8,128)(2,1)S(1)}, u32[]{:S(2)}, u32[]{:S(2)}) collective-permute-start(bf16[4,6,32,256]{3,2,1,0:T(8,128)(2,1)S(1)} %get-tuple-element.16), channel_id=1, source_target_pairs={{4,0},{8,4},{12,8},{16,12},{20,16},{24,20},{28,24},{5,1},{9,5},{13... | collective-permute-start | bytes 1179656 | tf_op jit(solution)/shard_map/ppermute | solution.py:20
  6.0 15.4 %collective-permute-done = bf16[4,6,32,256]{3,2,1,0:T(8,128)(2,1)S(1)} collective-permute-done((bf16[4,6,32,256]{3,2,1,0:T(8,128)(2,1)S(1)}, bf16[4,6,32,256]{3,2,1,0:T(8,128)(2,1)S(1)}, u32[]{:S(2)}, u32[]{:S(2)}) %collective-permute-start) | collective-permute-done | bytes 393248 | tf_op jit(solution)/shard_map/ppermute | solution.py:17
  21.7 1.9 %collective-permute-start.2 = (bf16[4,20,6,256]{3,2,1,0:T(8,128)(2,1)S(1)}, bf16[4,20,6,256]{3,2,1,0:T(8,128)(2,1)S(1)}, u32[]{:S(2)}, u32[]{:S(2)}) collective-permute-start(bf16[4,20,6,256]{3,2,1,0:T(8,128)(2,1)S(1)} %get-tuple-element.14), channel_id=1, source_target_pairs={{0,1},{1,2},{2,3},{4,5},{5,6},{6,7},{8,9},{9,10},{10,11},{12,13},{... | collective-permute-start | bytes 737288 | tf_op jit(solution)/shard_map/ppermute | solution.py:17
  23.6 3.6 %collective-permute-start.3 = (bf16[4,20,6,256]{3,2,1,0:T(8,128)(2,1)S(1)}, bf16[4,20,6,256]{3,2,1,0:T(8,128)(2,1)S(1)}, u32[]{:S(2)}, u32[]{:S(2)}) collective-permute-start(bf16[4,20,6,256]{3,2,1,0:T(8,128)(2,1)S(1)} %get-tuple-element.15), channel_id=1, source_target_pairs={{1,0},{2,1},{3,2},{5,4},{6,5},{7,6},{9,8},{10,9},{11,10},{13,12},{... | collective-permute-start | bytes 737288 | tf_op jit(solution)/shard_map/ppermute | solution.py:20
  27.3 2.7 %collective-permute-done.2 = bf16[4,20,6,256]{3,2,1,0:T(8,128)(2,1)S(1)} collective-permute-done((bf16[4,20,6,256]{3,2,1,0:T(8,128)(2,1)S(1)}, bf16[4,20,6,256]{3,2,1,0:T(8,128)(2,1)S(1)}, u32[]{:S(2)}, u32[]{:S(2)}) %collective-permute-start.2) | collective-permute-done | bytes 245792 | tf_op jit(solution)/shard_map/ppermute | solution.py:17
  30.0 1.8 %collective-permute-done.3 = bf16[4,20,6,256]{3,2,1,0:T(8,128)(2,1)S(1)} collective-permute-done((bf16[4,20,6,256]{3,2,1,0:T(8,128)(2,1)S(1)}, bf16[4,20,6,256]{3,2,1,0:T(8,128)(2,1)S(1)}, u32[]{:S(2)}, u32[]{:S(2)}) %collective-permute-start.3) | collective-permute-done | bytes 245792 | tf_op jit(solution)/shard_map/ppermute | solution.py:20
  31.8 0.9 maximum_convert_fusion
  32.7 2.2 %fusion.2 = f32[4,14,44,256]{3,2,1,0:T(8,128)S(1)} fusion(f32[4,20,44,256]{3,2,1,0:T(8,128)S(1)} %maximum_convert_fusion), kind=kLoop, calls=%fused_computation.13 | loop fusion | flops 8200192 | bytes 20185088 | tf_op jit(solution)/shard_map/add | solution.py:33
  35.0 1.9 %fusion.21 = f32[4,14,38,256]{3,2,1,0:T(8,128)S(1)} fusion(f32[4,14,44,256]{3,2,1,0:T(8,128)S(1)} %fusion.2), kind=kLoop, calls=%fused_computation.39 | loop fusion | flops 7081984 | bytes 17432576 | tf_op jit(solution)/shard_map/add | solution.py:33
  36.9 4.0 %fusion.15 = f32[4,14,38,256]{3,2,1,0:T(8,128)S(1)} fusion(f32[4,14,38,256]{3,2,1,0:T(8,128)S(1)} %fusion.21, pred[14,38]{1,0:T(8,128)(4,1)S(1)} %broadcast_and_fusion), kind=kLoop, calls=%fused_computation.32 | loop fusion | flops 7626752 | bytes 4358676 | tf_op jit(solution)/shard_map/jit(_where)/select_n | solution.py:84
  40.9 1.5 %fusion.52 = (f32[4,8,32,256]{3,2,1,0:T(8,128)S(1)}, f32[4,8,32,256]{3,2,1,0:T(8,128)S(1)}, f32[4,8,32,256]{3,2,1,0:T(8,128)S(1)}) fusion(f32[4,14,38,256]{3,2,1,0:T(8,128)S(1)} %fusion.15), kind=kLoop, calls=%fused_computation.132 | loop fusion | flops 6553600 | bytes 16777216 | tf_op jit(solution)/shard_map/slice | solution.py:85
  43.0 2.4 %copy.9 = f32[2,8,256,256]{3,1,2,0:T(8,128)S(1)} copy(f32[2,8,256,256]{3,2,1,0:T(8,128)S(1)} %bitcast.23) | data formatting | bytes 8388608
  45.5 7.5 %fusion = f32[65536,32]{0,1:T(8,128)S(1)} fusion(f32[12,65536]{1,0:T(8,128)S(1)} %bitcast.22, f32[32,12]{0,1:T(8,128)S(1)} %copy-done, f32[32]{0:T(128)S(1)} %copy-done.2), kind=kOutput, calls=%fused_computation.2 | convolution fusion | flops 304087040 | bytes 11536000 | tf_op jit(solution)/shard_map/dot_general | solution.py:48
  53.0 4.8 %fusion.1 = f32[4,65536]{1,0:T(4,128)S(1)} fusion(f32[65536,32]{0,1:T(8,128)S(1)} %fusion, f32[4,32]{1,0:T(4,128)S(1)} %copy-done.3, f32[4]{0:T(128)S(1)} %copy-done.4), kind=kOutput, calls=%fused_computation.4 | convolution fusion | flops 100925440 | bytes 9437712 | tf_op jit(solution)/shard_map/dot_general | solution.py:52
  57.8 0.8 slice_reduce_fusion
  60.7 2.5 %collective-permute-start.4 = (f32[4,4096]{1,0:T(4,128)S(1)}, f32[4,4096]{1,0:T(4,128)S(1)}, u32[]{:S(2)}, u32[]{:S(2)}) collective-permute-start(f32[4,4096]{1,0:T(4,128)S(1)} %get-tuple-element.9), channel_id=1, source_target_pairs={{0,4},{4,0},{8,12},{12,8},{16,20},{20,16},{24,28},{28,24},{1,5},{5... | collective-permute-start | bytes 196616 | tf_op jit(solution)/shard_map/ppermute | solution.py:26
  63.2 2.2 %collective-permute-done.4 = f32[4,4096]{1,0:T(4,128)S(1)} collective-permute-done((f32[4,4096]{1,0:T(4,128)S(1)}, f32[4,4096]{1,0:T(4,128)S(1)}, u32[]{:S(2)}, u32[]{:S(2)}) %collective-permute-start.4) | collective-permute-done | bytes 65568 | tf_op jit(solution)/shard_map/ppermute | solution.py:26
  65.6 3.0 %collective-permute-start.5 = (f32[4,2048]{1,0:T(4,128)S(1)}, f32[4,2048]{1,0:T(4,128)S(1)}, u32[]{:S(2)}, u32[]{:S(2)}) collective-permute-start(f32[4,2048]{1,0:T(4,128)S(1)} %get-tuple-element.7), channel_id=1, source_target_pairs={{0,8},{4,12},{8,0},{12,4},{16,24},{20,28},{24,16},{28,20},{1,9},{5... | collective-permute-start | bytes 98312 | tf_op jit(solution)/shard_map/ppermute | solution.py:26
  68.6 1.9 %collective-permute-done.5 = f32[4,2048]{1,0:T(4,128)S(1)} collective-permute-done((f32[4,2048]{1,0:T(4,128)S(1)}, f32[4,2048]{1,0:T(4,128)S(1)}, u32[]{:S(2)}, u32[]{:S(2)}) %collective-permute-start.5) | collective-permute-done | bytes 32800 | tf_op jit(solution)/shard_map/ppermute | solution.py:26
  70.6 3.1 %collective-permute-start.6 = (f32[4,1024]{1,0:T(4,128)S(1)}, f32[4,1024]{1,0:T(4,128)S(1)}, u32[]{:S(2)}, u32[]{:S(2)}) collective-permute-start(f32[4,1024]{1,0:T(4,128)S(1)} %get-tuple-element.5), channel_id=1, source_target_pairs={{0,16},{4,20},{8,24},{12,28},{16,0},{20,4},{24,8},{28,12},{1,17},{... | collective-permute-start | bytes 49160 | tf_op jit(solution)/shard_map/ppermute | solution.py:26
  73.7 1.7 %collective-permute-done.6 = f32[4,1024]{1,0:T(4,128)S(1)} collective-permute-done((f32[4,1024]{1,0:T(4,128)S(1)}, f32[4,1024]{1,0:T(4,128)S(1)}, u32[]{:S(2)}, u32[]{:S(2)}) %collective-permute-start.6) | collective-permute-done | bytes 16416 | tf_op jit(solution)/shard_map/ppermute | solution.py:26
  75.5 31.3 %all_gather.3 = f32[4,8192]{1,0:T(4,128)S(1)} all-gather(f32[4,1024]{1,0:T(4,128)S(1)} %pad_maximum_fusion.5), channel_id=1, replica_groups=mesh['depth'=8,'row'=4] {'depth'}, dimensions={1}, use_global_device_ids=true | all-gather | bytes 147456 | tf_op jit(solution)/shard_map/all_gather | solution.py:112
  (49 shorter events, 4.7 us)
Async XLA Ops:
  0.0 45.4 %copy-start = (f32[32,12]{0,1:T(8,128)S(1)}, f32[32,12]{0,1:T(8,128)}, u32[]{:S(2)}) copy-start(f32[32,12]{0,1:T(8,128)} %param.8) | copy-start | bytes 4612
  0.0 21.4 %copy-start.1 = (bf16[4,8,32,256]{3,2,1,0:T(8,128)(2,1)S(1)}, bf16[4,8,32,256]{3,2,1,0:T(8,128)(2,1)}, u32[]{:S(2)}) copy-start(bf16[4,8,32,256]{3,2,1,0:T(8,128)(2,1)} %param.7) | copy-start | bytes 1572868
  1.2 20.2 %collective-permute-start = (bf16[4,6,32,256]{3,2,1,0:T(8,128)(2,1)S(1)}, bf16[4,6,32,256]{3,2,1,0:T(8,128)(2,1)S(1)}, u32[]{:S(2)}, u32[]{:S(2)}) collective-permute-start(bf16[4,6,32,256]{3,2,1,0:T(8,128)(2,1)S(1)} %get-tuple-element.17), channel_id=1, source_target_pairs={{0,4},{4,8},{8,12},{12,16},{16,20},{20,24},{24,28},{1,5},{5,9},{9,... | collective-permute-start | bytes 1179656 | tf_op jit(solution)/shard_map/ppermute | solution.py:17
  4.7 16.8 %collective-permute-start.1 = (bf16[4,6,32,256]{3,2,1,0:T(8,128)(2,1)S(1)}, bf16[4,6,32,256]{3,2,1,0:T(8,128)(2,1)S(1)}, u32[]{:S(2)}, u32[]{:S(2)}) collective-permute-start(bf16[4,6,32,256]{3,2,1,0:T(8,128)(2,1)S(1)} %get-tuple-element.16), channel_id=1, source_target_pairs={{4,0},{8,4},{12,8},{16,12},{20,16},{24,20},{28,24},{5,1},{9,5},{13... | collective-permute-start | bytes 1179656 | tf_op jit(solution)/shard_map/ppermute | solution.py:20
  21.7 8.4 %collective-permute-start.2 = (bf16[4,20,6,256]{3,2,1,0:T(8,128)(2,1)S(1)}, bf16[4,20,6,256]{3,2,1,0:T(8,128)(2,1)S(1)}, u32[]{:S(2)}, u32[]{:S(2)}) collective-permute-start(bf16[4,20,6,256]{3,2,1,0:T(8,128)(2,1)S(1)} %get-tuple-element.14), channel_id=1, source_target_pairs={{0,1},{1,2},{2,3},{4,5},{5,6},{6,7},{8,9},{9,10},{10,11},{12,13},{... | collective-permute-start | bytes 737288 | tf_op jit(solution)/shard_map/ppermute | solution.py:17
  23.6 8.2 %collective-permute-start.3 = (bf16[4,20,6,256]{3,2,1,0:T(8,128)(2,1)S(1)}, bf16[4,20,6,256]{3,2,1,0:T(8,128)(2,1)S(1)}, u32[]{:S(2)}, u32[]{:S(2)}) collective-permute-start(bf16[4,20,6,256]{3,2,1,0:T(8,128)(2,1)S(1)} %get-tuple-element.15), channel_id=1, source_target_pairs={{1,0},{2,1},{3,2},{5,4},{6,5},{7,6},{9,8},{10,9},{11,10},{13,12},{... | collective-permute-start | bytes 737288 | tf_op jit(solution)/shard_map/ppermute | solution.py:20
  43.0 2.5 %copy-start.2 = (f32[32]{0:T(128)S(1)}, f32[32]{0:T(128)}, u32[]{:S(2)}) copy-start(f32[32]{0:T(128)} %param.9) | copy-start | bytes 388
  45.5 7.5 %copy-start.3 = (f32[4,32]{1,0:T(4,128)S(1)}, f32[4,32]{1,0:T(4,128)}, u32[]{:S(2)}) copy-start(f32[4,32]{1,0:T(4,128)} %param.10) | copy-start | bytes 1540
  45.5 7.5 %copy-start.4 = (f32[4]{0:T(128)S(1)}, f32[4]{0:T(128)}, u32[]{:S(2)}) copy-start(f32[4]{0:T(128)} %param.11) | copy-start | bytes 52
  59.3 14.4 %copy-start.5 = (s32[8]{0:T(128)S(1)}, s32[8]{0:T(128)}, u32[]{:S(2)}) copy-start(s32[8]{0:T(128)} %constant.78) | copy-start | bytes 100
  60.7 4.8 %collective-permute-start.4 = (f32[4,4096]{1,0:T(4,128)S(1)}, f32[4,4096]{1,0:T(4,128)S(1)}, u32[]{:S(2)}, u32[]{:S(2)}) collective-permute-start(f32[4,4096]{1,0:T(4,128)S(1)} %get-tuple-element.9), channel_id=1, source_target_pairs={{0,4},{4,0},{8,12},{12,8},{16,20},{20,16},{24,28},{28,24},{1,5},{5... | collective-permute-start | bytes 196616 | tf_op jit(solution)/shard_map/ppermute | solution.py:26
  65.6 4.9 %collective-permute-start.5 = (f32[4,2048]{1,0:T(4,128)S(1)}, f32[4,2048]{1,0:T(4,128)S(1)}, u32[]{:S(2)}, u32[]{:S(2)}) collective-permute-start(f32[4,2048]{1,0:T(4,128)S(1)} %get-tuple-element.7), channel_id=1, source_target_pairs={{0,8},{4,12},{8,0},{12,4},{16,24},{20,28},{24,16},{28,20},{1,9},{5... | collective-permute-start | bytes 98312 | tf_op jit(solution)/shard_map/ppermute | solution.py:26
  70.6 4.8 %collective-permute-start.6 = (f32[4,1024]{1,0:T(4,128)S(1)}, f32[4,1024]{1,0:T(4,128)S(1)}, u32[]{:S(2)}, u32[]{:S(2)}) collective-permute-start(f32[4,1024]{1,0:T(4,128)S(1)} %get-tuple-element.5), channel_id=1, source_target_pairs={{0,16},{4,20},{8,24},{12,28},{16,0},{20,4},{24,8},{28,12},{1,17},{... | collective-permute-start | bytes 49160 | tf_op jit(solution)/shard_map/ppermute | solution.py:26
where the time goes:
time: 109 us; the launch traced here: 108 us
  blocking collectives  31.3 us (29%)
  waiting for transfers between devices  25.8 us (24%)
  starting transfers between devices  18.9 us (17%)
  other arithmetic  13.9 us (13%)
  matrix products  12.3 us (11%)
  local copies, waits for them, and re-layouts  5.8 us (5%)
    all_gather x1, blocking collectives, local(): whole = lax.all_gather(current, 'depth', axis=1, tiled=True)  31.3 us
    ppermute x2, waiting for transfers between devices, with_halo(): lax.ppermute(lax.slice_in_dim(block, block.shape[dim] - width, None, axis...  18.2 us
    ppermute x3, starting transfers between devices, swapped(): lax.ppermute(x, axis, [(i, i ^ 1 << distance) for i in range(lax.axis_siz...  8.61 us
    dot_general x1, matrix products, shade(): jnp.dot(w_in, features, precision=lax.Precision.HIGHEST, preferred_elemen...  7.51 us
    ppermute x3, waiting for transfers between devices, swapped(): lax.ppermute(x, axis, [(i, i ^ 1 << distance) for i in range(lax.axis_siz...  5.85 us
    ppermute x2, starting transfers between devices, with_halo(): lax.ppermute(lax.slice_in_dim(block, block.shape[dim] - width, None, axis...  5.34 us
    ppermute x2, starting transfers between devices, with_halo(): lax.ppermute(lax.slice_in_dim(block, 0, width, axis=dim), axis, backward)  4.93 us
    dot_general x1, matrix products, shade(): jnp.dot(w_out, hidden, precision=lax.Precision.HIGHEST, preferred_element...  4.75 us
  transfers between devices with their start and end apart: 7, of which 6 were waited for; matrix products, arithmetic and copies ran while one was open for 0% of the time, Pallas kernels for 0%

commit v1 on v0

v1 whole, which is shorter than its diff:
```python
import functools

import jax
import jax.numpy as jnp
from jax import lax
from jax.experimental import pallas as pl
from jax.experimental.pallas import tpu as pltpu
from jax.sharding import PartitionSpec as P

FIELDS = 4
HALO = 6
LANES = 128
HIGHEST = lax.Precision.HIGHEST
F32 = jnp.float32
BF16 = jnp.bfloat16
depth_scale = 2.0
smooth_counts = (20.0, 15.0, 6.0, 1.0)
slope_counts = ((1, 45.0), (2, -9.0), (3, 1.0))


def dot(a, b, precision=None):
    return jnp.dot(a, b, preferred_element_type=F32, precision=precision)


def iota(shape, dim):
    return lax.broadcasted_iota(jnp.int32, shape, dim)


def smooth_count(distance):
    d = jnp.abs(distance)
    out = jnp.where(d == 0, smooth_counts[0], 0.0)
    for place in (1, 2, 3):
        out = jnp.where(d == place, smooth_counts[place], out)
    return out.astype(F32)


def split(x):
    high = x.astype(BF16)
    return high, (x - high.astype(F32)).astype(BF16)


def pack_kernel(fields, mine, theirs, straight, diagonal, left, right):
    side = lax.axis_index("depth") & 1
    layers, rows = fields.shape[1], fields.shape[2]
    kw, kh = layers * FIELDS, HALO * FIELDS
    for layer in range(layers):
        for field in range(FIELDS):
            plane = fields[field, layer].astype(F32)
            place = pl.ds(layer * FIELDS + field, rows, stride=kw)
            left[place, :] = plane[:, :LANES]
            right[place, :] = plane[:, LANES:]
    lane = iota((kw, LANES), 1)
    shift = pl.multiple_of(side * (kw - kh), 8)

    def halves(row, start, count):
        a = left[pl.ds(row * kw + start, count), :]
        b = right[pl.ds(row * kw + start, count), :]
        return jnp.where(side == 0, a, b), jnp.where(side == 0, b, a)

    extra_low = jnp.zeros((kw, LANES), F32)
    extra_high = jnp.zeros((kw, LANES), F32)
    for row in range(0, rows, 2):
        pairs = []
        for r in (row, row + 1):
            a = left[pl.ds(r * kw, kw), :]
            b = right[pl.ds(r * kw, kw), :]
            inside = (lane >= 3 * r) & (lane < 3 * r + 3)
            extra_low = jnp.where(inside, pltpu.roll(b, (3 * r) % LANES, 1), extra_low)
            extra_high = jnp.where(inside, pltpu.roll(a, (3 * r + 3) % LANES, 1), extra_high)
            own = jnp.where(side == 0, a, b)
            other = jnp.where(side == 0, b, a)
            mine[pl.ds(r * kw, kw), :] = own.astype(BF16)
            theirs[pl.ds(r * kw, kw), :] = other.astype(BF16)
            pairs.append(halves(r, shift, kh))
        both = pl.ds(row * kh, 2 * kh)
        straight[both, :] = jnp.concatenate([pairs[0][0], pairs[1][0]], 0).astype(BF16)
        diagonal[both, :] = jnp.concatenate([pairs[0][1], pairs[1][1]], 0).astype(BF16)
    own = jnp.where(side == 0, extra_low, extra_high)
    other = jnp.where(side == 0, extra_high, extra_low)
    mine[rows * kw :, :] = own.astype(BF16)
    theirs[rows * kw :, :] = other.astype(BF16)
    empty = jnp.zeros((kw - kh, LANES), F32)
    for source, target in ((own, straight), (other, diagonal)):
        part = jnp.where(side == 0, source[:kh], source[kw - kh :])
        target[rows * kh :, :] = jnp.concatenate([part, empty], 0).astype(BF16)


def band_kernel(mine, swap, straight, diagonal, first, second):
    odd = lax.axis_index("row") & 1
    kw = 8 * FIELDS
    rows = mine.shape[0] // kw - 1
    for out, from_end in ((first, 1 - odd), (second, odd)):
        at, extra = 0, HALO * sum(r.shape[0] // (rows + 1) for r in (mine, swap)) + 2 * HALO * HALO * FIELDS
        for source in (mine, swap, straight, diagonal):
            width = kw if source.shape[0] == (rows + 1) * kw else HALO * FIELDS
            start = pl.multiple_of(from_end * (rows - HALO) * width, 16)
            out[at : at + HALO * width, :] = source[pl.ds(start, HALO * width), :]
            out[extra : extra + 32, :] = source[rows * width : rows * width + 32, :]
            at += HALO * width
            extra += 32


def weights_kernel(params, w1, w2a, w2b, bias2, *, layers, hidden, slabs):
    depth = lax.axis_index("depth")
    side = depth & 1
    base = (depth - side) * layers
    total = slabs * layers
    zs = 2 * layers
    kk = (2 * layers + 2 * HALO) * FIELDS
    width = w1.shape[1] // 3
    table = params[0:hidden, :]
    row, col = iota((LANES, width), 0), iota((LANES, width), 1)
    field = col & 3
    pick1 = jnp.where(col < kk, field, jnp.where(col < 2 * kk, field + 4, jnp.where(col == 2 * kk, 12, -1)))
    pick2 = jnp.where(col < kk, field + 8, -1)
    part1 = dot(table, (row == pick1).astype(F32), HIGHEST)
    part2 = dot(table, (row == pick2).astype(F32), HIGHEST)
    kappa = iota((hidden, width), 1)
    slot = jnp.where(kappa < kk, kappa, kappa - kk) >> 2
    low, high = slot - 4 * layers // 2 - HALO, slot - 2 * layers
    zk = jnp.where(slot < layers, side * layers + slot, (1 - side) * layers + slot - layers)
    below, above = 2 * layers, -HALO
    zk = jnp.where(slot >= 2 * layers, high + jnp.where(side == 0, below, above), zk)
    zk = jnp.where(slot >= 2 * layers + HALO, low + jnp.where(side == 0, above, below), zk)
    scale = 1.0 / 64.0**3
    for z in range(zs):
        distance = zk - z
        center = smooth_count(distance) * scale
        slope = jnp.zeros((hidden, width), F32)
        for offset, count in slope_counts:
            for sign in (1, -1):
                at = base + z + sign * offset
                inside = ((at >= 0) & (at < total)).astype(F32)
                slope = slope + (inside * (sign * count)) * smooth_count(distance - sign * offset)
        center = jnp.where(kappa < kk, center, jnp.where(kappa < 2 * kk, center * (1.0 / 60.0), 1.0))
        high_part, low_part = split(center * part1 + (slope * (scale / 60.0)) * part2)
        at = pl.ds(z * hidden, hidden)
        w1[at, 0:width] = high_part
        w1[at, width : 2 * width] = low_part
        w1[at, 2 * width :] = high_part
    outs = FIELDS * layers
    rr, cc = iota((outs, LANES), 0), iota((outs, LANES), 1)
    group = layers * hidden
    source = params[hidden : hidden + 8, :]
    rows8 = iota((outs, 8), 0) // layers == iota((outs, 8), 1)
    spread = dot(rows8.astype(F32), source, HIGHEST)
    across = iota((LANES, group), 0) == (iota((LANES, group), 1) & (hidden - 1))
    full = dot(spread, across.astype(F32), HIGHEST)
    diagonal = (iota((outs, group), 0) & (layers - 1)) == iota((outs, group), 1) // hidden
    high_part, low_part = split(jnp.where(diagonal, full, 0.0))
    w2a[0:outs, :] = high_part
    w2a[outs:, :] = low_part
    w2b[...] = high_part
    bias = jnp.sum(jnp.where(cc == hidden, spread, 0.0), axis=1, keepdims=True)
    bias2[...] = jnp.broadcast_to(bias, bias2.shape)


def shade_kernel(mine, swap, straight, diagonal, first, second, w1, w2a, w2b, bias2, out, grid, edge, xhi, xlo, *, layers, rows):
    side = lax.axis_index("depth") & 1
    band = lax.axis_index("row")
    bands = lax.axis_size("row")
    odd = band & 1
    kw, kh = layers * FIELDS, HALO * FIELDS
    kk = 2 * (kw + kh)
    offsets = ((mine, 0, kw), (swap, kw, kw), (straight, 2 * kw, kh), (diagonal, 2 * kw + kh, kh))
    i, j = iota((LANES, LANES), 0), iota((LANES, LANES), 1)
    taps = smooth_count(i - j).astype(BF16)
    ir, ic = i // 3, i % 3
    spot = jnp.where(side == 0, (j + 3) & (LANES - 1), j)
    jr, jc = spot // 3, spot % 3
    apart = jnp.where(side == 0, ic - jc + 3, jc - ic + 3)
    border = jnp.where((ir == jr) & (i < 3 * rows) & (spot < 3 * rows), smooth_count(apart), 0.0).astype(BF16)
    for source, at, width in offsets:
        filtered = dot(source[0 : rows * width, :], taps)
        grid[HALO : HALO + rows, at : at + width, :] = filtered.reshape(rows, width, LANES)
        edge[0, at : at + width, :] = dot(source[rows * width : rows * width + 32, :], border)[:width]
    far = HALO + rows
    for source, base, which in ((first, odd, 2 - odd), (second, 1 - odd, 1 + odd)):
        place = (1 - base) * far
        start, extra = 0, HALO * kk
        filtered = dot(source[0 : HALO * kk, :], taps)
        edges = dot(source[HALO * kk :, :], border)
        for index, (unused, at, width) in enumerate(offsets):
            piece = filtered[start : start + HALO * width].reshape(HALO, width, LANES)
            grid[pl.ds(place, HALO), at : at + width, :] = piece
            edge[which, at : at + width, :] = edges[index * 32 : index * 32 + width]
            start += HALO * width
    lane = iota((16, LANES), 1)
    near = ((lane + jnp.where(side == 0, 3, 0)) & (LANES - 1)) < 3
    above = (band > 0).astype(F32)
    below = (band < bands - 1).astype(F32)

    def filter_rows(group, carry):
        at = pl.ds(pl.multiple_of(group * 16, 16), 16)
        after = pl.ds(pl.multiple_of(group * 16 + kk, 16), 16)
        edges = [edge[k, at, :] for k in range(3)]
        chain = [None] * 6
        ring = []
        for r in range(rows + 2 * HALO):
            which = 1 if r < HALO else 0 if r < HALO + rows else 2
            own_row = (r - HALO) % rows
            turned = pltpu.roll(edges[which], (-3 * own_row) % LANES, 1)
            value = grid[r, at, :] + jnp.where(near, turned, 0.0)
            for level in range(6):
                previous, chain[level] = chain[level], value
                if previous is None:
                    value = None
                    break
                value = previous + value
            if value is None:
                continue
            y = r - HALO - 3
            if y < 0:
                value = value * above
            elif y >= rows:
                value = value * below
            ring.append(value)
            if len(ring) == 7:
                slope = (ring[6] - ring[0]) - 9.0 * (ring[5] - ring[1]) + 45.0 * (ring[4] - ring[2])
                y -= 3
                xhi[y, at, :], xlo[y, at, :] = split(ring[3])
                xhi[y, after, :], xlo[y, after, :] = split(slope)
                ring.pop(0)
        return carry

    lax.fori_loop(0, kk // 16, filter_rows, 0)
    rest = xhi.shape[1] - 2 * kk
    ones = jnp.where(iota((rest, LANES), 0) == 0, 1.0, 0.0).astype(BF16)
    for y in range(rows):
        xhi[y, 2 * kk :, :] = ones
        xlo[y, 2 * kk :, :] = jnp.zeros((rest, LANES), BF16)
    wide = 2 * LANES
    outs = FIELDS * layers
    group = w2a.shape[1]
    sub = iota((layers, wide), 0)
    scale = depth_scale / (lax.axis_size("depth") * layers)

    def shade(pair, carry):
        y = 2 * pair
        high = jnp.concatenate([xhi[y], xhi[y + 1]], 1)
        low = jnp.concatenate([xlo[y], xlo[y + 1]], 1)
        stacked = jnp.concatenate([high, high, low], 0)
        total = jnp.zeros((1, wide), F32)
        front = jnp.ones((1, wide), F32)
        color = [jnp.zeros((layers, wide), F32) for unused in range(3)]
        for half in range(2):
            hidden = jnp.tanh(dot(w1[half * group : (half + 1) * group, :], stacked))
            hidden_high, hidden_low = split(hidden)
            o = dot(w2a[...], hidden_high)
            o = o[:outs] + o[outs:] + dot(w2b[...], hidden_low) + bias2[...]
            x = o[3 * layers :]
            optical = (jnp.maximum(x, 0.0) + jnp.log1p(jnp.exp(-jnp.abs(x)))) * scale
            through = optical
            for step in (1, 2, 4):
                through = through + jnp.where(sub >= step, pltpu.roll(through, step, 0), 0.0)
            through = through + total
            total = through[layers - 1 :]
            after = jnp.exp(-through)
            before = jnp.where(sub == 0, front, pltpu.roll(after, 1, 0))
            front = after[layers - 1 :]
            weight = before - after
            for c in range(3):
                color[c] = color[c] + weight / (1.0 + jnp.exp(-o[c * layers : (c + 1) * layers]))
        for c in range(3):
            line = jnp.sum(color[c], axis=0, keepdims=True)
            out[c, pl.ds(y, 1), :] = line[:, :LANES]
            out[c, pl.ds(y + 1, 1), :] = line[:, LANES:]
        out[3, pl.ds(y, 1), :] = front[:, :LANES]
        out[3, pl.ds(y + 1, 1), :] = front[:, LANES:]
        return carry

    lax.fori_loop(0, rows // 2, shade, 0)


def call(kernel, out_shape, operands, scratch=(), flops=0, name=None):
    vmem = pl.BlockSpec(memory_space=pltpu.VMEM)
    return pl.pallas_call(
        kernel,
        out_shape=out_shape,
        in_specs=[vmem] * len(operands),
        out_specs=jax.tree.map(lambda unused: vmem, out_shape),
        scratch_shapes=list(scratch),
        compiler_params=pltpu.CompilerParams(vmem_limit_bytes=40 * 2**20),
        cost_estimate=pl.CostEstimate(flops=flops, bytes_accessed=2**20, transcendentals=0),
        name=name,
    )(*operands)


def combine(front, back):
    color = front[0:3] + front[3:4] * back[0:3]
    return jnp.concatenate([color, front[3:4] * back[3:4]], 0)


def local(fields, w_in, b_in, w_out, b_out):
    layers, rows, columns = fields.shape[1:]
    hidden = w_in.shape[0]
    slabs = lax.axis_size("depth")
    bands = lax.axis_size("row")
    me = lax.axis_index("depth")
    side = me & 1
    kw, kh = layers * FIELDS, HALO * FIELDS
    kk = 2 * (kw + kh)
    shape = jax.ShapeDtypeStruct
    mine, theirs, own_halo, other_halo = call(
        pack_kernel,
        [
            shape(((rows + 1) * kw, LANES), BF16),
            shape(((rows + 1) * kw, LANES), BF16),
            shape((rows * kh + kw, LANES), BF16),
            shape((rows * kh + kw, LANES), BF16),
        ],
        (fields,),
        [pltpu.VMEM((rows * kw, LANES), F32)] * 2,
        name="pack",
    )
    swap_pairs = [(i, i ^ 1) for i in range(slabs)]
    odd, even = range(1, slabs, 2), range(0, slabs, 2)
    diagonal_pairs = [(i, i + 1) for i in odd if i + 1 < slabs] + [(i, i - 1) for i in even if i]
    straight_pairs = [(i, i + 2) for i in odd if i + 2 < slabs] + [(i, i - 2) for i in even if i]
    swap = lax.ppermute(theirs, "depth", swap_pairs)
    diagonal = lax.ppermute(other_halo, "depth", diagonal_pairs)
    straight = lax.ppermute(own_halo, "depth", straight_pairs)

    table = jnp.zeros((hidden + 8, LANES), F32)
    table = table.at[:hidden, :12].set(w_in).at[:hidden, 12].set(b_in)
    table = table.at[hidden : hidden + 4, :hidden].set(w_out).at[hidden : hidden + 4, hidden].set(b_out)
    width = 256
    outs = FIELDS * layers
    w1, w2a, w2b, bias2 = call(
        functools.partial(weights_kernel, layers=layers, hidden=hidden, slabs=slabs),
        [
            shape((2 * layers * hidden, 3 * width), BF16),
            shape((2 * outs, layers * hidden), BF16),
            shape((outs, layers * hidden), BF16),
            shape((outs, 2 * LANES), F32),
        ],
        (table,),
        flops=10**8,
        name="weights",
    )
    message = shape((HALO * kk + 4 * 32, LANES), BF16)
    first, second = call(band_kernel, [message, message], (mine, swap, straight, diagonal), name="band")
    within = [(i, i ^ 1) for i in range(bands)]
    across = [(i, i + 1) for i in range(1, bands - 1, 2)] + [(i + 1, i) for i in range(1, bands - 1, 2)]
    second = lax.ppermute(second, "row", across)
    first = lax.ppermute(first, "row", within)
    current = call(
        functools.partial(shade_kernel, layers=layers, rows=rows),
        shape((4, rows, LANES), F32),
        (mine, swap, straight, diagonal, first, second, w1, w2a, w2b, bias2),
        [
            pltpu.VMEM((rows + 2 * HALO, kk, LANES), F32),
            pltpu.VMEM((3, kk, LANES), F32),
            pltpu.VMEM((rows, width, LANES), BF16),
            pltpu.VMEM((rows, width, LANES), BF16),
        ],
        flops=10**10,
        name="shade",
    )
    step = 2
    while step < slabs:
        received = lax.ppermute(current, "depth", [(i, i ^ step) for i in range(slabs)])
        behind = (me & step) != 0
        current = combine(jnp.where(behind, received, current), jnp.where(behind, current, received))
        step *= 2
    current = jnp.concatenate([current[0:3], 1.0 - current[3:4]], 0)
    other = lax.ppermute(current, "depth", swap_pairs)
    first_half = jnp.where(side == 0, current, other)
    second_half = jnp.where(side == 0, other, current)
    return jnp.concatenate([first_half, second_half], 2)


def solution(mesh):
    return jax.shard_map(
        local,
        mesh=mesh,
        in_specs=(P(None, "depth", "row", None), P(), P(), P(), P()),
        out_specs=P(None, "row", None),
        check_vma=False,
    )
```

time: 109 us -> 57.5 us (0.53)
  the two profiles are of different devices: /device:TPU:4 before, /device:TPU:28 now
where the time goes in v1:
time: 57.5 us; the launch traced here: 57.2 us
  Pallas kernels  19.6 us (34%)
  waiting for transfers between devices  17.5 us (30%)
  starting transfers between devices  10.9 us (19%)
  local copies, waits for them, and re-layouts  5.59 us (10%)
  other arithmetic  3.32 us (6%)
    pallas_call x4, Pallas kernels, call(): pl.pallas_call(kernel, out_shape=out_shape, in_specs=[vmem] * len(operand...  19.6 us
    ppermute x2, waiting for transfers between devices, local(): lax.ppermute(current, 'depth', [(i, i ^ step) for i in range(slabs)])  9.23 us
    ppermute x1, waiting for transfers between devices, local(): other = lax.ppermute(current, 'depth', swap_pairs)  4.25 us
    ppermute x1, waiting for transfers between devices, local(): diagonal = lax.ppermute(other_halo, 'depth', diagonal_pairs)  4.05 us
    ppermute x1, starting transfers between devices, local(): diagonal = lax.ppermute(other_halo, 'depth', diagonal_pairs)  3.45 us
    another operation x3, other arithmetic  2.56 us
    unnamed x13, local copies, waits for them, and re-layouts  2.52 us
    ppermute x1, starting transfers between devices, local(): second = lax.ppermute(second, 'row', across)  2.5 us
  transfers between devices with their start and end apart: 8, of which 4 were waited for; matrix products, arithmetic and copies ran while one was open for 10% of the time, Pallas kernels for 1%

profile of v1, /device:TPU:28, one launch (start us, length us, event | category | flops | bytes accessed | tf_op | source)
XLA Modules:
  0.0 57.2 jit_solution(701685893892343685)
XLA Ops:
  0.0 1.0 %copy-done = bf16[4,8,32,256]{3,2,1,0:T(8,128)(2,1)S(1)} copy-done((bf16[4,8,32,256]{3,2,1,0:T(8,128)(2,1)S(1)}, bf16[4,8,32,256]{3,2,1,0:T(8,128)(2,1)}, u32[]{:S(2)}) %copy-start) | copy-done | bytes 524312
  1.0 0.8 %pack.1 = (bf16[1056,128]{1,0:T(8,128)(2,1)S(1)}, bf16[1056,128]{1,0:T(8,128)(2,1)S(1)}, bf16[800,128]{1,0:T(8,128)(2,1)S(1)}, bf16[800,128]{1,0:T(8,128)(2,1)S(1)}) custom-call(bf16[4,8,32,256]{3,2,1,0:T(8,128)(2,1)S(1)} %copy-done), custom_call_target="tpu_custom_call" | custom-call | bytes 1048576 | tf_op jit(solution)/shard_map/pack/pallas_call | solution.py:277
  1.9 1.6 %collective-permute-start = (bf16[1056,128]{1,0:T(8,128)(2,1)S(1)}, bf16[1056,128]{1,0:T(8,128)(2,1)S(1)}, u32[]{:S(2)}, u32[]{:S(2)}) collective-permute-start(bf16[1056,128]{1,0:T(8,128)(2,1)S(1)} %get-tuple-element.64), channel_id=1, source_target_pairs={{0,4},{4,0},{8,12},{12,8},{16,20},{20,16},{24,28},{28,24},{1,5},{5... | collective-permute-start | bytes 811016 | tf_op jit(solution)/shard_map/ppermute | solution.py:320
  3.4 2.4 %collective-permute-start.1 = (bf16[800,128]{1,0:T(8,128)(2,1)S(1)}, bf16[800,128]{1,0:T(8,128)(2,1)S(1)}, u32[]{:S(2)}, u32[]{:S(2)}) collective-permute-start(bf16[800,128]{1,0:T(8,128)(2,1)S(1)} %get-tuple-element.65), channel_id=1, source_target_pairs={{4,12},{12,20},{20,28},{8,0},{16,8},{24,16},{5,13},{13,21},{21,29}... | collective-permute-start | bytes 614408 | tf_op jit(solution)/shard_map/ppermute | solution.py:322
  5.8 3.4 %collective-permute-start.2 = (bf16[800,128]{1,0:T(8,128)(2,1)S(1)}, bf16[800,128]{1,0:T(8,128)(2,1)S(1)}, u32[]{:S(2)}, u32[]{:S(2)}) collective-permute-start(bf16[800,128]{1,0:T(8,128)(2,1)S(1)} %get-tuple-element.66), channel_id=1, source_target_pairs={{4,8},{12,16},{20,24},{8,4},{16,12},{24,20},{5,9},{13,17},{21,25},... | collective-permute-start | bytes 614408 | tf_op jit(solution)/shard_map/ppermute | solution.py:321
  9.4 0.7 %copy-done.3 = f32[32]{0:T(128)S(1)} copy-done((f32[32]{0:T(128)S(1)}, f32[32]{0:T(128)}, u32[]{:S(2)}) %copy-start.3) | copy-done | bytes 152
  10.1 0.7 %copy-done.4 = f32[4]{0:T(128)S(1)} copy-done((f32[4]{0:T(128)S(1)}, f32[4]{0:T(128)}, u32[]{:S(2)}) %copy-start.4) | copy-done | bytes 40
  10.8 0.1 copy.8
  10.9 0.6 %fusion.3 = (s32[1]{0:T(128)}, s32[1]{0:T(128)}) fusion(s32[2]{0:T(128)S(1)} %iota_multiply_fusion), kind=kLoop, calls=%fused_computation.21 | loop fusion | bytes 16 | tf_op jit(solution)/shard_map/slice.66
  11.5 0.6 %and_reduce_fusion = pred[]{:T(512)} fusion(s32[2]{0:T(128)S(1)} %copy-done.5), kind=kLoop, calls=%fused_computation.19 | loop fusion | flops 9 | bytes 9 | tf_op jit(solution)/shard_map/reduce.5
  12.2 4.0 %collective-permute-done.2.diagonal = bf16[800,128]{1,0:T(8,128)(2,1)S(1)} collective-permute-done((bf16[800,128]{1,0:T(8,128)(2,1)S(1)}, bf16[800,128]{1,0:T(8,128)(2,1)S(1)}, u32[]{:S(2)}, u32[]{:S(2)}) %collective-permute-start.2) | collective-permute-done | bytes 204832 | tf_op jit(solution)/shard_map/ppermute | solution.py:321
  16.3 2.5 %collective-permute-start.4 = (bf16[800,128]{1,0:T(8,128)(2,1)S(1)}, bf16[800,128]{1,0:T(8,128)(2,1)S(1)}, u32[]{:S(2)}, u32[]{:S(2)}) collective-permute-start(bf16[800,128]{1,0:T(8,128)(2,1)S(1)} %get-tuple-element.68), channel_id=1, source_target_pairs={{1,2},{2,1},{5,6},{6,5},{9,10},{10,9},{13,14},{14,13},{17,18},{18,... | collective-permute-start | bytes 614408 | tf_op jit(solution)/shard_map/ppermute | solution.py:345
  18.9 1.9 %dynamic-slice_select_fusion = f32[32,1]{1,0:T(8,128)S(1)} fusion(f32[32,1]{1,0:T(8,128)S(1)} %copy.7, s32[]{:T(128)} %bitcast.1, s32[]{:T(128)} %bitcast.2, pred[]{:T(512)} %and_reduce_fusion, f32[32,12]{1,0:T(8,128)S(1)} %copy.6), kind=kLoop, calls=%fused_computation.16 | loop fusion | flops 32 | bytes 1801 | tf_op jit(solution)/shard_map/select.5
  20.8 1.7 %scatter.15 = f32[40,128]{1,0:T(8,128)S(1)} dynamic-update-slice(f32[40,128]{1,0:T(8,128)S(1)} %scatter.14, f32[32,1]{1,0:T(8,128)S(1)} %dynamic-slice_select_fusion, s32[]{:T(128)} %bitcast.1, s32[]{:T(128)} %bitcast.2) | dynamic-update-slice | bytes 260 | tf_op jit(solution)/shard_map/scatter | solution.py:325
  22.5 0.3 scatter.16
  22.8 0.3 scatter.19.params
  23.1 0.6 %weights.1 = (bf16[512,768]{1,0:T(8,128)(2,1)S(1)}, bf16[64,256]{1,0:T(8,128)(2,1)S(1)}, bf16[32,256]{1,0:T(8,128)(2,1)S(1)}, f32[32,256]{1,0:T(8,128)S(1)}) custom-call(f32[40,128]{1,0:T(8,128)S(1)} %scatter.19.params), custom_call_target="tpu_custom_call" | custom-call | flops 100000000 | bytes 1048576 | tf_op jit(solution)/shard_map/weights/pallas_call | solution.py:277
  23.8 18.1 %shade.1 = f32[4,32,128]{2,1,0:T(8,128)S(1)} custom-call(bf16[1056,128]{1,0:T(8,128)(2,1)S(1)} %get-tuple-element.63.mine, bf16[1056,128]{1,0:T(8,128)(2,1)S(1)} %collective-permute-done.swap, bf16[800,128]{1,0:T(8,128)(2,1)S(1)} %collective-permute-done.1.straight, bf16[800,128]{1,0:T(8,128)(2,1)S(1)} %collective-permute-done.2.diagonal, ...), custom_call_target="tpu_custom_call" | custom-call | flops 10000000000 | bytes 1048576 | tf_op jit(solution)/shard_map/shade/pallas_call | solution.py:277
  41.9 0.5 collective-permute-start.5
  42.4 3.8 %collective-permute-done.5 = f32[4,32,128]{2,1,0:T(8,128)S(1)} collective-permute-done((f32[4,32,128]{2,1,0:T(8,128)S(1)}, f32[4,32,128]{2,1,0:T(8,128)S(1)}, u32[]{:S(2)}, u32[]{:S(2)}) %collective-permute-start.5) | collective-permute-done | bytes 65568 | tf_op jit(solution)/shard_map/ppermute | solution.py:362
  46.3 0.4 collective-permute-start.6
  46.7 5.4 %collective-permute-done.6 = f32[4,32,128]{2,1,0:T(8,128)S(1)} collective-permute-done((f32[4,32,128]{2,1,0:T(8,128)S(1)}, f32[4,32,128]{2,1,0:T(8,128)S(1)}, u32[]{:S(2)}, u32[]{:S(2)}) %collective-permute-start.6) | collective-permute-done | bytes 65568 | tf_op jit(solution)/shard_map/ppermute | solution.py:362
  52.2 4.2 %collective-permute-done.7 = f32[4,32,128]{2,1,0:T(8,128)S(1)} collective-permute-done((f32[4,32,128]{2,1,0:T(8,128)S(1)}, f32[4,32,128]{2,1,0:T(8,128)S(1)}, u32[]{:S(2)}, u32[]{:S(2)}) %collective-permute-start.7) | collective-permute-done | bytes 65568 | tf_op jit(solution)/shard_map/ppermute | solution.py:367
  56.5 0.7 %pad_maximum_fusion = f32[4,32,256]{2,1,0:T(8,128)} fusion(f32[4,32,128]{2,1,0:T(8,128)S(1)} %get-tuple-element.74, f32[4,32,128]{2,1,0:T(8,128)S(1)} %get-tuple-element.73), kind=kLoop, calls=%fused_computation | loop fusion | flops 32768 | bytes 262144 | tf_op jit(solution)/shard_map/concatenate | solution.py:370
  (29 shorter events, 0.5 us)
Async XLA Ops:
  0.0 1.0 %copy-start = (bf16[4,8,32,256]{3,2,1,0:T(8,128)(2,1)S(1)}, bf16[4,8,32,256]{3,2,1,0:T(8,128)(2,1)}, u32[]{:S(2)}) copy-start(bf16[4,8,32,256]{3,2,1,0:T(8,128)(2,1)} %fields.1) | copy-start | bytes 1572868
  1.0 8.2 %copy-start.1 = (f32[32,12]{0,1:T(8,128)S(1)}, f32[32,12]{0,1:T(8,128)}, u32[]{:S(2)}) copy-start(f32[32,12]{0,1:T(8,128)} %param.14) | copy-start | bytes 4612
  1.9 14.3 %collective-permute-start = (bf16[1056,128]{1,0:T(8,128)(2,1)S(1)}, bf16[1056,128]{1,0:T(8,128)(2,1)S(1)}, u32[]{:S(2)}, u32[]{:S(2)}) collective-permute-start(bf16[1056,128]{1,0:T(8,128)(2,1)S(1)} %get-tuple-element.64), channel_id=1, source_target_pairs={{0,4},{4,0},{8,12},{12,8},{16,20},{20,16},{24,28},{28,24},{1,5},{5... | collective-permute-start | bytes 811016 | tf_op jit(solution)/shard_map/ppermute | solution.py:320
  3.4 8.7 %collective-permute-start.1 = (bf16[800,128]{1,0:T(8,128)(2,1)S(1)}, bf16[800,128]{1,0:T(8,128)(2,1)S(1)}, u32[]{:S(2)}, u32[]{:S(2)}) collective-permute-start(bf16[800,128]{1,0:T(8,128)(2,1)S(1)} %get-tuple-element.65), channel_id=1, source_target_pairs={{4,12},{12,20},{20,28},{8,0},{16,8},{24,16},{5,13},{13,21},{21,29}... | collective-permute-start | bytes 614408 | tf_op jit(solution)/shard_map/ppermute | solution.py:322
  5.8 10.4 %collective-permute-start.2 = (bf16[800,128]{1,0:T(8,128)(2,1)S(1)}, bf16[800,128]{1,0:T(8,128)(2,1)S(1)}, u32[]{:S(2)}, u32[]{:S(2)}) collective-permute-start(bf16[800,128]{1,0:T(8,128)(2,1)S(1)} %get-tuple-element.66), channel_id=1, source_target_pairs={{4,8},{12,16},{20,24},{8,4},{16,12},{24,20},{5,9},{13,17},{21,25},... | collective-permute-start | bytes 614408 | tf_op jit(solution)/shard_map/ppermute | solution.py:321
  9.4 0.7 %copy-start.3 = (f32[32]{0:T(128)S(1)}, f32[32]{0:T(128)}, u32[]{:S(2)}) copy-start(f32[32]{0:T(128)} %param.15) | copy-start | bytes 388
  10.1 0.7 %copy-start.4 = (f32[4]{0:T(128)S(1)}, f32[4]{0:T(128)}, u32[]{:S(2)}) copy-start(f32[4]{0:T(128)} %param.17) | copy-start | bytes 52
  10.9 0.7 %copy-start.5 = (s32[2]{0:T(128)S(1)}, s32[2]{0:T(128)}, u32[]{:S(2)}) copy-start(s32[2]{0:T(128)} %constant.115.clone.1) | copy-start | bytes 28
  16.3 7.5 %collective-permute-start.3 = (bf16[800,128]{1,0:T(8,128)(2,1)S(1)}, bf16[800,128]{1,0:T(8,128)(2,1)S(1)}, u32[]{:S(2)}, u32[]{:S(2)}) collective-permute-start(bf16[800,128]{1,0:T(8,128)(2,1)S(1)} %get-tuple-element.67), channel_id=1, source_target_pairs={{0,1},{1,0},{2,3},{3,2},{4,5},{5,4},{6,7},{7,6},{8,9},{9,8},{10,11... | collective-permute-start | bytes 614408 | tf_op jit(solution)/shard_map/ppermute | solution.py:346
  16.3 7.4 %collective-permute-start.4 = (bf16[800,128]{1,0:T(8,128)(2,1)S(1)}, bf16[800,128]{1,0:T(8,128)(2,1)S(1)}, u32[]{:S(2)}, u32[]{:S(2)}) collective-permute-start(bf16[800,128]{1,0:T(8,128)(2,1)S(1)} %get-tuple-element.68), channel_id=1, source_target_pairs={{1,2},{2,1},{5,6},{6,5},{9,10},{10,9},{13,14},{14,13},{17,18},{18,... | collective-permute-start | bytes 614408 | tf_op jit(solution)/shard_map/ppermute | solution.py:345
  20.8 1.7 %copy-start.2 = (f32[4,32]{1,0:T(4,128)S(1)}, f32[4,32]{1,0:T(4,128)}, u32[]{:S(2)}) copy-start(f32[4,32]{1,0:T(4,128)} %param.16) | copy-start | bytes 1540
  41.9 4.3 %collective-permute-start.5 = (f32[4,32,128]{2,1,0:T(8,128)S(1)}, f32[4,32,128]{2,1,0:T(8,128)S(1)}, u32[]{:S(2)}, u32[]{:S(2)}) collective-permute-start(f32[4,32,128]{2,1,0:T(8,128)S(1)} %shade.1), channel_id=1, source_target_pairs={{0,8},{4,12},{8,0},{12,4},{16,24},{20,28},{24,16},{28,20},{1,9},{5... | collective-permute-start | bytes 196616 | tf_op jit(solution)/shard_map/ppermute | solution.py:362
  46.3 5.8 %collective-permute-start.6 = (f32[4,32,128]{2,1,0:T(8,128)S(1)}, f32[4,32,128]{2,1,0:T(8,128)S(1)}, u32[]{:S(2)}, u32[]{:S(2)}) collective-permute-start(f32[4,32,128]{2,1,0:T(8,128)S(1)} %pad_maximum_fusion.1), channel_id=1, source_target_pairs={{0,16},{4,20},{8,24},{12,28},{16,0},{20,4},{24,8},{28,12},{1,17},{... | collective-permute-start | bytes 196616 | tf_op jit(solution)/shard_map/ppermute | solution.py:362
  52.2 4.3 %collective-permute-start.7 = (f32[4,32,128]{2,1,0:T(8,128)S(1)}, f32[4,32,128]{2,1,0:T(8,128)S(1)}, u32[]{:S(2)}, u32[]{:S(2)}) collective-permute-start(f32[4,32,128]{2,1,0:T(8,128)S(1)} %pad_maximum_fusion.2), channel_id=1, source_target_pairs={{0,4},{4,0},{8,12},{12,8},{16,20},{20,16},{24,28},{28,24},{1,5},{5... | collective-permute-start | bytes 196616 | tf_op jit(solution)/shard_map/ppermute | solution.py:367

commit v2 on v1

--- a/solution.py
+++ b/solution.py
@@ -100,69 +100,69 @@
             extra += 32
 
 
-def weights_kernel(params, w1, w2a, w2b, bias2, *, layers, hidden, slabs):
+def weights_kernel(w_in, b_in, w_out, b_out, w1, w2, *, layers, hidden, slabs):
     depth = lax.axis_index("depth")
     side = depth & 1
     base = (depth - side) * layers
     total = slabs * layers
-    zs = 2 * layers
-    kk = (2 * layers + 2 * HALO) * FIELDS
-    width = w1.shape[1] // 3
-    table = params[0:hidden, :]
-    row, col = iota((LANES, width), 0), iota((LANES, width), 1)
+    width = w1.shape[2]
+    window = (layers + 2 * HALO) * FIELDS
+    kinds = w_in.shape[1]
+    row, col = iota((kinds, width), 0), iota((kinds, width), 1)
+    within = col % (2 * window)
     field = col & 3
-    pick1 = jnp.where(col < kk, field, jnp.where(col < 2 * kk, field + 4, jnp.where(col == 2 * kk, 12, -1)))
-    pick2 = jnp.where(col < kk, field + 8, -1)
-    part1 = dot(table, (row == pick1).astype(F32), HIGHEST)
-    part2 = dot(table, (row == pick2).astype(F32), HIGHEST)
+    ending = col >= 6 * window
+    pick1 = jnp.where(ending, -1, jnp.where(within < window, field, field + 4))
+    pick2 = jnp.where(ending | (within >= window), -1, field + 8)
+    eye = iota((hidden, hidden), 0) == iota((hidden, hidden), 1)
+    bias = jnp.sum(jnp.where(eye, b_in[...], 0.0), axis=1, keepdims=True)
+    part1 = dot(w_in[...], (row == pick1).astype(F32), HIGHEST)
+    part2 = dot(w_in[...], (row == pick2).astype(F32), HIGHEST)
     kappa = iota((hidden, width), 1)
-    slot = jnp.where(kappa < kk, kappa, kappa - kk) >> 2
-    low, high = slot - 4 * layers // 2 - HALO, slot - 2 * layers
-    zk = jnp.where(slot < layers, side * layers + slot, (1 - side) * layers + slot - layers)
-    below, above = 2 * layers, -HALO
-    zk = jnp.where(slot >= 2 * layers, high + jnp.where(side == 0, below, above), zk)
-    zk = jnp.where(slot >= 2 * layers + HALO, low + jnp.where(side == 0, above, below), zk)
+    part1 = jnp.where(kappa == 6 * window, bias, jnp.where(kappa == 6 * window + 1, bias, part1))
     scale = 1.0 / 64.0**3
-    for z in range(zs):
-        distance = zk - z
+    z, place = iota((layers, width), 0), iota((layers, width), 1)
+    inner = place % (2 * window)
+    slope_kind = inner >= window
+    last = place >= 6 * window
+    slot = jnp.where(slope_kind, inner - window, inner) >> 2
+    low_column = ((place >= 2 * window) & (place < 4 * window)) | (place == 6 * window + 1)
+    for half in range(2):
+        distance = slot - HALO - z
         center = smooth_count(distance) * scale
-        slope = jnp.zeros((hidden, width), F32)
+        slope = jnp.zeros((layers, width), F32)
         for offset, count in slope_counts:
             for sign in (1, -1):
-                at = base + z + sign * offset
+                at = base + half * layers + z + sign * offset
                 inside = ((at >= 0) & (at < total)).astype(F32)
                 slope = slope + (inside * (sign * count)) * smooth_count(distance - sign * offset)
-        center = jnp.where(kappa < kk, center, jnp.where(kappa < 2 * kk, center * (1.0 / 60.0), 1.0))
-        high_part, low_part = split(center * part1 + (slope * (scale / 60.0)) * part2)
-        at = pl.ds(z * hidden, hidden)
-        w1[at, 0:width] = high_part
-        w1[at, width : 2 * width] = low_part
-        w1[at, 2 * width :] = high_part
-    outs = FIELDS * layers
-    rr, cc = iota((outs, LANES), 0), iota((outs, LANES), 1)
-    group = layers * hidden
-    source = params[hidden : hidden + 8, :]
-    rows8 = iota((outs, 8), 0) // layers == iota((outs, 8), 1)
-    spread = dot(rows8.astype(F32), source, HIGHEST)
-    across = iota((LANES, group), 0) == (iota((LANES, group), 1) & (hidden - 1))
-    full = dot(spread, across.astype(F32), HIGHEST)
-    diagonal = (iota((outs, group), 0) & (layers - 1)) == iota((outs, group), 1) // hidden
-    high_part, low_part = split(jnp.where(diagonal, full, 0.0))
-    w2a[0:outs, :] = high_part
-    w2a[outs:, :] = low_part
-    w2b[...] = high_part
-    bias = jnp.sum(jnp.where(cc == hidden, spread, 0.0), axis=1, keepdims=True)
-    bias2[...] = jnp.broadcast_to(bias, bias2.shape)
-
-
-def shade_kernel(mine, swap, straight, diagonal, first, second, w1, w2a, w2b, bias2, out, grid, edge, xhi, xlo, *, layers, rows):
+        center = jnp.where(last, 1.0, jnp.where(slope_kind, center * (1.0 / 60.0), center))
+        product = center[None] * part1[:, None, :] + (slope * (scale / 60.0))[None] * part2[:, None, :]
+        high = product.astype(BF16).astype(F32)
+        chosen = jnp.where(low_column[None], product - high, high)
+        w1[half] = chosen.reshape(hidden * layers, width).astype(BF16)
+    outs = w_out.shape[0]
+    for c in range(outs):
+        values = jnp.sum(jnp.where(eye, w_out[c : c + 1, :], 0.0), axis=1, keepdims=True)
+        w2[c * hidden : (c + 1) * hidden, :] = jnp.broadcast_to(values, (hidden, LANES))
+    pick = iota((8, outs), 0) == iota((8, outs), 1)
+    values = jnp.sum(jnp.where(pick, b_out[...], 0.0), axis=1, keepdims=True)
+    w2[outs * hidden :, :] = jnp.broadcast_to(values, (8, LANES))
+
+
+def shade_kernel(mine, swap, straight, diagonal, first, second, w1, w2, out, grid, edge, kept, *, layers, rows):
     side = lax.axis_index("depth") & 1
     band = lax.axis_index("row")
     bands = lax.axis_size("row")
     odd = band & 1
     kw, kh = layers * FIELDS, HALO * FIELDS
     kk = 2 * (kw + kh)
-    offsets = ((mine, 0, kw), (swap, kw, kw), (straight, 2 * kw, kh), (diagonal, 2 * kw + kh, kh))
+    offsets = (
+        (mine, kh + side * kw, kw),
+        (swap, kh + (1 - side) * kw, kw),
+        (straight, (1 - side) * (kh + 2 * kw), kh),
+        (diagonal, side * (kh + 2 * kw), kh),
+    )
     i, j = iota((LANES, LANES), 0), iota((LANES, LANES), 1)
     taps = smooth_count(i - j).astype(BF16)
     ir, ic = i // 3, i % 3
@@ -171,19 +171,21 @@
     apart = jnp.where(side == 0, ic - jc + 3, jc - ic + 3)
     border = jnp.where((ir == jr) & (i < 3 * rows) & (spot < 3 * rows), smooth_count(apart), 0.0).astype(BF16)
     for source, at, width in offsets:
+        at = pl.ds(pl.multiple_of(at, 8), width)
         filtered = dot(source[0 : rows * width, :], taps)
-        grid[HALO : HALO + rows, at : at + width, :] = filtered.reshape(rows, width, LANES)
-        edge[0, at : at + width, :] = dot(source[rows * width : rows * width + 32, :], border)[:width]
+        grid[HALO : HALO + rows, at, :] = filtered.reshape(rows, width, LANES)
+        edge[0, at, :] = dot(source[rows * width : rows * width + 32, :], border)[:width]
     far = HALO + rows
     for source, base, which in ((first, odd, 2 - odd), (second, 1 - odd, 1 + odd)):
         place = (1 - base) * far
-        start, extra = 0, HALO * kk
+        start = 0
         filtered = dot(source[0 : HALO * kk, :], taps)
         edges = dot(source[HALO * kk :, :], border)
         for index, (unused, at, width) in enumerate(offsets):
+            at = pl.ds(pl.multiple_of(at, 8), width)
             piece = filtered[start : start + HALO * width].reshape(HALO, width, LANES)
-            grid[pl.ds(place, HALO), at : at + width, :] = piece
-            edge[which, at : at + width, :] = edges[index * 32 : index * 32 + width]
+            grid[pl.ds(place, HALO), at, :] = piece
+            edge[which, at, :] = edges[index * 32 : index * 32 + width]
             start += HALO * width
     lane = iota((16, LANES), 1)
     near = ((lane + jnp.where(side == 0, 3, 0)) & (LANES - 1)) < 3
@@ -192,7 +194,6 @@
 
     def filter_rows(group, carry):
         at = pl.ds(pl.multiple_of(group * 16, 16), 16)
-        after = pl.ds(pl.multiple_of(group * 16 + kk, 16), 16)
         edges = [edge[k, at, :] for k in range(3)]
         chain = [None] * 6
         ring = []
@@ -218,37 +219,42 @@
             if len(ring) == 7:
                 slope = (ring[6] - ring[0]) - 9.0 * (ring[5] - ring[1]) + 45.0 * (ring[4] - ring[2])
                 y -= 3
-                xhi[y, at, :], xlo[y, at, :] = split(ring[3])
-                xhi[y, after, :], xlo[y, after, :] = split(slope)
+                kept[0, y, at, :], kept[2, y, at, :] = split(ring[3])
+                kept[1, y, at, :], kept[3, y, at, :] = split(slope)
                 ring.pop(0)
         return carry
 
     lax.fori_loop(0, kk // 16, filter_rows, 0)
-    rest = xhi.shape[1] - 2 * kk
-    ones = jnp.where(iota((rest, LANES), 0) == 0, 1.0, 0.0).astype(BF16)
-    for y in range(rows):
-        xhi[y, 2 * kk :, :] = ones
-        xlo[y, 2 * kk :, :] = jnp.zeros((rest, LANES), BF16)
     wide = 2 * LANES
-    outs = FIELDS * layers
-    group = w2a.shape[1]
+    window = kw + 2 * kh
+    hidden = w1.shape[1] // layers
+    rest = w1.shape[2] - 6 * window
+    ones = jnp.where(iota((rest, wide), 0) < 2, 1.0, 0.0).astype(BF16)
     sub = iota((layers, wide), 0)
     scale = depth_scale / (lax.axis_size("depth") * layers)
 
+    def splat(index):
+        line = w2[index : index + 1, :]
+        return jnp.broadcast_to(jnp.concatenate([line, line], 1), (layers, wide))
+
     def shade(pair, carry):
         y = 2 * pair
-        high = jnp.concatenate([xhi[y], xhi[y + 1]], 1)
-        low = jnp.concatenate([xlo[y], xlo[y + 1]], 1)
-        stacked = jnp.concatenate([high, high, low], 0)
         total = jnp.zeros((1, wide), F32)
         front = jnp.ones((1, wide), F32)
         color = [jnp.zeros((layers, wide), F32) for unused in range(3)]
         for half in range(2):
-            hidden = jnp.tanh(dot(w1[half * group : (half + 1) * group, :], stacked))
-            hidden_high, hidden_low = split(hidden)
-            o = dot(w2a[...], hidden_high)
-            o = o[:outs] + o[outs:] + dot(w2b[...], hidden_low) + bias2[...]
-            x = o[3 * layers :]
+            at = pl.ds(half * kw, window)
+            c_high, s_high, c_low, s_low = [
+                jnp.concatenate([kept[k, y, at, :], kept[k, y + 1, at, :]], 1) for k in range(4)
+            ]
+            stacked = jnp.concatenate([c_high, s_high, c_high, s_high, c_low, s_low, ones], 0)
+            units = jnp.tanh(dot(w1[half], stacked))
+            o = [splat(4 * hidden + c) for c in range(4)]
+            for h in range(hidden):
+                unit = units[h * layers : (h + 1) * layers]
+                for c in range(4):
+                    o[c] = o[c] + splat(c * hidden + h) * unit
+            x = o[3]
             optical = (jnp.maximum(x, 0.0) + jnp.log1p(jnp.exp(-jnp.abs(x)))) * scale
             through = optical
             for step in (1, 2, 4):
@@ -260,7 +266,7 @@
             front = after[layers - 1 :]
             weight = before - after
             for c in range(3):
-                color[c] = color[c] + weight / (1.0 + jnp.exp(-o[c * layers : (c + 1) * layers]))
+                color[c] = color[c] + weight / (1.0 + jnp.exp(-o[c]))
         for c in range(3):
             line = jnp.sum(color[c], axis=0, keepdims=True)
             out[c, pl.ds(y, 1), :] = line[:, :LANES]
@@ -321,20 +327,11 @@
     diagonal = lax.ppermute(other_halo, "depth", diagonal_pairs)
     straight = lax.ppermute(own_halo, "depth", straight_pairs)
 
-    table = jnp.zeros((hidden + 8, LANES), F32)
-    table = table.at[:hidden, :12].set(w_in).at[:hidden, 12].set(b_in)
-    table = table.at[hidden : hidden + 4, :hidden].set(w_out).at[hidden : hidden + 4, hidden].set(b_out)
-    width = 256
-    outs = FIELDS * layers
-    w1, w2a, w2b, bias2 = call(
+    width = -(-(6 * (kw + 2 * kh) + 2) // 256) * 256
+    w1, w2 = call(
         functools.partial(weights_kernel, layers=layers, hidden=hidden, slabs=slabs),
-        [
-            shape((2 * layers * hidden, 3 * width), BF16),
-            shape((2 * outs, layers * hidden), BF16),
-            shape((outs, layers * hidden), BF16),
-            shape((outs, 2 * LANES), F32),
-        ],
-        (table,),
+        [shape((2, layers * hidden, width), BF16), shape((4 * hidden + 8, LANES), F32)],
+        (w_in, b_in[None], w_out, b_out[None]),
         flops=10**8,
         name="weights",
     )
@@ -347,12 +344,11 @@
     current = call(
         functools.partial(shade_kernel, layers=layers, rows=rows),
         shape((4, rows, LANES), F32),
-        (mine, swap, straight, diagonal, first, second, w1, w2a, w2b, bias2),
+        (mine, swap, straight, diagonal, first, second, w1, w2),
         [
             pltpu.VMEM((rows + 2 * HALO, kk, LANES), F32),
             pltpu.VMEM((3, kk, LANES), F32),
-            pltpu.VMEM((rows, width, LANES), BF16),
-            pltpu.VMEM((rows, width, LANES), BF16),
+            pltpu.VMEM((4, rows, kk, LANES), BF16),
         ],
         flops=10**10,
         name="shade",

time: 57.5 us -> 49.4 us (0.86)
  Pallas kernels: 19.6 us -> 11.9 us
  waiting for transfers between devices: 17.5 us -> 23.7 us
  local copies, waits for them, and re-layouts: 5.59 us -> 1.82 us
  other arithmetic: 3.32 us -> 0.75 us
    pallas_call x4, Pallas kernels: 19.6 us -> 11.9 us  [call(): pl.pallas_call(kernel, out_shape=out_shape, in_specs=[vmem] * len(operand...]
    ppermute x1, waiting for transfers between devices: 0.01 us -> 3.22 us  [local(): second = lax.ppermute(second, 'row', across)]
    another operation x3 -> x0, other arithmetic: 2.56 us -> none
    scatter x4 -> x0, local copies, waits for them, and re-layouts: 2.31 us -> none  [the longest x2 1.7 us: local(): table = table.at[:hidden, :12].set(w_in).at[:hidden, 12].set(b_in)]
    ppermute x1, waiting for transfers between devices: 0.01 us -> 1.71 us  [local(): straight = lax.ppermute(own_halo, 'depth', straight_pairs)]
    ppermute x1, waiting for transfers between devices: 4.05 us -> 5.25 us  [local(): diagonal = lax.ppermute(other_halo, 'depth', diagonal_pairs)]
    another operation x3 -> x0, local copies, waits for them, and re-layouts: 0.76 us -> none
    unnamed x13 -> x11, local copies, waits for them, and re-layouts: 2.52 us -> 1.82 us
  transfers between devices with their start and end apart: 8 -> 8, of which waited for: 4 -> 6; matrix products, arithmetic and copies ran while one was open for 10% -> 0% of each run, Pallas kernels for 1% -> 1%
where the time goes in v2:
time: 49.4 us; the launch traced here: 49.2 us
  waiting for transfers between devices  23.7 us (48%)
  Pallas kernels  11.9 us (24%)
  starting transfers between devices  10.9 us (22%)
  local copies, waits for them, and re-layouts  1.82 us (4%)
  other arithmetic  0.75 us (2%)
    pallas_call x4, Pallas kernels, call(): pl.pallas_call(kernel, out_shape=out_shape, in_specs=[vmem] * len(operand...  11.9 us
    ppermute x2, waiting for transfers between devices, local(): lax.ppermute(current, 'depth', [(i, i ^ step) for i in range(slabs)])  9.23 us
    ppermute x1, waiting for transfers between devices, local(): diagonal = lax.ppermute(other_halo, 'depth', diagonal_pairs)  5.25 us
    ppermute x1, waiting for transfers between devices, local(): other = lax.ppermute(current, 'depth', swap_pairs)  4.25 us
    ppermute x1, starting transfers between devices, local(): diagonal = lax.ppermute(other_halo, 'depth', diagonal_pairs)  3.45 us
    ppermute x1, waiting for transfers between devices, local(): second = lax.ppermute(second, 'row', across)  3.22 us
    ppermute x1, starting transfers between devices, local(): second = lax.ppermute(second, 'row', across)  2.5 us
    ppermute x1, starting transfers between devices, local(): straight = lax.ppermute(own_halo, 'depth', straight_pairs)  2.35 us
  transfers between devices with their start and end apart: 8, of which 6 were waited for; matrix products, arithmetic and copies ran while one was open for 0% of the time, Pallas kernels for 1%

profile of v2, /device:TPU:28, one launch (start us, length us, event | category | flops | bytes accessed | tf_op | source)
XLA Modules:
  0.0 49.2 jit_solution(6689260933002317827)
XLA Ops:
  0.0 1.0 %copy-done = bf16[4,8,32,256]{3,2,1,0:T(8,128)(2,1)S(1)} copy-done((bf16[4,8,32,256]{3,2,1,0:T(8,128)(2,1)S(1)}, bf16[4,8,32,256]{3,2,1,0:T(8,128)(2,1)}, u32[]{:S(2)}) %copy-start) | copy-done | bytes 524312
  1.0 0.8 %pack.1 = (bf16[1056,128]{1,0:T(8,128)(2,1)S(1)}, bf16[1056,128]{1,0:T(8,128)(2,1)S(1)}, bf16[800,128]{1,0:T(8,128)(2,1)S(1)}, bf16[800,128]{1,0:T(8,128)(2,1)S(1)}) custom-call(bf16[4,8,32,256]{3,2,1,0:T(8,128)(2,1)S(1)} %copy-done), custom_call_target="tpu_custom_call" | custom-call | bytes 1048576 | tf_op jit(solution)/shard_map/pack/pallas_call | solution.py:283
  1.9 1.6 %collective-permute-start = (bf16[1056,128]{1,0:T(8,128)(2,1)S(1)}, bf16[1056,128]{1,0:T(8,128)(2,1)S(1)}, u32[]{:S(2)}, u32[]{:S(2)}) collective-permute-start(bf16[1056,128]{1,0:T(8,128)(2,1)S(1)} %get-tuple-element.14), channel_id=1, source_target_pairs={{0,4},{4,0},{8,12},{12,8},{16,20},{20,16},{24,28},{28,24},{1,5},{5... | collective-permute-start | bytes 811016 | tf_op jit(solution)/shard_map/ppermute | solution.py:326
  3.4 2.4 %collective-permute-start.1 = (bf16[800,128]{1,0:T(8,128)(2,1)S(1)}, bf16[800,128]{1,0:T(8,128)(2,1)S(1)}, u32[]{:S(2)}, u32[]{:S(2)}) collective-permute-start(bf16[800,128]{1,0:T(8,128)(2,1)S(1)} %get-tuple-element.15), channel_id=1, source_target_pairs={{4,12},{12,20},{20,28},{8,0},{16,8},{24,16},{5,13},{13,21},{21,29}... | collective-permute-start | bytes 614408 | tf_op jit(solution)/shard_map/ppermute | solution.py:328
  5.8 3.4 %collective-permute-start.2 = (bf16[800,128]{1,0:T(8,128)(2,1)S(1)}, bf16[800,128]{1,0:T(8,128)(2,1)S(1)}, u32[]{:S(2)}, u32[]{:S(2)}) collective-permute-start(bf16[800,128]{1,0:T(8,128)(2,1)S(1)} %get-tuple-element.16), channel_id=1, source_target_pairs={{4,8},{12,16},{20,24},{8,4},{16,12},{24,20},{5,9},{13,17},{21,25},... | collective-permute-start | bytes 614408 | tf_op jit(solution)/shard_map/ppermute | solution.py:327
  9.3 1.7 %collective-permute-done.1.straight = bf16[800,128]{1,0:T(8,128)(2,1)S(1)} collective-permute-done((bf16[800,128]{1,0:T(8,128)(2,1)S(1)}, bf16[800,128]{1,0:T(8,128)(2,1)S(1)}, u32[]{:S(2)}, u32[]{:S(2)}) %collective-permute-start.1) | collective-permute-done | bytes 204832 | tf_op jit(solution)/shard_map/ppermute | solution.py:328
  11.0 5.3 %collective-permute-done.2.diagonal = bf16[800,128]{1,0:T(8,128)(2,1)S(1)} collective-permute-done((bf16[800,128]{1,0:T(8,128)(2,1)S(1)}, bf16[800,128]{1,0:T(8,128)(2,1)S(1)}, u32[]{:S(2)}, u32[]{:S(2)}) %collective-permute-start.2) | collective-permute-done | bytes 204832 | tf_op jit(solution)/shard_map/ppermute | solution.py:327
  16.2 0.0 collective-permute-done.swap
  16.3 0.1 collective-permute-start.3
  16.3 2.5 %collective-permute-start.4 = (bf16[800,128]{1,0:T(8,128)(2,1)S(1)}, bf16[800,128]{1,0:T(8,128)(2,1)S(1)}, u32[]{:S(2)}, u32[]{:S(2)}) collective-permute-start(bf16[800,128]{1,0:T(8,128)(2,1)S(1)} %get-tuple-element.18), channel_id=1, source_target_pairs={{1,2},{2,1},{5,6},{6,5},{9,10},{10,9},{13,14},{14,13},{17,18},{18,... | collective-permute-start | bytes 614408 | tf_op jit(solution)/shard_map/ppermute | solution.py:342
  18.9 0.0 copy-done.4
  18.9 0.1 copy.6.w_in
  19.0 0.7 %copy-done.1 = f32[4,32]{1,0:T(4,128)S(1)} copy-done((f32[4,32]{1,0:T(4,128)S(1)}, f32[4,32]{1,0:T(4,128)}, u32[]{:S(2)}) %copy-start.1) | copy-done | bytes 536
  19.6 0.5 %weights.1 = (bf16[2,256,512]{2,1,0:T(8,128)(2,1)S(1)}, f32[136,128]{1,0:T(8,128)S(1)}) custom-call(f32[32,12]{1,0:T(8,128)S(1)} %copy.6.w_in, f32[1,32]{1,0:T(1,128)S(1)} %bitcast.6, f32[4,32]{1,0:T(4,128)S(1)} %copy-done.1, f32[1,4]{1,0:T(1,128)S(1)} %bitcast.7), custom_call_target="tpu_custom_call" | custom-call | flops 100000000 | bytes 1048576 | tf_op jit(solution)/shard_map/weights/pallas_call | solution.py:283
  20.2 0.0 collective-permute-done.3.first
  20.2 3.2 %collective-permute-done.4.second = bf16[800,128]{1,0:T(8,128)(2,1)S(1)} collective-permute-done((bf16[800,128]{1,0:T(8,128)(2,1)S(1)}, bf16[800,128]{1,0:T(8,128)(2,1)S(1)}, u32[]{:S(2)}, u32[]{:S(2)}) %collective-permute-start.4) | collective-permute-done | bytes 204832 | tf_op jit(solution)/shard_map/ppermute | solution.py:342
  23.4 10.4 %shade.1 = f32[4,32,128]{2,1,0:T(8,128)S(1)} custom-call(bf16[1056,128]{1,0:T(8,128)(2,1)S(1)} %get-tuple-element.13.mine, bf16[1056,128]{1,0:T(8,128)(2,1)S(1)} %collective-permute-done.swap, bf16[800,128]{1,0:T(8,128)(2,1)S(1)} %collective-permute-done.1.straight, bf16[800,128]{1,0:T(8,128)(2,1)S(1)} %collective-permute-done.2.diagonal, ...), custom_call_target="tpu_custom_call" | custom-call | flops 10000000000 | bytes 1048576 | tf_op jit(solution)/shard_map/shade/pallas_call | solution.py:283
  33.9 0.5 %collective-permute-start.5 = (f32[4,32,128]{2,1,0:T(8,128)S(1)}, f32[4,32,128]{2,1,0:T(8,128)S(1)}, u32[]{:S(2)}, u32[]{:S(2)}) collective-permute-start(f32[4,32,128]{2,1,0:T(8,128)S(1)} %shade.1), channel_id=1, source_target_pairs={{0,8},{4,12},{8,0},{12,4},{16,24},{20,28},{24,16},{28,20},{1,9},{5... | collective-permute-start | bytes 196616 | tf_op jit(solution)/shard_map/ppermute | solution.py:358
  34.4 3.8 %collective-permute-done.5 = f32[4,32,128]{2,1,0:T(8,128)S(1)} collective-permute-done((f32[4,32,128]{2,1,0:T(8,128)S(1)}, f32[4,32,128]{2,1,0:T(8,128)S(1)}, u32[]{:S(2)}, u32[]{:S(2)}) %collective-permute-start.5) | collective-permute-done | bytes 65568 | tf_op jit(solution)/shard_map/ppermute | solution.py:358
  38.3 0.4 collective-permute-start.6
  38.7 5.4 %collective-permute-done.6 = f32[4,32,128]{2,1,0:T(8,128)S(1)} collective-permute-done((f32[4,32,128]{2,1,0:T(8,128)S(1)}, f32[4,32,128]{2,1,0:T(8,128)S(1)}, u32[]{:S(2)}, u32[]{:S(2)}) %collective-permute-start.6) | collective-permute-done | bytes 65568 | tf_op jit(solution)/shard_map/ppermute | solution.py:358
  44.2 0.1 collective-permute-start.7
  44.2 4.2 %collective-permute-done.7 = f32[4,32,128]{2,1,0:T(8,128)S(1)} collective-permute-done((f32[4,32,128]{2,1,0:T(8,128)S(1)}, f32[4,32,128]{2,1,0:T(8,128)S(1)}, u32[]{:S(2)}, u32[]{:S(2)}) %collective-permute-start.7) | collective-permute-done | bytes 65568 | tf_op jit(solution)/shard_map/ppermute | solution.py:363
  48.5 0.7 %pad_maximum_fusion = f32[4,32,256]{2,1,0:T(8,128)} fusion(f32[4,32,128]{2,1,0:T(8,128)S(1)} %get-tuple-element.22, f32[4,32,128]{2,1,0:T(8,128)S(1)} %get-tuple-element.21), kind=kLoop, calls=%fused_computation | loop fusion | flops 32768 | bytes 262144 | tf_op jit(solution)/shard_map/concatenate | solution.py:366
  (17 shorter events, 0.1 us)
Async XLA Ops:
  0.0 1.0 %copy-start = (bf16[4,8,32,256]{3,2,1,0:T(8,128)(2,1)S(1)}, bf16[4,8,32,256]{3,2,1,0:T(8,128)(2,1)}, u32[]{:S(2)}) copy-start(bf16[4,8,32,256]{3,2,1,0:T(8,128)(2,1)} %fields.1) | copy-start | bytes 1572868
  1.9 14.3 %collective-permute-start = (bf16[1056,128]{1,0:T(8,128)(2,1)S(1)}, bf16[1056,128]{1,0:T(8,128)(2,1)S(1)}, u32[]{:S(2)}, u32[]{:S(2)}) collective-permute-start(bf16[1056,128]{1,0:T(8,128)(2,1)S(1)} %get-tuple-element.14), channel_id=1, source_target_pairs={{0,4},{4,0},{8,12},{12,8},{16,20},{20,16},{24,28},{28,24},{1,5},{5... | collective-permute-start | bytes 811016 | tf_op jit(solution)/shard_map/ppermute | solution.py:326
  3.4 7.5 %collective-permute-start.1 = (bf16[800,128]{1,0:T(8,128)(2,1)S(1)}, bf16[800,128]{1,0:T(8,128)(2,1)S(1)}, u32[]{:S(2)}, u32[]{:S(2)}) collective-permute-start(bf16[800,128]{1,0:T(8,128)(2,1)S(1)} %get-tuple-element.15), channel_id=1, source_target_pairs={{4,12},{12,20},{20,28},{8,0},{16,8},{24,16},{5,13},{13,21},{21,29}... | collective-permute-start | bytes 614408 | tf_op jit(solution)/shard_map/ppermute | solution.py:328
  5.8 10.4 %collective-permute-start.2 = (bf16[800,128]{1,0:T(8,128)(2,1)S(1)}, bf16[800,128]{1,0:T(8,128)(2,1)S(1)}, u32[]{:S(2)}, u32[]{:S(2)}) collective-permute-start(bf16[800,128]{1,0:T(8,128)(2,1)S(1)} %get-tuple-element.16), channel_id=1, source_target_pairs={{4,8},{12,16},{20,24},{8,4},{16,12},{24,20},{5,9},{13,17},{21,25},... | collective-permute-start | bytes 614408 | tf_op jit(solution)/shard_map/ppermute | solution.py:327
  16.2 2.6 %copy-start.4 = (f32[32,12]{0,1:T(8,128)S(1)}, f32[32,12]{0,1:T(8,128)}, u32[]{:S(2)}) copy-start(f32[32,12]{0,1:T(8,128)} %param.6) | copy-start | bytes 4612
  16.3 3.9 %collective-permute-start.3 = (bf16[800,128]{1,0:T(8,128)(2,1)S(1)}, bf16[800,128]{1,0:T(8,128)(2,1)S(1)}, u32[]{:S(2)}, u32[]{:S(2)}) collective-permute-start(bf16[800,128]{1,0:T(8,128)(2,1)S(1)} %get-tuple-element.17), channel_id=1, source_target_pairs={{0,1},{1,0},{2,3},{3,2},{4,5},{5,4},{6,7},{7,6},{8,9},{9,8},{10,11... | collective-permute-start | bytes 614408 | tf_op jit(solution)/shard_map/ppermute | solution.py:343
  16.3 7.1 %collective-permute-start.4 = (bf16[800,128]{1,0:T(8,128)(2,1)S(1)}, bf16[800,128]{1,0:T(8,128)(2,1)S(1)}, u32[]{:S(2)}, u32[]{:S(2)}) collective-permute-start(bf16[800,128]{1,0:T(8,128)(2,1)S(1)} %get-tuple-element.18), channel_id=1, source_target_pairs={{1,2},{2,1},{5,6},{6,5},{9,10},{10,9},{13,14},{14,13},{17,18},{18,... | collective-permute-start | bytes 614408 | tf_op jit(solution)/shard_map/ppermute | solution.py:342
  19.0 0.7 %copy-start.1 = (f32[4,32]{1,0:T(4,128)S(1)}, f32[4,32]{1,0:T(4,128)}, u32[]{:S(2)}) copy-start(f32[4,32]{1,0:T(4,128)} %w_out.1) | copy-start | bytes 1540
  19.0 0.7 %copy-start.2 = (f32[32]{0:T(128)S(1)}, f32[32]{0:T(128)}, u32[]{:S(2)}) copy-start(f32[32]{0:T(128)} %param.7) | copy-start | bytes 388
  19.0 0.7 %copy-start.3 = (f32[4]{0:T(128)S(1)}, f32[4]{0:T(128)}, u32[]{:S(2)}) copy-start(f32[4]{0:T(128)} %param.9) | copy-start | bytes 52
  33.9 4.3 %collective-permute-start.5 = (f32[4,32,128]{2,1,0:T(8,128)S(1)}, f32[4,32,128]{2,1,0:T(8,128)S(1)}, u32[]{:S(2)}, u32[]{:S(2)}) collective-permute-start(f32[4,32,128]{2,1,0:T(8,128)S(1)} %shade.1), channel_id=1, source_target_pairs={{0,8},{4,12},{8,0},{12,4},{16,24},{20,28},{24,16},{28,20},{1,9},{5... | collective-permute-start | bytes 196616 | tf_op jit(solution)/shard_map/ppermute | solution.py:358
  38.3 5.8 %collective-permute-start.6 = (f32[4,32,128]{2,1,0:T(8,128)S(1)}, f32[4,32,128]{2,1,0:T(8,128)S(1)}, u32[]{:S(2)}, u32[]{:S(2)}) collective-permute-start(f32[4,32,128]{2,1,0:T(8,128)S(1)} %pad_maximum_fusion.1), channel_id=1, source_target_pairs={{0,16},{4,20},{8,24},{12,28},{16,0},{20,4},{24,8},{28,12},{1,17},{... | collective-permute-start | bytes 196616 | tf_op jit(solution)/shard_map/ppermute | solution.py:358
  44.2 4.3 %collective-permute-start.7 = (f32[4,32,128]{2,1,0:T(8,128)S(1)}, f32[4,32,128]{2,1,0:T(8,128)S(1)}, u32[]{:S(2)}, u32[]{:S(2)}) collective-permute-start(f32[4,32,128]{2,1,0:T(8,128)S(1)} %pad_maximum_fusion.2), channel_id=1, source_target_pairs={{0,4},{4,0},{8,12},{12,8},{16,20},{20,16},{24,28},{28,24},{1,5},{5... | collective-permute-start | bytes 196616 | tf_op jit(solution)/shard_map/ppermute | solution.py:363

commit v3 on v2

--- a/solution.py
+++ b/solution.py
@@ -224,7 +224,7 @@
                 ring.pop(0)
         return carry
 
-    lax.fori_loop(0, kk // 16, filter_rows, 0)
+    lax.fori_loop(0, kk // 16, filter_rows, 0, unroll=kk // 16)
     wide = 2 * LANES
     window = kw + 2 * kh
     hidden = w1.shape[1] // layers
@@ -275,7 +275,7 @@
         out[3, pl.ds(y + 1, 1), :] = front[:, LANES:]
         return carry
 
-    lax.fori_loop(0, rows // 2, shade, 0)
+    lax.fori_loop(0, rows // 2, shade, 0, unroll=8)
 
 
 def call(kernel, out_shape, operands, scratch=(), flops=0, name=None):

time: 49.4 us -> 45.8 us (0.927)
  Pallas kernels: 11.9 us -> 8.22 us
    pallas_call x4, Pallas kernels: 11.9 us -> 8.22 us  [call(): pl.pallas_call(kernel, out_shape=out_shape, in_specs=[vmem] * len(operand...]
where the time goes in v3:
time: 45.8 us; the launch traced here: 45.5 us
  waiting for transfers between devices  23.7 us (52%)
  starting transfers between devices  10.9 us (24%)
  Pallas kernels  8.22 us (18%)
  local copies, waits for them, and re-layouts  1.82 us (4%)
  other arithmetic  0.75 us (2%)
    ppermute x2, waiting for transfers between devices, local(): lax.ppermute(current, 'depth', [(i, i ^ step) for i in range(slabs)])  9.23 us
    pallas_call x4, Pallas kernels, call(): pl.pallas_call(kernel, out_shape=out_shape, in_specs=[vmem] * len(operand...  8.22 us
    ppermute x1, waiting for transfers between devices, local(): diagonal = lax.ppermute(other_halo, 'depth', diagonal_pairs)  5.25 us
    ppermute x1, waiting for transfers between devices, local(): other = lax.ppermute(current, 'depth', swap_pairs)  4.25 us
    ppermute x1, starting transfers between devices, local(): diagonal = lax.ppermute(other_halo, 'depth', diagonal_pairs)  3.45 us
    ppermute x1, waiting for transfers between devices, local(): second = lax.ppermute(second, 'row', across)  3.22 us
    ppermute x1, starting transfers between devices, local(): second = lax.ppermute(second, 'row', across)  2.5 us
    ppermute x1, starting transfers between devices, local(): straight = lax.ppermute(own_halo, 'depth', straight_pairs)  2.35 us
  transfers between devices with their start and end apart: 8, of which 6 were waited for; matrix products, arithmetic and copies ran while one was open for 0% of the time, Pallas kernels for 1%

profile of v3, /device:TPU:28, one launch (start us, length us, event | category | flops | bytes accessed | tf_op | source)
XLA Modules:
  0.0 45.5 jit_solution(12884257813135160619)
XLA Ops:
  0.0 1.0 %copy-done = bf16[4,8,32,256]{3,2,1,0:T(8,128)(2,1)S(1)} copy-done((bf16[4,8,32,256]{3,2,1,0:T(8,128)(2,1)S(1)}, bf16[4,8,32,256]{3,2,1,0:T(8,128)(2,1)}, u32[]{:S(2)}) %copy-start) | copy-done | bytes 524312
  1.0 0.8 %pack.1 = (bf16[1056,128]{1,0:T(8,128)(2,1)S(1)}, bf16[1056,128]{1,0:T(8,128)(2,1)S(1)}, bf16[800,128]{1,0:T(8,128)(2,1)S(1)}, bf16[800,128]{1,0:T(8,128)(2,1)S(1)}) custom-call(bf16[4,8,32,256]{3,2,1,0:T(8,128)(2,1)S(1)} %copy-done), custom_call_target="tpu_custom_call" | custom-call | bytes 1048576 | tf_op jit(solution)/shard_map/pack/pallas_call | solution.py:283
  1.9 1.6 %collective-permute-start = (bf16[1056,128]{1,0:T(8,128)(2,1)S(1)}, bf16[1056,128]{1,0:T(8,128)(2,1)S(1)}, u32[]{:S(2)}, u32[]{:S(2)}) collective-permute-start(bf16[1056,128]{1,0:T(8,128)(2,1)S(1)} %get-tuple-element.14), channel_id=1, source_target_pairs={{0,4},{4,0},{8,12},{12,8},{16,20},{20,16},{24,28},{28,24},{1,5},{5... | collective-permute-start | bytes 811016 | tf_op jit(solution)/shard_map/ppermute | solution.py:326
  3.4 2.4 %collective-permute-start.1 = (bf16[800,128]{1,0:T(8,128)(2,1)S(1)}, bf16[800,128]{1,0:T(8,128)(2,1)S(1)}, u32[]{:S(2)}, u32[]{:S(2)}) collective-permute-start(bf16[800,128]{1,0:T(8,128)(2,1)S(1)} %get-tuple-element.15), channel_id=1, source_target_pairs={{4,12},{12,20},{20,28},{8,0},{16,8},{24,16},{5,13},{13,21},{21,29}... | collective-permute-start | bytes 614408 | tf_op jit(solution)/shard_map/ppermute | solution.py:328
  5.8 3.4 %collective-permute-start.2 = (bf16[800,128]{1,0:T(8,128)(2,1)S(1)}, bf16[800,128]{1,0:T(8,128)(2,1)S(1)}, u32[]{:S(2)}, u32[]{:S(2)}) collective-permute-start(bf16[800,128]{1,0:T(8,128)(2,1)S(1)} %get-tuple-element.16), channel_id=1, source_target_pairs={{4,8},{12,16},{20,24},{8,4},{16,12},{24,20},{5,9},{13,17},{21,25},... | collective-permute-start | bytes 614408 | tf_op jit(solution)/shard_map/ppermute | solution.py:327
  9.3 1.7 %collective-permute-done.1.straight = bf16[800,128]{1,0:T(8,128)(2,1)S(1)} collective-permute-done((bf16[800,128]{1,0:T(8,128)(2,1)S(1)}, bf16[800,128]{1,0:T(8,128)(2,1)S(1)}, u32[]{:S(2)}, u32[]{:S(2)}) %collective-permute-start.1) | collective-permute-done | bytes 204832 | tf_op jit(solution)/shard_map/ppermute | solution.py:328
  11.0 5.3 %collective-permute-done.2.diagonal = bf16[800,128]{1,0:T(8,128)(2,1)S(1)} collective-permute-done((bf16[800,128]{1,0:T(8,128)(2,1)S(1)}, bf16[800,128]{1,0:T(8,128)(2,1)S(1)}, u32[]{:S(2)}, u32[]{:S(2)}) %collective-permute-start.2) | collective-permute-done | bytes 204832 | tf_op jit(solution)/shard_map/ppermute | solution.py:327
  16.2 0.0 collective-permute-done.swap
  16.3 0.1 collective-permute-start.3
  16.3 2.5 %collective-permute-start.4 = (bf16[800,128]{1,0:T(8,128)(2,1)S(1)}, bf16[800,128]{1,0:T(8,128)(2,1)S(1)}, u32[]{:S(2)}, u32[]{:S(2)}) collective-permute-start(bf16[800,128]{1,0:T(8,128)(2,1)S(1)} %get-tuple-element.18), channel_id=1, source_target_pairs={{1,2},{2,1},{5,6},{6,5},{9,10},{10,9},{13,14},{14,13},{17,18},{18,... | collective-permute-start | bytes 614408 | tf_op jit(solution)/shard_map/ppermute | solution.py:342
  18.9 0.0 copy-done.4
  18.9 0.1 copy.6.w_in
  19.0 0.7 %copy-done.1 = f32[4,32]{1,0:T(4,128)S(1)} copy-done((f32[4,32]{1,0:T(4,128)S(1)}, f32[4,32]{1,0:T(4,128)}, u32[]{:S(2)}) %copy-start.1) | copy-done | bytes 536
  19.6 0.5 %weights.1 = (bf16[2,256,512]{2,1,0:T(8,128)(2,1)S(1)}, f32[136,128]{1,0:T(8,128)S(1)}) custom-call(f32[32,12]{1,0:T(8,128)S(1)} %copy.6.w_in, f32[1,32]{1,0:T(1,128)S(1)} %bitcast.6, f32[4,32]{1,0:T(4,128)S(1)} %copy-done.1, f32[1,4]{1,0:T(1,128)S(1)} %bitcast.7), custom_call_target="tpu_custom_call" | custom-call | flops 100000000 | bytes 1048576 | tf_op jit(solution)/shard_map/weights/pallas_call | solution.py:283
  20.2 0.0 collective-permute-done.3.first
  20.2 3.2 %collective-permute-done.4.second = bf16[800,128]{1,0:T(8,128)(2,1)S(1)} collective-permute-done((bf16[800,128]{1,0:T(8,128)(2,1)S(1)}, bf16[800,128]{1,0:T(8,128)(2,1)S(1)}, u32[]{:S(2)}, u32[]{:S(2)}) %collective-permute-start.4) | collective-permute-done | bytes 204832 | tf_op jit(solution)/shard_map/ppermute | solution.py:342
  23.4 6.8 %shade.1 = f32[4,32,128]{2,1,0:T(8,128)S(1)} custom-call(bf16[1056,128]{1,0:T(8,128)(2,1)S(1)} %get-tuple-element.13.mine, bf16[1056,128]{1,0:T(8,128)(2,1)S(1)} %collective-permute-done.swap, bf16[800,128]{1,0:T(8,128)(2,1)S(1)} %collective-permute-done.1.straight, bf16[800,128]{1,0:T(8,128)(2,1)S(1)} %collective-permute-done.2.diagonal, ...), custom_call_target="tpu_custom_call" | custom-call | flops 10000000000 | bytes 1048576 | tf_op jit(solution)/shard_map/shade/pallas_call | solution.py:283
  30.2 0.5 %collective-permute-start.5 = (f32[4,32,128]{2,1,0:T(8,128)S(1)}, f32[4,32,128]{2,1,0:T(8,128)S(1)}, u32[]{:S(2)}, u32[]{:S(2)}) collective-permute-start(f32[4,32,128]{2,1,0:T(8,128)S(1)} %shade.1), channel_id=1, source_target_pairs={{0,8},{4,12},{8,0},{12,4},{16,24},{20,28},{24,16},{28,20},{1,9},{5... | collective-permute-start | bytes 196616 | tf_op jit(solution)/shard_map/ppermute | solution.py:358
  30.7 3.8 %collective-permute-done.5 = f32[4,32,128]{2,1,0:T(8,128)S(1)} collective-permute-done((f32[4,32,128]{2,1,0:T(8,128)S(1)}, f32[4,32,128]{2,1,0:T(8,128)S(1)}, u32[]{:S(2)}, u32[]{:S(2)}) %collective-permute-start.5) | collective-permute-done | bytes 65568 | tf_op jit(solution)/shard_map/ppermute | solution.py:358
  34.6 0.4 collective-permute-start.6
  35.0 5.4 %collective-permute-done.6 = f32[4,32,128]{2,1,0:T(8,128)S(1)} collective-permute-done((f32[4,32,128]{2,1,0:T(8,128)S(1)}, f32[4,32,128]{2,1,0:T(8,128)S(1)}, u32[]{:S(2)}, u32[]{:S(2)}) %collective-permute-start.6) | collective-permute-done | bytes 65568 | tf_op jit(solution)/shard_map/ppermute | solution.py:358
  40.5 0.1 collective-permute-start.7
  40.6 4.2 %collective-permute-done.7 = f32[4,32,128]{2,1,0:T(8,128)S(1)} collective-permute-done((f32[4,32,128]{2,1,0:T(8,128)S(1)}, f32[4,32,128]{2,1,0:T(8,128)S(1)}, u32[]{:S(2)}, u32[]{:S(2)}) %collective-permute-start.7) | collective-permute-done | bytes 65568 | tf_op jit(solution)/shard_map/ppermute | solution.py:363
  44.9 0.7 %pad_maximum_fusion = f32[4,32,256]{2,1,0:T(8,128)} fusion(f32[4,32,128]{2,1,0:T(8,128)S(1)} %get-tuple-element.22, f32[4,32,128]{2,1,0:T(8,128)S(1)} %get-tuple-element.21), kind=kLoop, calls=%fused_computation | loop fusion | flops 32768 | bytes 262144 | tf_op jit(solution)/shard_map/concatenate | solution.py:366
  (17 shorter events, 0.1 us)
Async XLA Ops:
  0.0 1.0 %copy-start = (bf16[4,8,32,256]{3,2,1,0:T(8,128)(2,1)S(1)}, bf16[4,8,32,256]{3,2,1,0:T(8,128)(2,1)}, u32[]{:S(2)}) copy-start(bf16[4,8,32,256]{3,2,1,0:T(8,128)(2,1)} %fields.1) | copy-start | bytes 1572868
  1.9 14.3 %collective-permute-start = (bf16[1056,128]{1,0:T(8,128)(2,1)S(1)}, bf16[1056,128]{1,0:T(8,128)(2,1)S(1)}, u32[]{:S(2)}, u32[]{:S(2)}) collective-permute-start(bf16[1056,128]{1,0:T(8,128)(2,1)S(1)} %get-tuple-element.14), channel_id=1, source_target_pairs={{0,4},{4,0},{8,12},{12,8},{16,20},{20,16},{24,28},{28,24},{1,5},{5... | collective-permute-start | bytes 811016 | tf_op jit(solution)/shard_map/ppermute | solution.py:326
  3.4 7.5 %collective-permute-start.1 = (bf16[800,128]{1,0:T(8,128)(2,1)S(1)}, bf16[800,128]{1,0:T(8,128)(2,1)S(1)}, u32[]{:S(2)}, u32[]{:S(2)}) collective-permute-start(bf16[800,128]{1,0:T(8,128)(2,1)S(1)} %get-tuple-element.15), channel_id=1, source_target_pairs={{4,12},{12,20},{20,28},{8,0},{16,8},{24,16},{5,13},{13,21},{21,29}... | collective-permute-start | bytes 614408 | tf_op jit(solution)/shard_map/ppermute | solution.py:328
  5.8 10.4 %collective-permute-start.2 = (bf16[800,128]{1,0:T(8,128)(2,1)S(1)}, bf16[800,128]{1,0:T(8,128)(2,1)S(1)}, u32[]{:S(2)}, u32[]{:S(2)}) collective-permute-start(bf16[800,128]{1,0:T(8,128)(2,1)S(1)} %get-tuple-element.16), channel_id=1, source_target_pairs={{4,8},{12,16},{20,24},{8,4},{16,12},{24,20},{5,9},{13,17},{21,25},... | collective-permute-start | bytes 614408 | tf_op jit(solution)/shard_map/ppermute | solution.py:327
  16.2 2.6 %copy-start.4 = (f32[32,12]{0,1:T(8,128)S(1)}, f32[32,12]{0,1:T(8,128)}, u32[]{:S(2)}) copy-start(f32[32,12]{0,1:T(8,128)} %param.6) | copy-start | bytes 4612
  16.3 3.9 %collective-permute-start.3 = (bf16[800,128]{1,0:T(8,128)(2,1)S(1)}, bf16[800,128]{1,0:T(8,128)(2,1)S(1)}, u32[]{:S(2)}, u32[]{:S(2)}) collective-permute-start(bf16[800,128]{1,0:T(8,128)(2,1)S(1)} %get-tuple-element.17), channel_id=1, source_target_pairs={{0,1},{1,0},{2,3},{3,2},{4,5},{5,4},{6,7},{7,6},{8,9},{9,8},{10,11... | collective-permute-start | bytes 614408 | tf_op jit(solution)/shard_map/ppermute | solution.py:343
  16.3 7.1 %collective-permute-start.4 = (bf16[800,128]{1,0:T(8,128)(2,1)S(1)}, bf16[800,128]{1,0:T(8,128)(2,1)S(1)}, u32[]{:S(2)}, u32[]{:S(2)}) collective-permute-start(bf16[800,128]{1,0:T(8,128)(2,1)S(1)} %get-tuple-element.18), channel_id=1, source_target_pairs={{1,2},{2,1},{5,6},{6,5},{9,10},{10,9},{13,14},{14,13},{17,18},{18,... | collective-permute-start | bytes 614408 | tf_op jit(solution)/shard_map/ppermute | solution.py:342
  19.0 0.7 %copy-start.1 = (f32[4,32]{1,0:T(4,128)S(1)}, f32[4,32]{1,0:T(4,128)}, u32[]{:S(2)}) copy-start(f32[4,32]{1,0:T(4,128)} %w_out.1) | copy-start | bytes 1540
  19.0 0.7 %copy-start.2 = (f32[32]{0:T(128)S(1)}, f32[32]{0:T(128)}, u32[]{:S(2)}) copy-start(f32[32]{0:T(128)} %param.7) | copy-start | bytes 388
  19.0 0.7 %copy-start.3 = (f32[4]{0:T(128)S(1)}, f32[4]{0:T(128)}, u32[]{:S(2)}) copy-start(f32[4]{0:T(128)} %param.9) | copy-start | bytes 52
  30.2 4.3 %collective-permute-start.5 = (f32[4,32,128]{2,1,0:T(8,128)S(1)}, f32[4,32,128]{2,1,0:T(8,128)S(1)}, u32[]{:S(2)}, u32[]{:S(2)}) collective-permute-start(f32[4,32,128]{2,1,0:T(8,128)S(1)} %shade.1), channel_id=1, source_target_pairs={{0,8},{4,12},{8,0},{12,4},{16,24},{20,28},{24,16},{28,20},{1,9},{5... | collective-permute-start | bytes 196616 | tf_op jit(solution)/shard_map/ppermute | solution.py:358
  34.6 5.8 %collective-permute-start.6 = (f32[4,32,128]{2,1,0:T(8,128)S(1)}, f32[4,32,128]{2,1,0:T(8,128)S(1)}, u32[]{:S(2)}, u32[]{:S(2)}) collective-permute-start(f32[4,32,128]{2,1,0:T(8,128)S(1)} %pad_maximum_fusion.1), channel_id=1, source_target_pairs={{0,16},{4,20},{8,24},{12,28},{16,0},{20,4},{24,8},{28,12},{1,17},{... | collective-permute-start | bytes 196616 | tf_op jit(solution)/shard_map/ppermute | solution.py:358
  40.5 4.3 %collective-permute-start.7 = (f32[4,32,128]{2,1,0:T(8,128)S(1)}, f32[4,32,128]{2,1,0:T(8,128)S(1)}, u32[]{:S(2)}, u32[]{:S(2)}) collective-permute-start(f32[4,32,128]{2,1,0:T(8,128)S(1)} %pad_maximum_fusion.2), channel_id=1, source_target_pairs={{0,4},{4,0},{8,12},{12,8},{16,20},{20,16},{24,28},{28,24},{1,5},{5... | collective-permute-start | bytes 196616 | tf_op jit(solution)/shard_map/ppermute | solution.py:363

commit v4 on v3

--- a/solution.py
+++ b/solution.py
@@ -150,11 +150,15 @@
     w2[outs * hidden :, :] = jnp.broadcast_to(values, (8, LANES))
 
 
-def shade_kernel(mine, swap, straight, diagonal, first, second, w1, w2, out, grid, edge, kept, *, layers, rows):
+def shade_kernel(*refs, layers, rows, own_rows, flip, masked):
+    if masked:
+        mine, swap, straight, diagonal, halo, w1, w2, done, out, grid, edge, kept = refs
+        out[...] = done[...]
+    else:
+        mine, swap, straight, diagonal, halo, w1, w2, out, grid, edge, kept = refs
     side = lax.axis_index("depth") & 1
     band = lax.axis_index("row")
-    bands = lax.axis_size("row")
-    odd = band & 1
+    top = 1 - (band & 1) if flip else band & 1
     kw, kh = layers * FIELDS, HALO * FIELDS
     kk = 2 * (kw + kh)
     offsets = (
@@ -163,44 +167,48 @@
         (straight, (1 - side) * (kh + 2 * kw), kh),
         (diagonal, side * (kh + 2 * kw), kh),
     )
+    own_place, halo_place = HALO * top, own_rows * (1 - top)
+    own_start, halo_start = (rows - own_rows) * (1 - top), (rows - HALO) * top
     i, j = iota((LANES, LANES), 0), iota((LANES, LANES), 1)
     taps = smooth_count(i - j).astype(BF16)
-    ir, ic = i // 3, i % 3
-    spot = jnp.where(side == 0, (j + 3) & (LANES - 1), j)
-    jr, jc = spot // 3, spot % 3
-    apart = jnp.where(side == 0, ic - jc + 3, jc - ic + 3)
-    border = jnp.where((ir == jr) & (i < 3 * rows) & (spot < 3 * rows), smooth_count(apart), 0.0).astype(BF16)
-    for source, at, width in offsets:
+
+    def border(shift):
+        spot = (j + jnp.where(side == 0, 3, 0) - 3 * shift) & (LANES - 1)
+        ir, ic, jr, jc = i // 3, i % 3, spot // 3, spot % 3
+        apart = jnp.where(side == 0, ic - jc + 3, jc - ic + 3)
+        return jnp.where((ir == jr) & (i < 3 * rows) & (spot < 3 * rows), smooth_count(apart), 0.0).astype(BF16)
+
+    own_border, halo_border = border(own_place - own_start), border(halo_place - halo_start)
+    start = 0
+    filtered_halo = dot(halo[0 : HALO * kk, :], taps)
+    edges = dot(halo[HALO * kk :, :], halo_border)
+    for index, (source, at, width) in enumerate(offsets):
         at = pl.ds(pl.multiple_of(at, 8), width)
-        filtered = dot(source[0 : rows * width, :], taps)
-        grid[HALO : HALO + rows, at, :] = filtered.reshape(rows, width, LANES)
-        edge[0, at, :] = dot(source[rows * width : rows * width + 32, :], border)[:width]
-    far = HALO + rows
-    for source, base, which in ((first, odd, 2 - odd), (second, 1 - odd, 1 + odd)):
-        place = (1 - base) * far
-        start = 0
-        filtered = dot(source[0 : HALO * kk, :], taps)
-        edges = dot(source[HALO * kk :, :], border)
-        for index, (unused, at, width) in enumerate(offsets):
-            at = pl.ds(pl.multiple_of(at, 8), width)
-            piece = filtered[start : start + HALO * width].reshape(HALO, width, LANES)
-            grid[pl.ds(place, HALO), at, :] = piece
-            edge[which, at, :] = edges[index * 32 : index * 32 + width]
-            start += HALO * width
+        span = pl.ds(pl.multiple_of(own_start * width, 16), own_rows * width)
+        filtered = dot(source[span, :], taps)
+        grid[pl.ds(own_place, own_rows), at, :] = filtered.reshape(own_rows, width, LANES)
+        edge[0, at, :] = dot(source[rows * width : rows * width + 32, :], own_border)[:width]
+        piece = filtered_halo[start : start + HALO * width].reshape(HALO, width, LANES)
+        grid[pl.ds(halo_place, HALO), at, :] = piece
+        edge[1, at, :] = edges[index * 32 : index * 32 + width]
+        start += HALO * width
+    total_rows = own_rows + HALO
+    out_rows = own_rows - HALO
     lane = iota((16, LANES), 1)
     near = ((lane + jnp.where(side == 0, 3, 0)) & (LANES - 1)) < 3
-    above = (band > 0).astype(F32)
-    below = (band < bands - 1).astype(F32)
+    before_in = jnp.where((top == 1) & (band == 0), 0.0, 1.0)
+    after_in = jnp.where((top == 0) & (band == lax.axis_size("row") - 1), 0.0, 1.0)
 
     def filter_rows(group, carry):
         at = pl.ds(pl.multiple_of(group * 16, 16), 16)
-        edges = [edge[k, at, :] for k in range(3)]
+        own_edge, halo_edge = edge[0, at, :], edge[1, at, :]
+        low_edge = jnp.where(top == 1, halo_edge, own_edge)
+        high_edge = jnp.where(top == 1, own_edge, halo_edge)
         chain = [None] * 6
         ring = []
-        for r in range(rows + 2 * HALO):
-            which = 1 if r < HALO else 0 if r < HALO + rows else 2
-            own_row = (r - HALO) % rows
-            turned = pltpu.roll(edges[which], (-3 * own_row) % LANES, 1)
+        for r in range(total_rows):
+            turned = low_edge if r < HALO else own_edge if r < own_rows else high_edge
+            turned = pltpu.roll(turned, (-3 * r) % LANES, 1)
             value = grid[r, at, :] + jnp.where(near, turned, 0.0)
             for level in range(6):
                 previous, chain[level] = chain[level], value
@@ -210,21 +218,22 @@
                 value = previous + value
             if value is None:
                 continue
-            y = r - HALO - 3
-            if y < 0:
-                value = value * above
-            elif y >= rows:
-                value = value * below
+            center = r - 3
+            if masked and center < HALO:
+                value = value * before_in
+            elif masked and center >= own_rows:
+                value = value * after_in
             ring.append(value)
             if len(ring) == 7:
                 slope = (ring[6] - ring[0]) - 9.0 * (ring[5] - ring[1]) + 45.0 * (ring[4] - ring[2])
-                y -= 3
+                y = center - 3 - HALO
                 kept[0, y, at, :], kept[2, y, at, :] = split(ring[3])
                 kept[1, y, at, :], kept[3, y, at, :] = split(slope)
                 ring.pop(0)
         return carry
 
     lax.fori_loop(0, kk // 16, filter_rows, 0, unroll=kk // 16)
+    first_row = HALO - own_place + own_start
     wide = 2 * LANES
     window = kw + 2 * kh
     hidden = w1.shape[1] // layers
@@ -269,13 +278,13 @@
                 color[c] = color[c] + weight / (1.0 + jnp.exp(-o[c]))
         for c in range(3):
             line = jnp.sum(color[c], axis=0, keepdims=True)
-            out[c, pl.ds(y, 1), :] = line[:, :LANES]
-            out[c, pl.ds(y + 1, 1), :] = line[:, LANES:]
-        out[3, pl.ds(y, 1), :] = front[:, :LANES]
-        out[3, pl.ds(y + 1, 1), :] = front[:, LANES:]
+            out[c, pl.ds(first_row + y, 1), :] = line[:, :LANES]
+            out[c, pl.ds(first_row + y + 1, 1), :] = line[:, LANES:]
+        out[3, pl.ds(first_row + y, 1), :] = front[:, :LANES]
+        out[3, pl.ds(first_row + y + 1, 1), :] = front[:, LANES:]
         return carry
 
-    lax.fori_loop(0, rows // 2, shade, 0, unroll=8)
+    lax.fori_loop(0, out_rows // 2, shade, 0, unroll=out_rows // 2)
 
 
 def call(kernel, out_shape, operands, scratch=(), flops=0, name=None):
@@ -335,24 +344,32 @@
         flops=10**8,
         name="weights",
     )
+    mine, w1, w2 = lax.optimization_barrier((mine, w1, w2))
     message = shape((HALO * kk + 4 * 32, LANES), BF16)
     first, second = call(band_kernel, [message, message], (mine, swap, straight, diagonal), name="band")
     within = [(i, i ^ 1) for i in range(bands)]
     across = [(i, i + 1) for i in range(1, bands - 1, 2)] + [(i + 1, i) for i in range(1, bands - 1, 2)]
     second = lax.ppermute(second, "row", across)
     first = lax.ppermute(first, "row", within)
-    current = call(
-        functools.partial(shade_kernel, layers=layers, rows=rows),
-        shape((4, rows, LANES), F32),
-        (mine, swap, straight, diagonal, first, second, w1, w2),
-        [
-            pltpu.VMEM((rows + 2 * HALO, kk, LANES), F32),
-            pltpu.VMEM((3, kk, LANES), F32),
-            pltpu.VMEM((4, rows, kk, LANES), BF16),
-        ],
-        flops=10**10,
-        name="shade",
-    )
+
+    def shaded(own_rows, flip, halo, previous, name):
+        return call(
+            functools.partial(
+                shade_kernel, layers=layers, rows=rows, own_rows=own_rows, flip=flip, masked=bool(previous)
+            ),
+            shape((4, rows, LANES), F32),
+            (mine, swap, straight, diagonal, halo, w1, w2, *previous),
+            [
+                pltpu.VMEM((own_rows + HALO, kk, LANES), F32),
+                pltpu.VMEM((2, kk, LANES), F32),
+                pltpu.VMEM((4, own_rows - HALO, kk, LANES), BF16),
+            ],
+            flops=10**10,
+            name=name,
+        )
+
+    current = shaded(rows, False, first, (), "shade_most")
+    current = shaded(2 * HALO, True, second, (current,), "shade_rest")
     step = 2
     while step < slabs:
         received = lax.ppermute(current, "depth", [(i, i ^ step) for i in range(slabs)])

time: 45.8 us -> 43 us (0.939)
  the two profiles are of different devices: /device:TPU:28 before, /device:TPU:0 now
where the time goes in v4:
time: 43 us; the launch traced here: 42.8 us
  starting transfers between devices  17.3 us (40%)
  waiting for transfers between devices  14.3 us (33%)
  Pallas kernels  8.54 us (20%)
  local copies, waits for them, and re-layouts  1.82 us (4%)
  other arithmetic  0.75 us (2%)
    pallas_call x5, Pallas kernels, call(): pl.pallas_call(kernel, out_shape=out_shape, in_specs=[vmem] * len(operand...  8.54 us
    ppermute x2, starting transfers between devices, local(): lax.ppermute(current, 'depth', [(i, i ^ step) for i in range(slabs)])  7.97 us
    ppermute x1, waiting for transfers between devices, local(): straight = lax.ppermute(own_halo, 'depth', straight_pairs)  6.25 us
    ppermute x2, waiting for transfers between devices, local(): lax.ppermute(current, 'depth', [(i, i ^ step) for i in range(slabs)])  4.9 us
    ppermute x1, starting transfers between devices, local(): other = lax.ppermute(current, 'depth', swap_pairs)  3.58 us
    ppermute x1, starting transfers between devices, local(): swap = lax.ppermute(theirs, 'depth', swap_pairs)  3 us
    ppermute x1, waiting for transfers between devices, local(): other = lax.ppermute(current, 'depth', swap_pairs)  2.37 us
    unnamed x11, local copies, waits for them, and re-layouts  1.82 us
  transfers between devices with their start and end apart: 8, of which 5 were waited for; matrix products, arithmetic and copies ran while one was open for 0% of the time, Pallas kernels for 14%

profile of v4, /device:TPU:0, one launch (start us, length us, event | category | flops | bytes accessed | tf_op | source)
XLA Modules:
  0.0 42.8 jit_solution(624789194124827566)
XLA Ops:
  0.0 1.0 %copy-done = bf16[4,8,32,256]{3,2,1,0:T(8,128)(2,1)S(1)} copy-done((bf16[4,8,32,256]{3,2,1,0:T(8,128)(2,1)S(1)}, bf16[4,8,32,256]{3,2,1,0:T(8,128)(2,1)}, u32[]{:S(2)}) %copy-start) | copy-done | bytes 524312
  1.0 0.8 %pack.1 = (bf16[1056,128]{1,0:T(8,128)(2,1)S(1)}, bf16[1056,128]{1,0:T(8,128)(2,1)S(1)}, bf16[800,128]{1,0:T(8,128)(2,1)S(1)}, bf16[800,128]{1,0:T(8,128)(2,1)S(1)}) custom-call(bf16[4,8,32,256]{3,2,1,0:T(8,128)(2,1)S(1)} %copy-done), custom_call_target="tpu_custom_call" | custom-call | bytes 1048576 | tf_op jit(solution)/shard_map/pack/pallas_call | solution.py:292
  1.9 3.0 %collective-permute-start = (bf16[1056,128]{1,0:T(8,128)(2,1)S(1)}, bf16[1056,128]{1,0:T(8,128)(2,1)S(1)}, u32[]{:S(2)}, u32[]{:S(2)}) collective-permute-start(bf16[1056,128]{1,0:T(8,128)(2,1)S(1)} %get-tuple-element.20), channel_id=1, source_target_pairs={{0,4},{4,0},{8,12},{12,8},{16,20},{20,16},{24,28},{28,24},{1,5},{5... | collective-permute-start | bytes 811016 | tf_op jit(solution)/shard_map/ppermute | solution.py:335
  4.9 1.3 %collective-permute-start.1 = (bf16[800,128]{1,0:T(8,128)(2,1)S(1)}, bf16[800,128]{1,0:T(8,128)(2,1)S(1)}, u32[]{:S(2)}, u32[]{:S(2)}) collective-permute-start(bf16[800,128]{1,0:T(8,128)(2,1)S(1)} %get-tuple-element.21), channel_id=1, source_target_pairs={{4,12},{12,20},{20,28},{8,0},{16,8},{24,16},{5,13},{13,21},{21,29}... | collective-permute-start | bytes 614408 | tf_op jit(solution)/shard_map/ppermute | solution.py:337
  6.2 0.7 %collective-permute-start.2 = (bf16[800,128]{1,0:T(8,128)(2,1)S(1)}, bf16[800,128]{1,0:T(8,128)(2,1)S(1)}, u32[]{:S(2)}, u32[]{:S(2)}) collective-permute-start(bf16[800,128]{1,0:T(8,128)(2,1)S(1)} %get-tuple-element.22), channel_id=1, source_target_pairs={{4,8},{12,16},{20,24},{8,4},{16,12},{24,20},{5,9},{13,17},{21,25},... | collective-permute-start | bytes 614408 | tf_op jit(solution)/shard_map/ppermute | solution.py:336
  6.9 0.1 copy.6.w_in
  7.0 0.7 %copy-done.1 = f32[4,32]{1,0:T(4,128)S(1)} copy-done((f32[4,32]{1,0:T(4,128)S(1)}, f32[4,32]{1,0:T(4,128)}, u32[]{:S(2)}) %copy-start.1) | copy-done | bytes 536
  7.6 0.5 %weights.1 = (bf16[2,256,512]{2,1,0:T(8,128)(2,1)S(1)}, f32[136,128]{1,0:T(8,128)S(1)}) custom-call(f32[32,12]{1,0:T(8,128)S(1)} %copy.6.w_in, f32[1,32]{1,0:T(1,128)S(1)} %bitcast.6, f32[4,32]{1,0:T(4,128)S(1)} %copy-done.1, f32[1,4]{1,0:T(1,128)S(1)} %bitcast.7), custom_call_target="tpu_custom_call" | custom-call | flops 100000000 | bytes 1048576 | tf_op jit(solution)/shard_map/weights/pallas_call | solution.py:292
  8.2 6.2 %collective-permute-done.1.straight.refs_2_ = bf16[800,128]{1,0:T(8,128)(2,1)S(1)} collective-permute-done((bf16[800,128]{1,0:T(8,128)(2,1)S(1)}, bf16[800,128]{1,0:T(8,128)(2,1)S(1)}, u32[]{:S(2)}, u32[]{:S(2)}) %collective-permute-start.1) | collective-permute-done | bytes 204832 | tf_op jit(solution)/shard_map/ppermute | solution.py:337
  14.4 0.0 collective-permute-done.2.diagonal.refs_3_
  14.4 0.0 collective-permute-done.swap.refs_1_
  14.5 0.1 collective-permute-start.4
  14.6 0.7 %collective-permute-start.3 = (bf16[800,128]{1,0:T(8,128)(2,1)S(1)}, bf16[800,128]{1,0:T(8,128)(2,1)S(1)}, u32[]{:S(2)}, u32[]{:S(2)}) collective-permute-start(bf16[800,128]{1,0:T(8,128)(2,1)S(1)} %get-tuple-element.23), channel_id=1, source_target_pairs={{1,2},{2,1},{5,6},{6,5},{9,10},{10,9},{13,14},{14,13},{17,18},{18,... | collective-permute-start | bytes 614408 | tf_op jit(solution)/shard_map/ppermute | solution.py:352
  15.3 0.8 %collective-permute-done.4.refs_4_ = bf16[800,128]{1,0:T(8,128)(2,1)S(1)} collective-permute-done((bf16[800,128]{1,0:T(8,128)(2,1)S(1)}, bf16[800,128]{1,0:T(8,128)(2,1)S(1)}, u32[]{:S(2)}, u32[]{:S(2)}) %collective-permute-start.4) | collective-permute-done | bytes 204832 | tf_op jit(solution)/shard_map/ppermute | solution.py:353
  16.0 5.4 %shade_most.1.refs_7_ = f32[4,32,128]{2,1,0:T(8,128)S(1)} custom-call(bf16[1056,128]{1,0:T(8,128)(2,1)S(1)} %get-tuple-element.19.mine.refs_0_, bf16[1056,128]{1,0:T(8,128)(2,1)S(1)} %collective-permute-done.swap.refs_1_, bf16[800,128]{1,0:T(8,128)(2,1)S(1)} %collective-permute-done.1.straight.refs_2_, ...), custom_call_target="tpu_custom_call" | custom-call | flops 10000000000 | bytes 1048576 | tf_op jit(solution)/shard_map/shade_most/pallas_call | solution.py:292
  21.4 0.0 collective-permute-done.3.refs_4_
  21.4 1.8 %shade_rest.1 = f32[4,32,128]{2,1,0:T(8,128)S(1)} custom-call(bf16[1056,128]{1,0:T(8,128)(2,1)S(1)} %get-tuple-element.19.mine.refs_0_, bf16[1056,128]{1,0:T(8,128)(2,1)S(1)} %collective-permute-done.swap.refs_1_, bf16[800,128]{1,0:T(8,128)(2,1)S(1)} %collective-permute-done.1.straight.refs_2_, bf16[800,128]{1,0:T(8,128)(2,1)S(1)} %collective-permute-done.2.diagonal.refs_3_, ...), custom_call_target="tpu_custom_call" | custom-call | flops 10000000000 | bytes 1048576 | tf_op jit(solution)/shard_map/shade_rest/pallas_call | solution.py:292
  23.2 4.9 %collective-permute-start.5 = (f32[4,32,128]{2,1,0:T(8,128)S(1)}, f32[4,32,128]{2,1,0:T(8,128)S(1)}, u32[]{:S(2)}, u32[]{:S(2)}) collective-permute-start(f32[4,32,128]{2,1,0:T(8,128)S(1)} %shade_rest.1), channel_id=1, source_target_pairs={{0,8},{4,12},{8,0},{12,4},{16,24},{20,28},{24,16},{28,20},{1,9},{5... | collective-permute-start | bytes 196616 | tf_op jit(solution)/shard_map/ppermute | solution.py:375
  28.0 2.2 %collective-permute-done.5 = f32[4,32,128]{2,1,0:T(8,128)S(1)} collective-permute-done((f32[4,32,128]{2,1,0:T(8,128)S(1)}, f32[4,32,128]{2,1,0:T(8,128)S(1)}, u32[]{:S(2)}, u32[]{:S(2)}) %collective-permute-start.5) | collective-permute-done | bytes 65568 | tf_op jit(solution)/shard_map/ppermute | solution.py:375
  30.3 3.1 %collective-permute-start.6 = (f32[4,32,128]{2,1,0:T(8,128)S(1)}, f32[4,32,128]{2,1,0:T(8,128)S(1)}, u32[]{:S(2)}, u32[]{:S(2)}) collective-permute-start(f32[4,32,128]{2,1,0:T(8,128)S(1)} %pad_maximum_fusion.1), channel_id=1, source_target_pairs={{0,16},{4,20},{8,24},{12,28},{16,0},{20,4},{24,8},{28,12},{1,17},{... | collective-permute-start | bytes 196616 | tf_op jit(solution)/shard_map/ppermute | solution.py:375
  33.4 2.7 %collective-permute-done.6 = f32[4,32,128]{2,1,0:T(8,128)S(1)} collective-permute-done((f32[4,32,128]{2,1,0:T(8,128)S(1)}, f32[4,32,128]{2,1,0:T(8,128)S(1)}, u32[]{:S(2)}, u32[]{:S(2)}) %collective-permute-start.6) | collective-permute-done | bytes 65568 | tf_op jit(solution)/shard_map/ppermute | solution.py:375
  36.2 3.6 %collective-permute-start.7 = (f32[4,32,128]{2,1,0:T(8,128)S(1)}, f32[4,32,128]{2,1,0:T(8,128)S(1)}, u32[]{:S(2)}, u32[]{:S(2)}) collective-permute-start(f32[4,32,128]{2,1,0:T(8,128)S(1)} %pad_maximum_fusion.2), channel_id=1, source_target_pairs={{0,4},{4,0},{8,12},{12,8},{16,20},{20,16},{24,28},{28,24},{1,5},{5... | collective-permute-start | bytes 196616 | tf_op jit(solution)/shard_map/ppermute | solution.py:380
  39.7 2.4 %collective-permute-done.7 = f32[4,32,128]{2,1,0:T(8,128)S(1)} collective-permute-done((f32[4,32,128]{2,1,0:T(8,128)S(1)}, f32[4,32,128]{2,1,0:T(8,128)S(1)}, u32[]{:S(2)}, u32[]{:S(2)}) %collective-permute-start.7) | collective-permute-done | bytes 65568 | tf_op jit(solution)/shard_map/ppermute | solution.py:380
  42.1 0.7 %pad_maximum_fusion = f32[4,32,256]{2,1,0:T(8,128)} fusion(f32[4,32,128]{2,1,0:T(8,128)S(1)} %get-tuple-element.28, f32[4,32,128]{2,1,0:T(8,128)S(1)} %get-tuple-element.27), kind=kLoop, calls=%fused_computation | loop fusion | flops 32768 | bytes 262144 | tf_op jit(solution)/shard_map/concatenate | solution.py:383
  (18 shorter events, 0.1 us)
Async XLA Ops:
  0.0 1.0 %copy-start = (bf16[4,8,32,256]{3,2,1,0:T(8,128)(2,1)S(1)}, bf16[4,8,32,256]{3,2,1,0:T(8,128)(2,1)}, u32[]{:S(2)}) copy-start(bf16[4,8,32,256]{3,2,1,0:T(8,128)(2,1)} %fields.1) | copy-start | bytes 1572868
  1.0 5.8 %copy-start.4 = (f32[32,12]{0,1:T(8,128)S(1)}, f32[32,12]{0,1:T(8,128)}, u32[]{:S(2)}) copy-start(f32[32,12]{0,1:T(8,128)} %param.6) | copy-start | bytes 4612
  1.9 12.6 %collective-permute-start = (bf16[1056,128]{1,0:T(8,128)(2,1)S(1)}, bf16[1056,128]{1,0:T(8,128)(2,1)S(1)}, u32[]{:S(2)}, u32[]{:S(2)}) collective-permute-start(bf16[1056,128]{1,0:T(8,128)(2,1)S(1)} %get-tuple-element.20), channel_id=1, source_target_pairs={{0,4},{4,0},{8,12},{12,8},{16,20},{20,16},{24,28},{28,24},{1,5},{5... | collective-permute-start | bytes 811016 | tf_op jit(solution)/shard_map/ppermute | solution.py:335
  4.9 9.5 %collective-permute-start.1 = (bf16[800,128]{1,0:T(8,128)(2,1)S(1)}, bf16[800,128]{1,0:T(8,128)(2,1)S(1)}, u32[]{:S(2)}, u32[]{:S(2)}) collective-permute-start(bf16[800,128]{1,0:T(8,128)(2,1)S(1)} %get-tuple-element.21), channel_id=1, source_target_pairs={{4,12},{12,20},{20,28},{8,0},{16,8},{24,16},{5,13},{13,21},{21,29}... | collective-permute-start | bytes 614408 | tf_op jit(solution)/shard_map/ppermute | solution.py:337
  6.2 8.3 %collective-permute-start.2 = (bf16[800,128]{1,0:T(8,128)(2,1)S(1)}, bf16[800,128]{1,0:T(8,128)(2,1)S(1)}, u32[]{:S(2)}, u32[]{:S(2)}) collective-permute-start(bf16[800,128]{1,0:T(8,128)(2,1)S(1)} %get-tuple-element.22), channel_id=1, source_target_pairs={{4,8},{12,16},{20,24},{8,4},{16,12},{24,20},{5,9},{13,17},{21,25},... | collective-permute-start | bytes 614408 | tf_op jit(solution)/shard_map/ppermute | solution.py:336
  7.0 0.7 %copy-start.1 = (f32[4,32]{1,0:T(4,128)S(1)}, f32[4,32]{1,0:T(4,128)}, u32[]{:S(2)}) copy-start(f32[4,32]{1,0:T(4,128)} %w_out.1) | copy-start | bytes 1540
  7.0 0.7 %copy-start.2 = (f32[32]{0:T(128)S(1)}, f32[32]{0:T(128)}, u32[]{:S(2)}) copy-start(f32[32]{0:T(128)} %param.7) | copy-start | bytes 388
  7.0 0.7 %copy-start.3 = (f32[4]{0:T(128)S(1)}, f32[4]{0:T(128)}, u32[]{:S(2)}) copy-start(f32[4]{0:T(128)} %param.9) | copy-start | bytes 52
  14.5 1.5 %collective-permute-start.4 = (bf16[800,128]{1,0:T(8,128)(2,1)S(1)}, bf16[800,128]{1,0:T(8,128)(2,1)S(1)}, u32[]{:S(2)}, u32[]{:S(2)}) collective-permute-start(bf16[800,128]{1,0:T(8,128)(2,1)S(1)} %get-tuple-element.26), channel_id=1, source_target_pairs={{0,1},{1,0},{2,3},{3,2},{4,5},{5,4},{6,7},{7,6},{8,9},{9,8},{10,11... | collective-permute-start | bytes 614408 | tf_op jit(solution)/shard_map/ppermute | solution.py:353
  14.6 6.8 %collective-permute-start.3 = (bf16[800,128]{1,0:T(8,128)(2,1)S(1)}, bf16[800,128]{1,0:T(8,128)(2,1)S(1)}, u32[]{:S(2)}, u32[]{:S(2)}) collective-permute-start(bf16[800,128]{1,0:T(8,128)(2,1)S(1)} %get-tuple-element.23), channel_id=1, source_target_pairs={{1,2},{2,1},{5,6},{6,5},{9,10},{10,9},{13,14},{14,13},{17,18},{18,... | collective-permute-start | bytes 614408 | tf_op jit(solution)/shard_map/ppermute | solution.py:352
  23.2 7.1 %collective-permute-start.5 = (f32[4,32,128]{2,1,0:T(8,128)S(1)}, f32[4,32,128]{2,1,0:T(8,128)S(1)}, u32[]{:S(2)}, u32[]{:S(2)}) collective-permute-start(f32[4,32,128]{2,1,0:T(8,128)S(1)} %shade_rest.1), channel_id=1, source_target_pairs={{0,8},{4,12},{8,0},{12,4},{16,24},{20,28},{24,16},{28,20},{1,9},{5... | collective-permute-start | bytes 196616 | tf_op jit(solution)/shard_map/ppermute | solution.py:375
  30.3 5.8 %collective-permute-start.6 = (f32[4,32,128]{2,1,0:T(8,128)S(1)}, f32[4,32,128]{2,1,0:T(8,128)S(1)}, u32[]{:S(2)}, u32[]{:S(2)}) collective-permute-start(f32[4,32,128]{2,1,0:T(8,128)S(1)} %pad_maximum_fusion.1), channel_id=1, source_target_pairs={{0,16},{4,20},{8,24},{12,28},{16,0},{20,4},{24,8},{28,12},{1,17},{... | collective-permute-start | bytes 196616 | tf_op jit(solution)/shard_map/ppermute | solution.py:375
  36.2 6.0 %collective-permute-start.7 = (f32[4,32,128]{2,1,0:T(8,128)S(1)}, f32[4,32,128]{2,1,0:T(8,128)S(1)}, u32[]{:S(2)}, u32[]{:S(2)}) collective-permute-start(f32[4,32,128]{2,1,0:T(8,128)S(1)} %pad_maximum_fusion.2), channel_id=1, source_target_pairs={{0,4},{4,0},{8,12},{12,8},{16,20},{20,16},{24,28},{28,24},{1,5},{5... | collective-permute-start | bytes 196616 | tf_op jit(solution)/shard_map/ppermute | solution.py:380

commit v5 on v3

--- a/solution.py
+++ b/solution.py
@@ -121,6 +121,7 @@
     kappa = iota((hidden, width), 1)
     part1 = jnp.where(kappa == 6 * window, bias, jnp.where(kappa == 6 * window + 1, bias, part1))
     scale = 1.0 / 64.0**3
+    row_sign = jnp.where((lax.axis_index("row") & 1) == 0, -1.0 / 60.0, 1.0 / 60.0)
     z, place = iota((layers, width), 0), iota((layers, width), 1)
     inner = place % (2 * window)
     slope_kind = inner >= window
@@ -136,7 +137,7 @@
                 at = base + half * layers + z + sign * offset
                 inside = ((at >= 0) & (at < total)).astype(F32)
                 slope = slope + (inside * (sign * count)) * smooth_count(distance - sign * offset)
-        center = jnp.where(last, 1.0, jnp.where(slope_kind, center * (1.0 / 60.0), center))
+        center = jnp.where(last, 1.0, jnp.where(slope_kind, center * row_sign, center))
         product = center[None] * part1[:, None, :] + (slope * (scale / 60.0))[None] * part2[:, None, :]
         high = product.astype(BF16).astype(F32)
         chosen = jnp.where(low_column[None], product - high, high)
@@ -144,87 +145,74 @@
     outs = w_out.shape[0]
     for c in range(outs):
         values = jnp.sum(jnp.where(eye, w_out[c : c + 1, :], 0.0), axis=1, keepdims=True)
-        w2[c * hidden : (c + 1) * hidden, :] = jnp.broadcast_to(values, (hidden, LANES))
+        factor = 0.5 if c < 3 else 1.0
+        w2[c * hidden : (c + 1) * hidden, :] = jnp.broadcast_to(factor * values, (hidden, LANES))
     pick = iota((8, outs), 0) == iota((8, outs), 1)
     values = jnp.sum(jnp.where(pick, b_out[...], 0.0), axis=1, keepdims=True)
+    values = jnp.where(iota((8, 1), 0) < 3, 0.5 * values, values)
     w2[outs * hidden :, :] = jnp.broadcast_to(values, (8, LANES))
 
 
-def shade_kernel(mine, swap, straight, diagonal, first, second, w1, w2, out, grid, edge, kept, *, layers, rows):
-    side = lax.axis_index("depth") & 1
-    band = lax.axis_index("row")
-    bands = lax.axis_size("row")
-    odd = band & 1
+def places(side, layers):
     kw, kh = layers * FIELDS, HALO * FIELDS
-    kk = 2 * (kw + kh)
-    offsets = (
-        (mine, kh + side * kw, kw),
-        (swap, kh + (1 - side) * kw, kw),
-        (straight, (1 - side) * (kh + 2 * kw), kh),
-        (diagonal, side * (kh + 2 * kw), kh),
-    )
+    far = kh + 2 * kw
+    return ((kh + side * kw, kw), (kh + (1 - side) * kw, kw), ((1 - side) * far, kh), (side * far, kh))
+
+
+def tap_matrix():
+    return smooth_count(iota((LANES, LANES), 0) - iota((LANES, LANES), 1)).astype(BF16)
+
+
+def border(side, first, sign, low, high):
     i, j = iota((LANES, LANES), 0), iota((LANES, LANES), 1)
-    taps = smooth_count(i - j).astype(BF16)
-    ir, ic = i // 3, i % 3
-    spot = jnp.where(side == 0, (j + 3) & (LANES - 1), j)
-    jr, jc = spot // 3, spot % 3
+    spot = (j + jnp.where(side == 0, 3, 0)) & (LANES - 1)
+    ir, ic, jr, jc = i // 3, i % 3, spot // 3, spot % 3
     apart = jnp.where(side == 0, ic - jc + 3, jc - ic + 3)
-    border = jnp.where((ir == jr) & (i < 3 * rows) & (spot < 3 * rows), smooth_count(apart), 0.0).astype(BF16)
-    for source, at, width in offsets:
+    here = (ir == first + sign * jr) & (jr >= low) & (jr < high)
+    return jnp.where(here, smooth_count(apart), 0.0).astype(BF16)
+
+
+def place_halo(halo, grid, edge, layers, side, flipped, edges):
+    kk = 2 * (layers + HALO) * FIELDS
+    filtered = dot(halo[0 : HALO * kk, :], tap_matrix())
+    added = dot(halo[HALO * kk :, :], edges)
+    start = 0
+    for index, (at, width) in enumerate(places(side, layers)):
         at = pl.ds(pl.multiple_of(at, 8), width)
-        filtered = dot(source[0 : rows * width, :], taps)
-        grid[HALO : HALO + rows, at, :] = filtered.reshape(rows, width, LANES)
-        edge[0, at, :] = dot(source[rows * width : rows * width + 32, :], border)[:width]
-    far = HALO + rows
-    for source, base, which in ((first, odd, 2 - odd), (second, 1 - odd, 1 + odd)):
-        place = (1 - base) * far
-        start = 0
-        filtered = dot(source[0 : HALO * kk, :], taps)
-        edges = dot(source[HALO * kk :, :], border)
-        for index, (unused, at, width) in enumerate(offsets):
-            at = pl.ds(pl.multiple_of(at, 8), width)
-            piece = filtered[start : start + HALO * width].reshape(HALO, width, LANES)
-            grid[pl.ds(place, HALO), at, :] = piece
-            edge[which, at, :] = edges[index * 32 : index * 32 + width]
-            start += HALO * width
-    lane = iota((16, LANES), 1)
-    near = ((lane + jnp.where(side == 0, 3, 0)) & (LANES - 1)) < 3
-    above = (band > 0).astype(F32)
-    below = (band < bands - 1).astype(F32)
-
-    def filter_rows(group, carry):
-        at = pl.ds(pl.multiple_of(group * 16, 16), 16)
-        edges = [edge[k, at, :] for k in range(3)]
-        chain = [None] * 6
-        ring = []
-        for r in range(rows + 2 * HALO):
-            which = 1 if r < HALO else 0 if r < HALO + rows else 2
-            own_row = (r - HALO) % rows
-            turned = pltpu.roll(edges[which], (-3 * own_row) % LANES, 1)
-            value = grid[r, at, :] + jnp.where(near, turned, 0.0)
-            for level in range(6):
-                previous, chain[level] = chain[level], value
-                if previous is None:
-                    value = None
-                    break
-                value = previous + value
-            if value is None:
-                continue
-            y = r - HALO - 3
-            if y < 0:
-                value = value * above
-            elif y >= rows:
-                value = value * below
-            ring.append(value)
-            if len(ring) == 7:
-                slope = (ring[6] - ring[0]) - 9.0 * (ring[5] - ring[1]) + 45.0 * (ring[4] - ring[2])
-                y -= 3
-                kept[0, y, at, :], kept[2, y, at, :] = split(ring[3])
-                kept[1, y, at, :], kept[3, y, at, :] = split(slope)
-                ring.pop(0)
-        return carry
-
-    lax.fori_loop(0, kk // 16, filter_rows, 0, unroll=kk // 16)
+        for row in range(HALO):
+            grid[jnp.where(flipped, HALO - 1 - row, row), at, :] = filtered[start : start + width]
+            start += width
+        edge[at, :] = added[index * 32 : index * 32 + width]
+
+
+def near_cut(side):
+    return ((iota((16, LANES), 1) + jnp.where(side == 0, 3, 0)) & (LANES - 1)) < 3
+
+
+def next_row(value, chain, ring, scale=None):
+    for level in range(6):
+        previous, chain[level] = chain[level], value
+        if previous is None:
+            return None
+        value = previous + value
+    if scale is not None:
+        value = value * scale
+    ring.append(value)
+    if len(ring) < 7:
+        return None
+    slope = (ring[6] - ring[0]) - 9.0 * (ring[5] - ring[1]) + 45.0 * (ring[4] - ring[2])
+    center = ring[3]
+    ring.pop(0)
+    return center, slope
+
+
+def keep(kept, y, at, center, slope):
+    kept[0, y, at, :], kept[2, y, at, :] = split(center)
+    kept[1, y, at, :], kept[3, y, at, :] = split(slope)
+
+
+def shade_rows(kept, w1, w2, out, layers, first, flipped, last):
+    kw, kh = layers * FIELDS, HALO * FIELDS
     wide = 2 * LANES
     window = kw + 2 * kh
     hidden = w1.shape[1] // layers
@@ -237,8 +225,10 @@
         line = w2[index : index + 1, :]
         return jnp.broadcast_to(jnp.concatenate([line, line], 1), (layers, wide))
 
-    def shade(pair, carry):
-        y = 2 * pair
+    def target(k):
+        return pl.ds(jnp.where(flipped, last - first - k, first + k), 1)
+
+    for y in range(0, kept.shape[1], 2):
         total = jnp.zeros((1, wide), F32)
         front = jnp.ones((1, wide), F32)
         color = [jnp.zeros((layers, wide), F32) for unused in range(3)]
@@ -255,7 +245,7 @@
                 for c in range(4):
                     o[c] = o[c] + splat(c * hidden + h) * unit
             x = o[3]
-            optical = (jnp.maximum(x, 0.0) + jnp.log1p(jnp.exp(-jnp.abs(x)))) * scale
+            optical = (jnp.maximum(x, 0.0) + jnp.log(1.0 + jnp.exp(-jnp.abs(x)))) * scale
             through = optical
             for step in (1, 2, 4):
                 through = through + jnp.where(sub >= step, pltpu.roll(through, step, 0), 0.0)
@@ -266,16 +256,73 @@
             front = after[layers - 1 :]
             weight = before - after
             for c in range(3):
-                color[c] = color[c] + weight / (1.0 + jnp.exp(-o[c]))
-        for c in range(3):
-            line = jnp.sum(color[c], axis=0, keepdims=True)
-            out[c, pl.ds(y, 1), :] = line[:, :LANES]
-            out[c, pl.ds(y + 1, 1), :] = line[:, LANES:]
-        out[3, pl.ds(y, 1), :] = front[:, :LANES]
-        out[3, pl.ds(y + 1, 1), :] = front[:, LANES:]
+                color[c] = color[c] + weight * jnp.tanh(o[c])
+        lines = [0.5 * (1.0 - front + jnp.sum(color[c], axis=0, keepdims=True)) for c in range(3)]
+        for c, line in enumerate(lines + [front]):
+            out[c, target(y), :] = line[:, :LANES]
+            out[c, target(y + 1), :] = line[:, LANES:]
+
+
+def most_kernel(mine, swap, straight, diagonal, halo, w1, w2, out, state, grid, edge, kept, *, layers, rows):
+    side = lax.axis_index("depth") & 1
+    flipped = (lax.axis_index("row") & 1) == 0
+    kk = 2 * (layers + HALO) * FIELDS
+    first, sign = jnp.where(flipped, rows + HALO - 1, -HALO), jnp.where(flipped, -1, 1)
+    own_border = border(side, first, sign, HALO, rows + HALO)
+    halo_border = border(side, jnp.where(flipped, HALO - 1, rows - HALO), sign, 0, HALO)
+    place_halo(halo, grid, edge.at[1], layers, side, flipped, halo_border)
+    taps = tap_matrix()
+    for source, (at, width) in zip((mine, swap, straight, diagonal), places(side, layers)):
+        at = pl.ds(pl.multiple_of(at, 8), width)
+        filtered = dot(source[0 : rows * width, :], taps)
+        for row in range(rows):
+            place = jnp.where(flipped, rows + HALO - 1 - row, row + HALO)
+            grid[place, at, :] = filtered[row * width : (row + 1) * width]
+        edge[0, at, :] = dot(source[rows * width : rows * width + 32, :], own_border)[:width]
+    near = near_cut(side)
+
+    def filter_rows(group, carry):
+        at = pl.ds(pl.multiple_of(group * 16, 16), 16)
+        edges = edge[1, at, :], edge[0, at, :]
+        chain, ring = [None] * 6, []
+        for r in range(rows + HALO):
+            turned = pltpu.roll(edges[r >= HALO], (-3 * r) % LANES, 1)
+            given = next_row(grid[r, at, :] + jnp.where(near, turned, 0.0), chain, ring)
+            if given is not None:
+                keep(kept, r - 2 * HALO, at, *given)
+        for index, value in enumerate(chain + ring):
+            state[index, at, :] = value
         return carry
 
-    lax.fori_loop(0, rows // 2, shade, 0, unroll=8)
+    lax.fori_loop(0, kk // 16, filter_rows, 0, unroll=kk // 16)
+    shade_rows(kept, w1, w2, out, layers, 0, flipped, rows - 1)
+
+
+def rest_kernel(halo, w1, w2, state, done, out, grid, edge, kept, *, layers, rows):
+    out[...] = done[...]
+    side = lax.axis_index("depth") & 1
+    band = lax.axis_index("row")
+    flipped = (band & 1) == 0
+    kk = 2 * (layers + HALO) * FIELDS
+    halo_border = border(side, jnp.where(flipped, rows - 1, 0), jnp.where(flipped, -1, 1), 0, HALO)
+    place_halo(halo, grid, edge, layers, side, flipped, halo_border)
+    near = near_cut(side)
+    outside = jnp.where(flipped, band == 0, band == lax.axis_size("row") - 1)
+    inside = jnp.where(outside, 0.0, 1.0)
+
+    def filter_rows(group, carry):
+        at = pl.ds(pl.multiple_of(group * 16, 16), 16)
+        edges = edge[at, :]
+        values = [state[index, at, :] for index in range(12)]
+        chain, ring = values[:6], values[6:]
+        for r in range(HALO):
+            turned = pltpu.roll(edges, (-3 * r) % LANES, 1)
+            value = grid[r, at, :] + jnp.where(near, turned, 0.0)
+            keep(kept, r, at, *next_row(value, chain, ring, inside if r >= 3 else None))
+        return carry
+
+    lax.fori_loop(0, kk // 16, filter_rows, 0, unroll=kk // 16)
+    shade_rows(kept, w1, w2, out, layers, rows - HALO, flipped, rows - 1)
 
 
 def call(kernel, out_shape, operands, scratch=(), flops=0, name=None):
@@ -335,23 +382,38 @@
         flops=10**8,
         name="weights",
     )
+    mine, w1, w2 = lax.optimization_barrier((mine, w1, w2))
     message = shape((HALO * kk + 4 * 32, LANES), BF16)
     first, second = call(band_kernel, [message, message], (mine, swap, straight, diagonal), name="band")
     within = [(i, i ^ 1) for i in range(bands)]
     across = [(i, i + 1) for i in range(1, bands - 1, 2)] + [(i + 1, i) for i in range(1, bands - 1, 2)]
     second = lax.ppermute(second, "row", across)
     first = lax.ppermute(first, "row", within)
-    current = call(
-        functools.partial(shade_kernel, layers=layers, rows=rows),
-        shape((4, rows, LANES), F32),
-        (mine, swap, straight, diagonal, first, second, w1, w2),
+
+    image = shape((4, rows, LANES), F32)
+    current, state = call(
+        functools.partial(most_kernel, layers=layers, rows=rows),
+        [image, shape((12, kk, LANES), F32)],
+        (mine, swap, straight, diagonal, first, w1, w2),
         [
-            pltpu.VMEM((rows + 2 * HALO, kk, LANES), F32),
-            pltpu.VMEM((3, kk, LANES), F32),
-            pltpu.VMEM((4, rows, kk, LANES), BF16),
+            pltpu.VMEM((rows + HALO, kk, LANES), F32),
+            pltpu.VMEM((2, kk, LANES), F32),
+            pltpu.VMEM((4, rows - HALO, kk, LANES), BF16),
         ],
         flops=10**10,
-        name="shade",
+        name="shade_most",
+    )
+    current = call(
+        functools.partial(rest_kernel, layers=layers, rows=rows),
+        image,
+        (second, w1, w2, state, current),
+        [
+            pltpu.VMEM((HALO, kk, LANES), F32),
+            pltpu.VMEM((kk, LANES), F32),
+            pltpu.VMEM((4, HALO, kk, LANES), BF16),
+        ],
+        flops=10**9,
+        name="shade_rest",
     )
     step = 2
     while step < slabs:

time: 45.8 us -> 42.6 us (0.930)
  the two profiles are of different devices: /device:TPU:28 before, /device:TPU:0 now
where the time goes in v5:
time: 42.6 us; the launch traced here: 42.4 us
  starting transfers between devices  17.3 us (41%)
  waiting for transfers between devices  14.3 us (34%)
  Pallas kernels  8.14 us (19%)
  local copies, waits for them, and re-layouts  1.82 us (4%)
  other arithmetic  0.75 us (2%)
    pallas_call x5, Pallas kernels, call(): pl.pallas_call(kernel, out_shape=out_shape, in_specs=[vmem] * len(operand...  8.14 us
    ppermute x2, starting transfers between devices, local(): lax.ppermute(current, 'depth', [(i, i ^ step) for i in range(slabs)])  7.97 us
    ppermute x1, waiting for transfers between devices, local(): straight = lax.ppermute(own_halo, 'depth', straight_pairs)  6.24 us
    ppermute x2, waiting for transfers between devices, local(): lax.ppermute(current, 'depth', [(i, i ^ step) for i in range(slabs)])  4.9 us
    ppermute x1, starting transfers between devices, local(): other = lax.ppermute(current, 'depth', swap_pairs)  3.58 us
    ppermute x1, starting transfers between devices, local(): swap = lax.ppermute(theirs, 'depth', swap_pairs)  3 us
    ppermute x1, waiting for transfers between devices, local(): other = lax.ppermute(current, 'depth', swap_pairs)  2.37 us
    unnamed x11, local copies, waits for them, and re-layouts  1.82 us
  transfers between devices with their start and end apart: 8, of which 5 were waited for; matrix products, arithmetic and copies ran while one was open for 0% of the time, Pallas kernels for 14%

profile of v5, /device:TPU:0, one launch (start us, length us, event | category | flops | bytes accessed | tf_op | source)
XLA Modules:
  0.0 42.4 jit_solution(1862588396868686645)
XLA Ops:
  0.0 1.0 %copy-done = bf16[4,8,32,256]{3,2,1,0:T(8,128)(2,1)S(1)} copy-done((bf16[4,8,32,256]{3,2,1,0:T(8,128)(2,1)S(1)}, bf16[4,8,32,256]{3,2,1,0:T(8,128)(2,1)}, u32[]{:S(2)}) %copy-start) | copy-done | bytes 524312
  1.0 0.8 %pack.1 = (bf16[1056,128]{1,0:T(8,128)(2,1)S(1)}, bf16[1056,128]{1,0:T(8,128)(2,1)S(1)}, bf16[800,128]{1,0:T(8,128)(2,1)S(1)}, bf16[800,128]{1,0:T(8,128)(2,1)S(1)}) custom-call(bf16[4,8,32,256]{3,2,1,0:T(8,128)(2,1)S(1)} %copy-done), custom_call_target="tpu_custom_call" | custom-call | bytes 1048576 | tf_op jit(solution)/shard_map/pack/pallas_call | solution.py:330
  1.9 3.0 %collective-permute-start = (bf16[1056,128]{1,0:T(8,128)(2,1)S(1)}, bf16[1056,128]{1,0:T(8,128)(2,1)S(1)}, u32[]{:S(2)}, u32[]{:S(2)}) collective-permute-start(bf16[1056,128]{1,0:T(8,128)(2,1)S(1)} %get-tuple-element.22), channel_id=1, source_target_pairs={{0,4},{4,0},{8,12},{12,8},{16,20},{20,16},{24,28},{28,24},{1,5},{5... | collective-permute-start | bytes 811016 | tf_op jit(solution)/shard_map/ppermute | solution.py:373
  4.9 1.3 %collective-permute-start.1 = (bf16[800,128]{1,0:T(8,128)(2,1)S(1)}, bf16[800,128]{1,0:T(8,128)(2,1)S(1)}, u32[]{:S(2)}, u32[]{:S(2)}) collective-permute-start(bf16[800,128]{1,0:T(8,128)(2,1)S(1)} %get-tuple-element.23), channel_id=1, source_target_pairs={{4,12},{12,20},{20,28},{8,0},{16,8},{24,16},{5,13},{13,21},{21,29}... | collective-permute-start | bytes 614408 | tf_op jit(solution)/shard_map/ppermute | solution.py:375
  6.2 0.7 %collective-permute-start.2 = (bf16[800,128]{1,0:T(8,128)(2,1)S(1)}, bf16[800,128]{1,0:T(8,128)(2,1)S(1)}, u32[]{:S(2)}, u32[]{:S(2)}) collective-permute-start(bf16[800,128]{1,0:T(8,128)(2,1)S(1)} %get-tuple-element.24), channel_id=1, source_target_pairs={{4,8},{12,16},{20,24},{8,4},{16,12},{24,20},{5,9},{13,17},{21,25},... | collective-permute-start | bytes 614408 | tf_op jit(solution)/shard_map/ppermute | solution.py:374
  6.9 0.1 copy.6.w_in
  7.0 0.7 %copy-done.1 = f32[4,32]{1,0:T(4,128)S(1)} copy-done((f32[4,32]{1,0:T(4,128)S(1)}, f32[4,32]{1,0:T(4,128)}, u32[]{:S(2)}) %copy-start.1) | copy-done | bytes 536
  7.6 0.5 %weights.1 = (bf16[2,256,512]{2,1,0:T(8,128)(2,1)S(1)}, f32[136,128]{1,0:T(8,128)S(1)}) custom-call(f32[32,12]{1,0:T(8,128)S(1)} %copy.6.w_in, f32[1,32]{1,0:T(1,128)S(1)} %bitcast.6, f32[4,32]{1,0:T(4,128)S(1)} %copy-done.1, f32[1,4]{1,0:T(1,128)S(1)} %bitcast.7), custom_call_target="tpu_custom_call" | custom-call | flops 100000000 | bytes 1048576 | tf_op jit(solution)/shard_map/weights/pallas_call | solution.py:330
  8.2 6.2 %collective-permute-done.1.straight = bf16[800,128]{1,0:T(8,128)(2,1)S(1)} collective-permute-done((bf16[800,128]{1,0:T(8,128)(2,1)S(1)}, bf16[800,128]{1,0:T(8,128)(2,1)S(1)}, u32[]{:S(2)}, u32[]{:S(2)}) %collective-permute-start.1) | collective-permute-done | bytes 204832 | tf_op jit(solution)/shard_map/ppermute | solution.py:375
  14.4 0.0 collective-permute-done.2.diagonal
  14.4 0.0 collective-permute-done.swap
  14.5 0.1 collective-permute-start.4
  14.6 0.7 %collective-permute-start.3 = (bf16[800,128]{1,0:T(8,128)(2,1)S(1)}, bf16[800,128]{1,0:T(8,128)(2,1)S(1)}, u32[]{:S(2)}, u32[]{:S(2)}) collective-permute-start(bf16[800,128]{1,0:T(8,128)(2,1)S(1)} %get-tuple-element.25), channel_id=1, source_target_pairs={{1,2},{2,1},{5,6},{6,5},{9,10},{10,9},{13,14},{14,13},{17,18},{18,... | collective-permute-start | bytes 614408 | tf_op jit(solution)/shard_map/ppermute | solution.py:390
  15.3 0.8 %collective-permute-done.4.halo = bf16[800,128]{1,0:T(8,128)(2,1)S(1)} collective-permute-done((bf16[800,128]{1,0:T(8,128)(2,1)S(1)}, bf16[800,128]{1,0:T(8,128)(2,1)S(1)}, u32[]{:S(2)}, u32[]{:S(2)}) %collective-permute-start.4) | collective-permute-done | bytes 204832 | tf_op jit(solution)/shard_map/ppermute | solution.py:391
  16.0 5.3 %shade_most.1 = (f32[4,32,128]{2,1,0:T(8,128)S(1)}, f32[12,112,128]{2,1,0:T(8,128)S(1)}) custom-call(bf16[1056,128]{1,0:T(8,128)(2,1)S(1)} %get-tuple-element.21.mine, bf16[1056,128]{1,0:T(8,128)(2,1)S(1)} %collective-permute-done.swap, bf16[800,128]{1,0:T(8,128)(2,1)S(1)} %collective-permute-done.1.straight, ...), custom_call_target="tpu_custom_call" | custom-call | flops 10000000000 | bytes 1048576 | tf_op jit(solution)/shard_map/shade_most/pallas_call | solution.py:330
  21.3 0.0 collective-permute-done.3.halo
  21.3 1.5 %shade_rest.1 = f32[4,32,128]{2,1,0:T(8,128)S(1)} custom-call(bf16[800,128]{1,0:T(8,128)(2,1)S(1)} %collective-permute-done.3.halo, bf16[2,256,512]{2,1,0:T(8,128)(2,1)S(1)} %get-tuple-element.26.w1, f32[136,128]{1,0:T(8,128)S(1)} %get-tuple-element.27.w2, f32[12,112,128]{2,1,0:T(8,128)S(1)} %get-tuple-element.29.state, f32[4,32,128]{2,1,0:T(8,128)S(1)} %get-tuple-element.30.done), custom_call_target="tpu_custom_call" | custom-call | flops 1000000000 | bytes 1048576 | tf_op jit(solution)/shard_map/shade_rest/pallas_call | solution.py:330
  22.8 4.9 %collective-permute-start.5 = (f32[4,32,128]{2,1,0:T(8,128)S(1)}, f32[4,32,128]{2,1,0:T(8,128)S(1)}, u32[]{:S(2)}, u32[]{:S(2)}) collective-permute-start(f32[4,32,128]{2,1,0:T(8,128)S(1)} %shade_rest.1), channel_id=1, source_target_pairs={{0,8},{4,12},{8,0},{12,4},{16,24},{20,28},{24,16},{28,20},{1,9},{5... | collective-permute-start | bytes 196616 | tf_op jit(solution)/shard_map/ppermute | solution.py:420
  27.6 2.2 %collective-permute-done.5 = f32[4,32,128]{2,1,0:T(8,128)S(1)} collective-permute-done((f32[4,32,128]{2,1,0:T(8,128)S(1)}, f32[4,32,128]{2,1,0:T(8,128)S(1)}, u32[]{:S(2)}, u32[]{:S(2)}) %collective-permute-start.5) | collective-permute-done | bytes 65568 | tf_op jit(solution)/shard_map/ppermute | solution.py:420
  29.9 3.1 %collective-permute-start.6 = (f32[4,32,128]{2,1,0:T(8,128)S(1)}, f32[4,32,128]{2,1,0:T(8,128)S(1)}, u32[]{:S(2)}, u32[]{:S(2)}) collective-permute-start(f32[4,32,128]{2,1,0:T(8,128)S(1)} %pad_maximum_fusion.1), channel_id=1, source_target_pairs={{0,16},{4,20},{8,24},{12,28},{16,0},{20,4},{24,8},{28,12},{1,17},{... | collective-permute-start | bytes 196616 | tf_op jit(solution)/shard_map/ppermute | solution.py:420
  33.0 2.7 %collective-permute-done.6 = f32[4,32,128]{2,1,0:T(8,128)S(1)} collective-permute-done((f32[4,32,128]{2,1,0:T(8,128)S(1)}, f32[4,32,128]{2,1,0:T(8,128)S(1)}, u32[]{:S(2)}, u32[]{:S(2)}) %collective-permute-start.6) | collective-permute-done | bytes 65568 | tf_op jit(solution)/shard_map/ppermute | solution.py:420
  35.8 3.6 %collective-permute-start.7 = (f32[4,32,128]{2,1,0:T(8,128)S(1)}, f32[4,32,128]{2,1,0:T(8,128)S(1)}, u32[]{:S(2)}, u32[]{:S(2)}) collective-permute-start(f32[4,32,128]{2,1,0:T(8,128)S(1)} %pad_maximum_fusion.2), channel_id=1, source_target_pairs={{0,4},{4,0},{8,12},{12,8},{16,20},{20,16},{24,28},{28,24},{1,5},{5... | collective-permute-start | bytes 196616 | tf_op jit(solution)/shard_map/ppermute | solution.py:425
  39.3 2.4 %collective-permute-done.7 = f32[4,32,128]{2,1,0:T(8,128)S(1)} collective-permute-done((f32[4,32,128]{2,1,0:T(8,128)S(1)}, f32[4,32,128]{2,1,0:T(8,128)S(1)}, u32[]{:S(2)}, u32[]{:S(2)}) %collective-permute-start.7) | collective-permute-done | bytes 65568 | tf_op jit(solution)/shard_map/ppermute | solution.py:425
  41.7 0.7 %pad_maximum_fusion = f32[4,32,256]{2,1,0:T(8,128)} fusion(f32[4,32,128]{2,1,0:T(8,128)S(1)} %get-tuple-element.32, f32[4,32,128]{2,1,0:T(8,128)S(1)} %get-tuple-element.31), kind=kLoop, calls=%fused_computation | loop fusion | flops 32768 | bytes 262144 | tf_op jit(solution)/shard_map/concatenate | solution.py:428
  (18 shorter events, 0.1 us)
Async XLA Ops:
  0.0 1.0 %copy-start = (bf16[4,8,32,256]{3,2,1,0:T(8,128)(2,1)S(1)}, bf16[4,8,32,256]{3,2,1,0:T(8,128)(2,1)}, u32[]{:S(2)}) copy-start(bf16[4,8,32,256]{3,2,1,0:T(8,128)(2,1)} %fields.1) | copy-start | bytes 1572868
  1.0 5.8 %copy-start.4 = (f32[32,12]{0,1:T(8,128)S(1)}, f32[32,12]{0,1:T(8,128)}, u32[]{:S(2)}) copy-start(f32[32,12]{0,1:T(8,128)} %param.6) | copy-start | bytes 4612
  1.9 12.6 %collective-permute-start = (bf16[1056,128]{1,0:T(8,128)(2,1)S(1)}, bf16[1056,128]{1,0:T(8,128)(2,1)S(1)}, u32[]{:S(2)}, u32[]{:S(2)}) collective-permute-start(bf16[1056,128]{1,0:T(8,128)(2,1)S(1)} %get-tuple-element.22), channel_id=1, source_target_pairs={{0,4},{4,0},{8,12},{12,8},{16,20},{20,16},{24,28},{28,24},{1,5},{5... | collective-permute-start | bytes 811016 | tf_op jit(solution)/shard_map/ppermute | solution.py:373
  4.9 9.5 %collective-permute-start.1 = (bf16[800,128]{1,0:T(8,128)(2,1)S(1)}, bf16[800,128]{1,0:T(8,128)(2,1)S(1)}, u32[]{:S(2)}, u32[]{:S(2)}) collective-permute-start(bf16[800,128]{1,0:T(8,128)(2,1)S(1)} %get-tuple-element.23), channel_id=1, source_target_pairs={{4,12},{12,20},{20,28},{8,0},{16,8},{24,16},{5,13},{13,21},{21,29}... | collective-permute-start | bytes 614408 | tf_op jit(solution)/shard_map/ppermute | solution.py:375
  6.2 8.3 %collective-permute-start.2 = (bf16[800,128]{1,0:T(8,128)(2,1)S(1)}, bf16[800,128]{1,0:T(8,128)(2,1)S(1)}, u32[]{:S(2)}, u32[]{:S(2)}) collective-permute-start(bf16[800,128]{1,0:T(8,128)(2,1)S(1)} %get-tuple-element.24), channel_id=1, source_target_pairs={{4,8},{12,16},{20,24},{8,4},{16,12},{24,20},{5,9},{13,17},{21,25},... | collective-permute-start | bytes 614408 | tf_op jit(solution)/shard_map/ppermute | solution.py:374
  7.0 0.7 %copy-start.1 = (f32[4,32]{1,0:T(4,128)S(1)}, f32[4,32]{1,0:T(4,128)}, u32[]{:S(2)}) copy-start(f32[4,32]{1,0:T(4,128)} %w_out.1) | copy-start | bytes 1540
  7.0 0.7 %copy-start.2 = (f32[32]{0:T(128)S(1)}, f32[32]{0:T(128)}, u32[]{:S(2)}) copy-start(f32[32]{0:T(128)} %param.7) | copy-start | bytes 388
  7.0 0.7 %copy-start.3 = (f32[4]{0:T(128)S(1)}, f32[4]{0:T(128)}, u32[]{:S(2)}) copy-start(f32[4]{0:T(128)} %param.9) | copy-start | bytes 52
  14.5 1.5 %collective-permute-start.4 = (bf16[800,128]{1,0:T(8,128)(2,1)S(1)}, bf16[800,128]{1,0:T(8,128)(2,1)S(1)}, u32[]{:S(2)}, u32[]{:S(2)}) collective-permute-start(bf16[800,128]{1,0:T(8,128)(2,1)S(1)} %get-tuple-element.28), channel_id=1, source_target_pairs={{0,1},{1,0},{2,3},{3,2},{4,5},{5,4},{6,7},{7,6},{8,9},{9,8},{10,11... | collective-permute-start | bytes 614408 | tf_op jit(solution)/shard_map/ppermute | solution.py:391
  14.6 6.7 %collective-permute-start.3 = (bf16[800,128]{1,0:T(8,128)(2,1)S(1)}, bf16[800,128]{1,0:T(8,128)(2,1)S(1)}, u32[]{:S(2)}, u32[]{:S(2)}) collective-permute-start(bf16[800,128]{1,0:T(8,128)(2,1)S(1)} %get-tuple-element.25), channel_id=1, source_target_pairs={{1,2},{2,1},{5,6},{6,5},{9,10},{10,9},{13,14},{14,13},{17,18},{18,... | collective-permute-start | bytes 614408 | tf_op jit(solution)/shard_map/ppermute | solution.py:390
  22.8 7.1 %collective-permute-start.5 = (f32[4,32,128]{2,1,0:T(8,128)S(1)}, f32[4,32,128]{2,1,0:T(8,128)S(1)}, u32[]{:S(2)}, u32[]{:S(2)}) collective-permute-start(f32[4,32,128]{2,1,0:T(8,128)S(1)} %shade_rest.1), channel_id=1, source_target_pairs={{0,8},{4,12},{8,0},{12,4},{16,24},{20,28},{24,16},{28,20},{1,9},{5... | collective-permute-start | bytes 196616 | tf_op jit(solution)/shard_map/ppermute | solution.py:420
  29.9 5.8 %collective-permute-start.6 = (f32[4,32,128]{2,1,0:T(8,128)S(1)}, f32[4,32,128]{2,1,0:T(8,128)S(1)}, u32[]{:S(2)}, u32[]{:S(2)}) collective-permute-start(f32[4,32,128]{2,1,0:T(8,128)S(1)} %pad_maximum_fusion.1), channel_id=1, source_target_pairs={{0,16},{4,20},{8,24},{12,28},{16,0},{20,4},{24,8},{28,12},{1,17},{... | collective-permute-start | bytes 196616 | tf_op jit(solution)/shard_map/ppermute | solution.py:420
  35.8 6.0 %collective-permute-start.7 = (f32[4,32,128]{2,1,0:T(8,128)S(1)}, f32[4,32,128]{2,1,0:T(8,128)S(1)}, u32[]{:S(2)}, u32[]{:S(2)}) collective-permute-start(f32[4,32,128]{2,1,0:T(8,128)S(1)} %pad_maximum_fusion.2), channel_id=1, source_target_pairs={{0,4},{4,0},{8,12},{12,8},{16,20},{20,16},{24,28},{28,24},{1,5},{5... | collective-permute-start | bytes 196616 | tf_op jit(solution)/shard_map/ppermute | solution.py:425

commit v6 on v5

--- a/solution.py
+++ b/solution.py
@@ -373,6 +373,7 @@
     swap = lax.ppermute(theirs, "depth", swap_pairs)
     diagonal = lax.ppermute(other_halo, "depth", diagonal_pairs)
     straight = lax.ppermute(own_halo, "depth", straight_pairs)
+    swap, diagonal, straight = lax.optimization_barrier((swap, diagonal, straight))
 
     width = -(-(6 * (kw + 2 * kh) + 2) // 256) * 256
     w1, w2 = call(
@@ -415,17 +416,21 @@
         flops=10**9,
         name="shade_rest",
     )
+    def exchanged(distance):
+        return lax.ppermute(current, "depth", [(i, i ^ distance) for i in range(slabs)])
+
+    def composed(own, received, step):
+        behind = (me & step) != 0
+        return combine(jnp.where(behind, received, own), jnp.where(behind, own, received))
+
     step = 2
-    while step < slabs:
-        received = lax.ppermute(current, "depth", [(i, i ^ step) for i in range(slabs)])
-        behind = (me & step) != 0
-        current = combine(jnp.where(behind, received, current), jnp.where(behind, current, received))
+    while 2 * step < slabs:
+        current = composed(current, exchanged(step), step)
         step *= 2
-    current = jnp.concatenate([current[0:3], 1.0 - current[3:4]], 0)
-    other = lax.ppermute(current, "depth", swap_pairs)
-    first_half = jnp.where(side == 0, current, other)
-    second_half = jnp.where(side == 0, other, current)
-    return jnp.concatenate([first_half, second_half], 2)
+    across_x, across_z, across_both = exchanged(1), exchanged(step), exchanged(1 ^ step)
+    own, other = composed(current, across_z, step), composed(across_x, across_both, step)
+    whole = jnp.concatenate([jnp.where(side == 0, own, other), jnp.where(side == 0, other, own)], 2)
+    return jnp.concatenate([whole[0:3], 1.0 - whole[3:4]], 0)
 
 
 def solution(mesh):

time: 42.6 us -> 42.3 us (level)
  starting transfers between devices: 17.3 us -> 11.9 us
  waiting for transfers between devices: 14.3 us -> 19.2 us
    ppermute x3 -> x4, starting transfers between devices: 11.6 us -> 6.22 us  [exchanged(): lax.ppermute(current, 'depth', [(i, i ^ distance) for i in range(slabs)])]
    ppermute x1, waiting for transfers between devices: 6.24 us -> 9.38 us  [local(): straight = lax.ppermute(own_halo, 'depth', straight_pairs)]
    ppermute x3 -> x4, waiting for transfers between devices: 7.27 us -> 9.06 us  [exchanged(): lax.ppermute(current, 'depth', [(i, i ^ distance) for i in range(slabs)])]
  transfers between devices with their start and end apart: 8 -> 9, of which waited for: 5 -> 6; matrix products, arithmetic and copies ran while one was open for 0% -> 0% of each run, Pallas kernels for 14% -> 14%
where the time goes in v6:
time: 42.3 us; the launch traced here: 42.1 us
  waiting for transfers between devices  19.2 us (45%)
  starting transfers between devices  11.9 us (28%)
  Pallas kernels  8.15 us (19%)
  local copies, waits for them, and re-layouts  1.82 us (4%)
  other arithmetic  0.79 us (2%)
    ppermute x1, waiting for transfers between devices, local(): straight = lax.ppermute(own_halo, 'depth', straight_pairs)  9.38 us
    ppermute x4, waiting for transfers between devices, exchanged(): lax.ppermute(current, 'depth', [(i, i ^ distance) for i in range(slabs)])  9.06 us
    pallas_call x5, Pallas kernels, call(): pl.pallas_call(kernel, out_shape=out_shape, in_specs=[vmem] * len(operand...  8.15 us
    ppermute x4, starting transfers between devices, exchanged(): lax.ppermute(current, 'depth', [(i, i ^ distance) for i in range(slabs)])  6.22 us
    ppermute x1, starting transfers between devices, local(): swap = lax.ppermute(theirs, 'depth', swap_pairs)  3 us
    unnamed x11, local copies, waits for them, and re-layouts  1.82 us
    ppermute x1, starting transfers between devices, local(): straight = lax.ppermute(own_halo, 'depth', straight_pairs)  1.29 us
  transfers between devices with their start and end apart: 9, of which 6 were waited for; matrix products, arithmetic and copies ran while one was open for 0% of the time, Pallas kernels for 14%

profile of v6, /device:TPU:0, one launch (start us, length us, event | category | flops | bytes accessed | tf_op | source)
XLA Modules:
  0.0 42.1 jit_solution(2166242711764113390)
XLA Ops:
  0.0 1.0 %copy-done = bf16[4,8,32,256]{3,2,1,0:T(8,128)(2,1)S(1)} copy-done((bf16[4,8,32,256]{3,2,1,0:T(8,128)(2,1)S(1)}, bf16[4,8,32,256]{3,2,1,0:T(8,128)(2,1)}, u32[]{:S(2)}) %copy-start) | copy-done | bytes 524312
  1.0 0.8 %pack.1 = (bf16[1056,128]{1,0:T(8,128)(2,1)S(1)}, bf16[1056,128]{1,0:T(8,128)(2,1)S(1)}, bf16[800,128]{1,0:T(8,128)(2,1)S(1)}, bf16[800,128]{1,0:T(8,128)(2,1)S(1)}) custom-call(bf16[4,8,32,256]{3,2,1,0:T(8,128)(2,1)S(1)} %copy-done), custom_call_target="tpu_custom_call" | custom-call | bytes 1048576 | tf_op jit(solution)/shard_map/pack/pallas_call | solution.py:330
  1.9 3.0 %collective-permute-start = (bf16[1056,128]{1,0:T(8,128)(2,1)S(1)}, bf16[1056,128]{1,0:T(8,128)(2,1)S(1)}, u32[]{:S(2)}, u32[]{:S(2)}) collective-permute-start(bf16[1056,128]{1,0:T(8,128)(2,1)S(1)} %get-tuple-element.25), channel_id=1, source_target_pairs={{0,4},{4,0},{8,12},{12,8},{16,20},{20,16},{24,28},{28,24},{1,5},{5... | collective-permute-start | bytes 811016 | tf_op jit(solution)/shard_map/ppermute | solution.py:373
  4.9 0.7 %collective-permute-start.1 = (bf16[800,128]{1,0:T(8,128)(2,1)S(1)}, bf16[800,128]{1,0:T(8,128)(2,1)S(1)}, u32[]{:S(2)}, u32[]{:S(2)}) collective-permute-start(bf16[800,128]{1,0:T(8,128)(2,1)S(1)} %get-tuple-element.26), channel_id=1, source_target_pairs={{4,8},{12,16},{20,24},{8,4},{16,12},{24,20},{5,9},{13,17},{21,25},... | collective-permute-start | bytes 614408 | tf_op jit(solution)/shard_map/ppermute | solution.py:374
  5.6 1.3 %collective-permute-start.2 = (bf16[800,128]{1,0:T(8,128)(2,1)S(1)}, bf16[800,128]{1,0:T(8,128)(2,1)S(1)}, u32[]{:S(2)}, u32[]{:S(2)}) collective-permute-start(bf16[800,128]{1,0:T(8,128)(2,1)S(1)} %get-tuple-element.27), channel_id=1, source_target_pairs={{4,12},{12,20},{20,28},{8,0},{16,8},{24,16},{5,13},{13,21},{21,29}... | collective-permute-start | bytes 614408 | tf_op jit(solution)/shard_map/ppermute | solution.py:375
  6.9 0.1 copy.6.w_in
  7.0 0.7 %copy-done.1 = f32[4,32]{1,0:T(4,128)S(1)} copy-done((f32[4,32]{1,0:T(4,128)S(1)}, f32[4,32]{1,0:T(4,128)}, u32[]{:S(2)}) %copy-start.1) | copy-done | bytes 536
  7.6 0.5 %weights.1 = (bf16[2,256,512]{2,1,0:T(8,128)(2,1)S(1)}, f32[136,128]{1,0:T(8,128)S(1)}) custom-call(f32[32,12]{1,0:T(8,128)S(1)} %copy.6.w_in, f32[1,32]{1,0:T(1,128)S(1)} %bitcast.8, f32[4,32]{1,0:T(4,128)S(1)} %copy-done.1, f32[1,4]{1,0:T(1,128)S(1)} %bitcast.9), custom_call_target="tpu_custom_call" | custom-call | flops 100000000 | bytes 1048576 | tf_op jit(solution)/shard_map/weights/pallas_call | solution.py:330
  8.2 0.0 collective-permute-done.1.diagonal
  8.2 9.4 %collective-permute-done.2.straight = bf16[800,128]{1,0:T(8,128)(2,1)S(1)} collective-permute-done((bf16[800,128]{1,0:T(8,128)(2,1)S(1)}, bf16[800,128]{1,0:T(8,128)(2,1)S(1)}, u32[]{:S(2)}, u32[]{:S(2)}) %collective-permute-start.2) | collective-permute-done | bytes 204832 | tf_op jit(solution)/shard_map/ppermute | solution.py:375
  17.6 0.1 collective-permute-start.4
  17.7 0.7 %collective-permute-start.3 = (bf16[800,128]{1,0:T(8,128)(2,1)S(1)}, bf16[800,128]{1,0:T(8,128)(2,1)S(1)}, u32[]{:S(2)}, u32[]{:S(2)}) collective-permute-start(bf16[800,128]{1,0:T(8,128)(2,1)S(1)} %get-tuple-element.31), channel_id=1, source_target_pairs={{1,2},{2,1},{5,6},{6,5},{9,10},{10,9},{13,14},{14,13},{17,18},{18,... | collective-permute-start | bytes 614408 | tf_op jit(solution)/shard_map/ppermute | solution.py:391
  18.4 0.8 %collective-permute-done.4.halo = bf16[800,128]{1,0:T(8,128)(2,1)S(1)} collective-permute-done((bf16[800,128]{1,0:T(8,128)(2,1)S(1)}, bf16[800,128]{1,0:T(8,128)(2,1)S(1)}, u32[]{:S(2)}, u32[]{:S(2)}) %collective-permute-start.4) | collective-permute-done | bytes 204832 | tf_op jit(solution)/shard_map/ppermute | solution.py:392
  19.2 5.3 %shade_most.1 = (f32[4,32,128]{2,1,0:T(8,128)S(1)}, f32[12,112,128]{2,1,0:T(8,128)S(1)}) custom-call(bf16[1056,128]{1,0:T(8,128)(2,1)S(1)} %get-tuple-element.24.mine, bf16[1056,128]{1,0:T(8,128)(2,1)S(1)} %collective-permute-done.swap, bf16[800,128]{1,0:T(8,128)(2,1)S(1)} %collective-permute-done.2.straight, ...), custom_call_target="tpu_custom_call" | custom-call | flops 10000000000 | bytes 1048576 | tf_op jit(solution)/shard_map/shade_most/pallas_call | solution.py:330
  24.4 1.5 %shade_rest.1 = f32[4,32,128]{2,1,0:T(8,128)S(1)} custom-call(bf16[800,128]{1,0:T(8,128)(2,1)S(1)} %collective-permute-done.3.halo, bf16[2,256,512]{2,1,0:T(8,128)(2,1)S(1)} %get-tuple-element.32.w1, f32[136,128]{1,0:T(8,128)S(1)} %get-tuple-element.33.w2, f32[12,112,128]{2,1,0:T(8,128)S(1)} %get-tuple-element.35.state, f32[4,32,128]{2,1,0:T(8,128)S(1)} %get-tuple-element.36.done), custom_call_target="tpu_custom_call" | custom-call | flops 1000000000 | bytes 1048576 | tf_op jit(solution)/shard_map/shade_rest/pallas_call | solution.py:330
  25.9 1.8 %collective-permute-start.5 = (f32[4,32,128]{2,1,0:T(8,128)S(1)}, f32[4,32,128]{2,1,0:T(8,128)S(1)}, u32[]{:S(2)}, u32[]{:S(2)}) collective-permute-start(f32[4,32,128]{2,1,0:T(8,128)S(1)} %shade_rest.1), channel_id=1, source_target_pairs={{0,8},{4,12},{8,0},{12,4},{16,24},{20,28},{24,16},{28,20},{1,9},{5... | collective-permute-start | bytes 196616 | tf_op jit(solution)/shard_map/ppermute | solution.py:420
  27.7 2.6 %collective-permute-done.5 = f32[4,32,128]{2,1,0:T(8,128)S(1)} collective-permute-done((f32[4,32,128]{2,1,0:T(8,128)S(1)}, f32[4,32,128]{2,1,0:T(8,128)S(1)}, u32[]{:S(2)}, u32[]{:S(2)}) %collective-permute-start.5) | collective-permute-done | bytes 65568 | tf_op jit(solution)/shard_map/ppermute | solution.py:420
  30.3 3.7 %collective-permute-start.7 = (f32[4,32,128]{2,1,0:T(8,128)S(1)}, f32[4,32,128]{2,1,0:T(8,128)S(1)}, u32[]{:S(2)}, u32[]{:S(2)}) collective-permute-start(f32[4,32,128]{2,1,0:T(8,128)S(1)} %pad_maximum_fusion.1), channel_id=1, source_target_pairs={{0,20},{4,16},{8,28},{12,24},{16,4},{20,0},{24,12},{28,8},{1,21},{... | collective-permute-start | bytes 196616 | tf_op jit(solution)/shard_map/ppermute | solution.py:420
  34.0 0.5 %collective-permute-start.8 = (f32[4,32,128]{2,1,0:T(8,128)S(1)}, f32[4,32,128]{2,1,0:T(8,128)S(1)}, u32[]{:S(2)}, u32[]{:S(2)}) collective-permute-start(f32[4,32,128]{2,1,0:T(8,128)S(1)} %pad_maximum_fusion.1), channel_id=1, source_target_pairs={{0,4},{4,0},{8,12},{12,8},{16,20},{20,16},{24,28},{28,24},{1,5},{5... | collective-permute-start | bytes 196616 | tf_op jit(solution)/shard_map/ppermute | solution.py:420
  34.6 0.2 collective-permute-start.6
  34.8 3.7 %collective-permute-done.7 = f32[4,32,128]{2,1,0:T(8,128)S(1)} collective-permute-done((f32[4,32,128]{2,1,0:T(8,128)S(1)}, f32[4,32,128]{2,1,0:T(8,128)S(1)}, u32[]{:S(2)}, u32[]{:S(2)}) %collective-permute-start.7) | collective-permute-done | bytes 65568 | tf_op jit(solution)/shard_map/ppermute | solution.py:420
  38.5 0.4 collective-permute-done.8
  38.9 2.4 %collective-permute-done.6 = f32[4,32,128]{2,1,0:T(8,128)S(1)} collective-permute-done((f32[4,32,128]{2,1,0:T(8,128)S(1)}, f32[4,32,128]{2,1,0:T(8,128)S(1)}, u32[]{:S(2)}, u32[]{:S(2)}) %collective-permute-start.6) | collective-permute-done | bytes 65568 | tf_op jit(solution)/shard_map/ppermute | solution.py:420
  41.4 0.7 %pad_maximum_fusion = f32[4,32,256]{2,1,0:T(8,128)} fusion(f32[1,32,256]{2,1,0:T(8,128)S(1)} %fusion.6, f32[3,32,256]{2,1,0:T(8,128)S(1)} %fusion), kind=kLoop, calls=%fused_computation.2 | loop fusion | flops 32768 | bytes 262144 | tf_op jit(solution)/shard_map/concatenate | solution.py:433
  (23 shorter events, 0.2 us)
Async XLA Ops:
  0.0 1.0 %copy-start = (bf16[4,8,32,256]{3,2,1,0:T(8,128)(2,1)S(1)}, bf16[4,8,32,256]{3,2,1,0:T(8,128)(2,1)}, u32[]{:S(2)}) copy-start(bf16[4,8,32,256]{3,2,1,0:T(8,128)(2,1)} %fields.1) | copy-start | bytes 1572868
  1.0 5.8 %copy-start.4 = (f32[32,12]{0,1:T(8,128)S(1)}, f32[32,12]{0,1:T(8,128)}, u32[]{:S(2)}) copy-start(f32[32,12]{0,1:T(8,128)} %param.6) | copy-start | bytes 4612
  1.9 15.7 %collective-permute-start = (bf16[1056,128]{1,0:T(8,128)(2,1)S(1)}, bf16[1056,128]{1,0:T(8,128)(2,1)S(1)}, u32[]{:S(2)}, u32[]{:S(2)}) collective-permute-start(bf16[1056,128]{1,0:T(8,128)(2,1)S(1)} %get-tuple-element.25), channel_id=1, source_target_pairs={{0,4},{4,0},{8,12},{12,8},{16,20},{20,16},{24,28},{28,24},{1,5},{5... | collective-permute-start | bytes 811016 | tf_op jit(solution)/shard_map/ppermute | solution.py:373
  4.9 3.3 %collective-permute-start.1 = (bf16[800,128]{1,0:T(8,128)(2,1)S(1)}, bf16[800,128]{1,0:T(8,128)(2,1)S(1)}, u32[]{:S(2)}, u32[]{:S(2)}) collective-permute-start(bf16[800,128]{1,0:T(8,128)(2,1)S(1)} %get-tuple-element.26), channel_id=1, source_target_pairs={{4,8},{12,16},{20,24},{8,4},{16,12},{24,20},{5,9},{13,17},{21,25},... | collective-permute-start | bytes 614408 | tf_op jit(solution)/shard_map/ppermute | solution.py:374
  5.6 12.0 %collective-permute-start.2 = (bf16[800,128]{1,0:T(8,128)(2,1)S(1)}, bf16[800,128]{1,0:T(8,128)(2,1)S(1)}, u32[]{:S(2)}, u32[]{:S(2)}) collective-permute-start(bf16[800,128]{1,0:T(8,128)(2,1)S(1)} %get-tuple-element.27), channel_id=1, source_target_pairs={{4,12},{12,20},{20,28},{8,0},{16,8},{24,16},{5,13},{13,21},{21,29}... | collective-permute-start | bytes 614408 | tf_op jit(solution)/shard_map/ppermute | solution.py:375
  7.0 0.7 %copy-start.1 = (f32[4,32]{1,0:T(4,128)S(1)}, f32[4,32]{1,0:T(4,128)}, u32[]{:S(2)}) copy-start(f32[4,32]{1,0:T(4,128)} %w_out.1) | copy-start | bytes 1540
  7.0 0.7 %copy-start.2 = (f32[32]{0:T(128)S(1)}, f32[32]{0:T(128)}, u32[]{:S(2)}) copy-start(f32[32]{0:T(128)} %param.7) | copy-start | bytes 388
  7.0 0.7 %copy-start.3 = (f32[4]{0:T(128)S(1)}, f32[4]{0:T(128)}, u32[]{:S(2)}) copy-start(f32[4]{0:T(128)} %param.9) | copy-start | bytes 52
  17.6 1.5 %collective-permute-start.4 = (bf16[800,128]{1,0:T(8,128)(2,1)S(1)}, bf16[800,128]{1,0:T(8,128)(2,1)S(1)}, u32[]{:S(2)}, u32[]{:S(2)}) collective-permute-start(bf16[800,128]{1,0:T(8,128)(2,1)S(1)} %get-tuple-element.34), channel_id=1, source_target_pairs={{0,1},{1,0},{2,3},{3,2},{4,5},{5,4},{6,7},{7,6},{8,9},{9,8},{10,11... | collective-permute-start | bytes 614408 | tf_op jit(solution)/shard_map/ppermute | solution.py:392
  17.7 6.7 %collective-permute-start.3 = (bf16[800,128]{1,0:T(8,128)(2,1)S(1)}, bf16[800,128]{1,0:T(8,128)(2,1)S(1)}, u32[]{:S(2)}, u32[]{:S(2)}) collective-permute-start(bf16[800,128]{1,0:T(8,128)(2,1)S(1)} %get-tuple-element.31), channel_id=1, source_target_pairs={{1,2},{2,1},{5,6},{6,5},{9,10},{10,9},{13,14},{14,13},{17,18},{18,... | collective-permute-start | bytes 614408 | tf_op jit(solution)/shard_map/ppermute | solution.py:391
  25.9 4.3 %collective-permute-start.5 = (f32[4,32,128]{2,1,0:T(8,128)S(1)}, f32[4,32,128]{2,1,0:T(8,128)S(1)}, u32[]{:S(2)}, u32[]{:S(2)}) collective-permute-start(f32[4,32,128]{2,1,0:T(8,128)S(1)} %shade_rest.1), channel_id=1, source_target_pairs={{0,8},{4,12},{8,0},{12,4},{16,24},{20,28},{24,16},{28,20},{1,9},{5... | collective-permute-start | bytes 196616 | tf_op jit(solution)/shard_map/ppermute | solution.py:420
  30.3 8.2 %collective-permute-start.7 = (f32[4,32,128]{2,1,0:T(8,128)S(1)}, f32[4,32,128]{2,1,0:T(8,128)S(1)}, u32[]{:S(2)}, u32[]{:S(2)}) collective-permute-start(f32[4,32,128]{2,1,0:T(8,128)S(1)} %pad_maximum_fusion.1), channel_id=1, source_target_pairs={{0,20},{4,16},{8,28},{12,24},{16,4},{20,0},{24,12},{28,8},{1,21},{... | collective-permute-start | bytes 196616 | tf_op jit(solution)/shard_map/ppermute | solution.py:420
  34.0 4.9 %collective-permute-start.8 = (f32[4,32,128]{2,1,0:T(8,128)S(1)}, f32[4,32,128]{2,1,0:T(8,128)S(1)}, u32[]{:S(2)}, u32[]{:S(2)}) collective-permute-start(f32[4,32,128]{2,1,0:T(8,128)S(1)} %pad_maximum_fusion.1), channel_id=1, source_target_pairs={{0,4},{4,0},{8,12},{12,8},{16,20},{20,16},{24,28},{28,24},{1,5},{5... | collective-permute-start | bytes 196616 | tf_op jit(solution)/shard_map/ppermute | solution.py:420
  34.6 6.7 %collective-permute-start.6 = (f32[4,32,128]{2,1,0:T(8,128)S(1)}, f32[4,32,128]{2,1,0:T(8,128)S(1)}, u32[]{:S(2)}, u32[]{:S(2)}) collective-permute-start(f32[4,32,128]{2,1,0:T(8,128)S(1)} %pad_maximum_fusion.1), channel_id=1, source_target_pairs={{0,16},{4,20},{8,24},{12,28},{16,0},{20,4},{24,8},{28,12},{1,17},{... | collective-permute-start | bytes 196616 | tf_op jit(solution)/shard_map/ppermute | solution.py:420

commit v7 on v6

--- a/solution.py
+++ b/solution.py
@@ -43,18 +43,19 @@
     side = lax.axis_index("depth") & 1
     layers, rows = fields.shape[1], fields.shape[2]
     kw, kh = layers * FIELDS, HALO * FIELDS
+    pitch = left.shape[0] // rows
     for layer in range(layers):
         for field in range(FIELDS):
             plane = fields[field, layer].astype(F32)
-            place = pl.ds(layer * FIELDS + field, rows, stride=kw)
+            place = pl.ds(layer * FIELDS + field, rows, stride=pitch)
             left[place, :] = plane[:, :LANES]
             right[place, :] = plane[:, LANES:]
     lane = iota((kw, LANES), 1)
     shift = pl.multiple_of(side * (kw - kh), 8)
 
     def halves(row, start, count):
-        a = left[pl.ds(row * kw + start, count), :]
-        b = right[pl.ds(row * kw + start, count), :]
+        a = left[pl.ds(row * pitch + start, count), :]
+        b = right[pl.ds(row * pitch + start, count), :]
         return jnp.where(side == 0, a, b), jnp.where(side == 0, b, a)
 
     extra_low = jnp.zeros((kw, LANES), F32)
@@ -62,8 +63,8 @@
     for row in range(0, rows, 2):
         pairs = []
         for r in (row, row + 1):
-            a = left[pl.ds(r * kw, kw), :]
-            b = right[pl.ds(r * kw, kw), :]
+            a = left[pl.ds(r * pitch, kw), :]
+            b = right[pl.ds(r * pitch, kw), :]
             inside = (lane >= 3 * r) & (lane < 3 * r + 3)
             extra_low = jnp.where(inside, pltpu.roll(b, (3 * r) % LANES, 1), extra_low)
             extra_high = jnp.where(inside, pltpu.roll(a, (3 * r + 3) % LANES, 1), extra_high)
@@ -100,9 +101,28 @@
             extra += 32
 
 
-def weights_kernel(w_in, b_in, w_out, b_out, w1, w2, *, layers, hidden, slabs):
+def tap_matrix():
+    return smooth_count(iota((LANES, LANES), 0) - iota((LANES, LANES), 1)).astype(BF16)
+
+
+def border(side, first, sign, low, high):
+    i, j = iota((LANES, LANES), 0), iota((LANES, LANES), 1)
+    spot = (j + jnp.where(side == 0, 3, 0)) & (LANES - 1)
+    ir, ic, jr, jc = i // 3, i % 3, spot // 3, spot % 3
+    apart = jnp.where(side == 0, ic - jc + 3, jc - ic + 3)
+    here = (ir == first + sign * jr) & (jr >= low) & (jr < high)
+    return jnp.where(here, smooth_count(apart), 0.0).astype(BF16)
+
+
+def weights_kernel(w_in, b_in, w_out, b_out, w1, w2, filters, *, layers, rows, hidden, slabs):
     depth = lax.axis_index("depth")
     side = depth & 1
+    flipped = (lax.axis_index("row") & 1) == 0
+    sign = jnp.where(flipped, -1, 1)
+    filters[0] = tap_matrix()
+    filters[1] = border(side, jnp.where(flipped, rows + HALO - 1, -HALO), sign, HALO, rows + HALO)
+    filters[2] = border(side, jnp.where(flipped, HALO - 1, rows - HALO), sign, 0, HALO)
+    filters[3] = border(side, jnp.where(flipped, rows - 1, 0), sign, 0, HALO)
     base = (depth - side) * layers
     total = slabs * layers
     width = w1.shape[2]
@@ -121,7 +141,7 @@
     kappa = iota((hidden, width), 1)
     part1 = jnp.where(kappa == 6 * window, bias, jnp.where(kappa == 6 * window + 1, bias, part1))
     scale = 1.0 / 64.0**3
-    row_sign = jnp.where((lax.axis_index("row") & 1) == 0, -1.0 / 60.0, 1.0 / 60.0)
+    row_sign = jnp.where(flipped, -1.0 / 60.0, 1.0 / 60.0)
     z, place = iota((layers, width), 0), iota((layers, width), 1)
     inner = place % (2 * window)
     slope_kind = inner >= window
@@ -159,22 +179,9 @@
     return ((kh + side * kw, kw), (kh + (1 - side) * kw, kw), ((1 - side) * far, kh), (side * far, kh))
 
 
-def tap_matrix():
-    return smooth_count(iota((LANES, LANES), 0) - iota((LANES, LANES), 1)).astype(BF16)
-
-
-def border(side, first, sign, low, high):
-    i, j = iota((LANES, LANES), 0), iota((LANES, LANES), 1)
-    spot = (j + jnp.where(side == 0, 3, 0)) & (LANES - 1)
-    ir, ic, jr, jc = i // 3, i % 3, spot // 3, spot % 3
-    apart = jnp.where(side == 0, ic - jc + 3, jc - ic + 3)
-    here = (ir == first + sign * jr) & (jr >= low) & (jr < high)
-    return jnp.where(here, smooth_count(apart), 0.0).astype(BF16)
-
-
-def place_halo(halo, grid, edge, layers, side, flipped, edges):
+def place_halo(halo, grid, edge, layers, side, flipped, taps, edges):
     kk = 2 * (layers + HALO) * FIELDS
-    filtered = dot(halo[0 : HALO * kk, :], tap_matrix())
+    filtered = dot(halo[0 : HALO * kk, :], taps)
     added = dot(halo[HALO * kk :, :], edges)
     start = 0
     for index, (at, width) in enumerate(places(side, layers)):
@@ -263,15 +270,12 @@
             out[c, target(y + 1), :] = line[:, LANES:]
 
 
-def most_kernel(mine, swap, straight, diagonal, halo, w1, w2, out, state, grid, edge, kept, *, layers, rows):
+def most_kernel(mine, swap, straight, diagonal, halo, w1, w2, filters, out, state, grid, edge, kept, *, layers, rows):
     side = lax.axis_index("depth") & 1
     flipped = (lax.axis_index("row") & 1) == 0
     kk = 2 * (layers + HALO) * FIELDS
-    first, sign = jnp.where(flipped, rows + HALO - 1, -HALO), jnp.where(flipped, -1, 1)
-    own_border = border(side, first, sign, HALO, rows + HALO)
-    halo_border = border(side, jnp.where(flipped, HALO - 1, rows - HALO), sign, 0, HALO)
-    place_halo(halo, grid, edge.at[1], layers, side, flipped, halo_border)
-    taps = tap_matrix()
+    taps, own_border = filters[0], filters[1]
+    place_halo(halo, grid, edge.at[1], layers, side, flipped, taps, filters[2])
     for source, (at, width) in zip((mine, swap, straight, diagonal), places(side, layers)):
         at = pl.ds(pl.multiple_of(at, 8), width)
         filtered = dot(source[0 : rows * width, :], taps)
@@ -298,14 +302,13 @@
     shade_rows(kept, w1, w2, out, layers, 0, flipped, rows - 1)
 
 
-def rest_kernel(halo, w1, w2, state, done, out, grid, edge, kept, *, layers, rows):
+def rest_kernel(halo, w1, w2, filters, state, done, out, grid, edge, kept, *, layers, rows):
     out[...] = done[...]
     side = lax.axis_index("depth") & 1
     band = lax.axis_index("row")
     flipped = (band & 1) == 0
     kk = 2 * (layers + HALO) * FIELDS
-    halo_border = border(side, jnp.where(flipped, rows - 1, 0), jnp.where(flipped, -1, 1), 0, HALO)
-    place_halo(halo, grid, edge, layers, side, flipped, halo_border)
+    place_halo(halo, grid, edge, layers, side, flipped, filters[0], filters[3])
     near = near_cut(side)
     outside = jnp.where(flipped, band == 0, band == lax.axis_size("row") - 1)
     inside = jnp.where(outside, 0.0, 1.0)
@@ -363,7 +366,7 @@
             shape((rows * kh + kw, LANES), BF16),
         ],
         (fields,),
-        [pltpu.VMEM((rows * kw, LANES), F32)] * 2,
+        [pltpu.VMEM((rows * (kw + 4), LANES), F32)] * 2,
         name="pack",
     )
     swap_pairs = [(i, i ^ 1) for i in range(slabs)]
@@ -376,14 +379,18 @@
     swap, diagonal, straight = lax.optimization_barrier((swap, diagonal, straight))
 
     width = -(-(6 * (kw + 2 * kh) + 2) // 256) * 256
-    w1, w2 = call(
-        functools.partial(weights_kernel, layers=layers, hidden=hidden, slabs=slabs),
-        [shape((2, layers * hidden, width), BF16), shape((4 * hidden + 8, LANES), F32)],
+    w1, w2, filters = call(
+        functools.partial(weights_kernel, layers=layers, rows=rows, hidden=hidden, slabs=slabs),
+        [
+            shape((2, layers * hidden, width), BF16),
+            shape((4 * hidden + 8, LANES), F32),
+            shape((4, LANES, LANES), BF16),
+        ],
         (w_in, b_in[None], w_out, b_out[None]),
         flops=10**8,
         name="weights",
     )
-    mine, w1, w2 = lax.optimization_barrier((mine, w1, w2))
+    mine, w1, w2, filters = lax.optimization_barrier((mine, w1, w2, filters))
     message = shape((HALO * kk + 4 * 32, LANES), BF16)
     first, second = call(band_kernel, [message, message], (mine, swap, straight, diagonal), name="band")
     within = [(i, i ^ 1) for i in range(bands)]
@@ -395,7 +402,7 @@
     current, state = call(
         functools.partial(most_kernel, layers=layers, rows=rows),
         [image, shape((12, kk, LANES), F32)],
-        (mine, swap, straight, diagonal, first, w1, w2),
+        (mine, swap, straight, diagonal, first, w1, w2, filters),
         [
             pltpu.VMEM((rows + HALO, kk, LANES), F32),
             pltpu.VMEM((2, kk, LANES), F32),
@@ -407,7 +414,7 @@
     current = call(
         functools.partial(rest_kernel, layers=layers, rows=rows),
         image,
-        (second, w1, w2, state, current),
+        (second, w1, w2, filters, state, current),
         [
             pltpu.VMEM((HALO, kk, LANES), F32),
             pltpu.VMEM((kk, LANES), F32),

time: 42.3 us -> 41.7 us (0.986)
  Pallas kernels: 8.15 us -> 7.7 us
    pallas_call x5, Pallas kernels: 8.15 us -> 7.7 us  [call(): pl.pallas_call(kernel, out_shape=out_shape, in_specs=[vmem] * len(operand...]
where the time goes in v7:
time: 41.7 us; the launch traced here: 41.5 us
  waiting for transfers between devices  19.1 us (46%)
  starting transfers between devices  11.9 us (29%)
  Pallas kernels  7.7 us (18%)
  local copies, waits for them, and re-layouts  1.82 us (4%)
  other arithmetic  0.79 us (2%)
    ppermute x1, waiting for transfers between devices, local(): straight = lax.ppermute(own_halo, 'depth', straight_pairs)  9.28 us
    ppermute x4, waiting for transfers between devices, exchanged(): lax.ppermute(current, 'depth', [(i, i ^ distance) for i in range(slabs)])  9.06 us
    pallas_call x5, Pallas kernels, call(): pl.pallas_call(kernel, out_shape=out_shape, in_specs=[vmem] * len(operand...  7.7 us
    ppermute x4, starting transfers between devices, exchanged(): lax.ppermute(current, 'depth', [(i, i ^ distance) for i in range(slabs)])  6.22 us
    ppermute x1, starting transfers between devices, local(): swap = lax.ppermute(theirs, 'depth', swap_pairs)  3 us
    unnamed x11, local copies, waits for them, and re-layouts  1.82 us
    ppermute x1, starting transfers between devices, local(): straight = lax.ppermute(own_halo, 'depth', straight_pairs)  1.29 us
  transfers between devices with their start and end apart: 9, of which 6 were waited for; matrix products, arithmetic and copies ran while one was open for 0% of the time, Pallas kernels for 14%

profile of v7, /device:TPU:0, one launch (start us, length us, event | category | flops | bytes accessed | tf_op | source)
XLA Modules:
  0.0 41.5 jit_solution(1887375231761633127)
XLA Ops:
  0.0 1.0 %copy-done = bf16[4,8,32,256]{3,2,1,0:T(8,128)(2,1)S(1)} copy-done((bf16[4,8,32,256]{3,2,1,0:T(8,128)(2,1)S(1)}, bf16[4,8,32,256]{3,2,1,0:T(8,128)(2,1)}, u32[]{:S(2)}) %copy-start) | copy-done | bytes 524312
  1.0 0.3 pack.1
  1.4 3.0 %collective-permute-start = (bf16[1056,128]{1,0:T(8,128)(2,1)S(1)}, bf16[1056,128]{1,0:T(8,128)(2,1)S(1)}, u32[]{:S(2)}, u32[]{:S(2)}) collective-permute-start(bf16[1056,128]{1,0:T(8,128)(2,1)S(1)} %get-tuple-element.28), channel_id=1, source_target_pairs={{0,4},{4,0},{8,12},{12,8},{16,20},{20,16},{24,28},{28,24},{1,5},{5... | collective-permute-start | bytes 811016 | tf_op jit(solution)/shard_map/ppermute | solution.py:376
  4.4 0.7 %collective-permute-start.1 = (bf16[800,128]{1,0:T(8,128)(2,1)S(1)}, bf16[800,128]{1,0:T(8,128)(2,1)S(1)}, u32[]{:S(2)}, u32[]{:S(2)}) collective-permute-start(bf16[800,128]{1,0:T(8,128)(2,1)S(1)} %get-tuple-element.29), channel_id=1, source_target_pairs={{4,8},{12,16},{20,24},{8,4},{16,12},{24,20},{5,9},{13,17},{21,25},... | collective-permute-start | bytes 614408 | tf_op jit(solution)/shard_map/ppermute | solution.py:377
  5.0 1.3 %collective-permute-start.2 = (bf16[800,128]{1,0:T(8,128)(2,1)S(1)}, bf16[800,128]{1,0:T(8,128)(2,1)S(1)}, u32[]{:S(2)}, u32[]{:S(2)}) collective-permute-start(bf16[800,128]{1,0:T(8,128)(2,1)S(1)} %get-tuple-element.30), channel_id=1, source_target_pairs={{4,12},{12,20},{20,28},{8,0},{16,8},{24,16},{5,13},{13,21},{21,29}... | collective-permute-start | bytes 614408 | tf_op jit(solution)/shard_map/ppermute | solution.py:378
  6.4 0.1 copy.6.w_in
  6.4 0.7 %copy-done.1 = f32[4,32]{1,0:T(4,128)S(1)} copy-done((f32[4,32]{1,0:T(4,128)S(1)}, f32[4,32]{1,0:T(4,128)}, u32[]{:S(2)}) %copy-start.1) | copy-done | bytes 536
  7.1 0.6 %weights.1 = (bf16[2,256,512]{2,1,0:T(8,128)(2,1)S(1)}, f32[136,128]{1,0:T(8,128)S(1)}, bf16[4,128,128]{2,1,0:T(8,128)(2,1)S(1)}) custom-call(f32[32,12]{1,0:T(8,128)S(1)} %copy.6.w_in, f32[1,32]{1,0:T(1,128)S(1)} %bitcast.8, f32[4,32]{1,0:T(4,128)S(1)} %copy-done.1, f32[1,4]{1,0:T(1,128)S(1)} %bitcast.9), custom_call_target="tpu_custom_call" | custom-call | flops 100000000 | bytes 1048576 | tf_op jit(solution)/shard_map/weights/pallas_call | solution.py:333
  7.8 0.0 collective-permute-done.1.diagonal
  7.8 9.3 %collective-permute-done.2.straight = bf16[800,128]{1,0:T(8,128)(2,1)S(1)} collective-permute-done((bf16[800,128]{1,0:T(8,128)(2,1)S(1)}, bf16[800,128]{1,0:T(8,128)(2,1)S(1)}, u32[]{:S(2)}, u32[]{:S(2)}) %collective-permute-start.2) | collective-permute-done | bytes 204832 | tf_op jit(solution)/shard_map/ppermute | solution.py:378
  17.1 0.1 collective-permute-start.4
  17.2 0.7 %collective-permute-start.3 = (bf16[800,128]{1,0:T(8,128)(2,1)S(1)}, bf16[800,128]{1,0:T(8,128)(2,1)S(1)}, u32[]{:S(2)}, u32[]{:S(2)}) collective-permute-start(bf16[800,128]{1,0:T(8,128)(2,1)S(1)} %get-tuple-element.34), channel_id=1, source_target_pairs={{1,2},{2,1},{5,6},{6,5},{9,10},{10,9},{13,14},{14,13},{17,18},{18,... | collective-permute-start | bytes 614408 | tf_op jit(solution)/shard_map/ppermute | solution.py:398
  17.9 0.8 %collective-permute-done.4.halo = bf16[800,128]{1,0:T(8,128)(2,1)S(1)} collective-permute-done((bf16[800,128]{1,0:T(8,128)(2,1)S(1)}, bf16[800,128]{1,0:T(8,128)(2,1)S(1)}, u32[]{:S(2)}, u32[]{:S(2)}) %collective-permute-start.4) | collective-permute-done | bytes 204832 | tf_op jit(solution)/shard_map/ppermute | solution.py:399
  18.6 5.3 %shade_most.1 = (f32[4,32,128]{2,1,0:T(8,128)S(1)}, f32[12,112,128]{2,1,0:T(8,128)S(1)}) custom-call(bf16[1056,128]{1,0:T(8,128)(2,1)S(1)} %get-tuple-element.27.mine, bf16[1056,128]{1,0:T(8,128)(2,1)S(1)} %collective-permute-done.swap, bf16[800,128]{1,0:T(8,128)(2,1)S(1)} %collective-permute-done.2.straight, ...), custom_call_target="tpu_custom_call" | custom-call | flops 10000000000 | bytes 1048576 | tf_op jit(solution)/shard_map/shade_most/pallas_call | solution.py:333
  23.9 1.5 %shade_rest.1 = f32[4,32,128]{2,1,0:T(8,128)S(1)} custom-call(bf16[800,128]{1,0:T(8,128)(2,1)S(1)} %collective-permute-done.3.halo, bf16[2,256,512]{2,1,0:T(8,128)(2,1)S(1)} %get-tuple-element.35.w1, f32[136,128]{1,0:T(8,128)S(1)} %get-tuple-element.36.w2, bf16[4,128,128]{2,1,0:T(8,128)(2,1)S(1)} %get-tuple-element.37.filters, ...), custom_call_target="tpu_custom_call" | custom-call | flops 1000000000 | bytes 1048576 | tf_op jit(solution)/shard_map/shade_rest/pallas_call | solution.py:333
  25.4 1.8 %collective-permute-start.5 = (f32[4,32,128]{2,1,0:T(8,128)S(1)}, f32[4,32,128]{2,1,0:T(8,128)S(1)}, u32[]{:S(2)}, u32[]{:S(2)}) collective-permute-start(f32[4,32,128]{2,1,0:T(8,128)S(1)} %shade_rest.1), channel_id=1, source_target_pairs={{0,8},{4,12},{8,0},{12,4},{16,24},{20,28},{24,16},{28,20},{1,9},{5... | collective-permute-start | bytes 196616 | tf_op jit(solution)/shard_map/ppermute | solution.py:427
  27.1 2.6 %collective-permute-done.5 = f32[4,32,128]{2,1,0:T(8,128)S(1)} collective-permute-done((f32[4,32,128]{2,1,0:T(8,128)S(1)}, f32[4,32,128]{2,1,0:T(8,128)S(1)}, u32[]{:S(2)}, u32[]{:S(2)}) %collective-permute-start.5) | collective-permute-done | bytes 65568 | tf_op jit(solution)/shard_map/ppermute | solution.py:427
  29.8 3.7 %collective-permute-start.7 = (f32[4,32,128]{2,1,0:T(8,128)S(1)}, f32[4,32,128]{2,1,0:T(8,128)S(1)}, u32[]{:S(2)}, u32[]{:S(2)}) collective-permute-start(f32[4,32,128]{2,1,0:T(8,128)S(1)} %pad_maximum_fusion.1), channel_id=1, source_target_pairs={{0,20},{4,16},{8,28},{12,24},{16,4},{20,0},{24,12},{28,8},{1,21},{... | collective-permute-start | bytes 196616 | tf_op jit(solution)/shard_map/ppermute | solution.py:427
  33.5 0.5 %collective-permute-start.8 = (f32[4,32,128]{2,1,0:T(8,128)S(1)}, f32[4,32,128]{2,1,0:T(8,128)S(1)}, u32[]{:S(2)}, u32[]{:S(2)}) collective-permute-start(f32[4,32,128]{2,1,0:T(8,128)S(1)} %pad_maximum_fusion.1), channel_id=1, source_target_pairs={{0,4},{4,0},{8,12},{12,8},{16,20},{20,16},{24,28},{28,24},{1,5},{5... | collective-permute-start | bytes 196616 | tf_op jit(solution)/shard_map/ppermute | solution.py:427
  34.0 0.2 collective-permute-start.6
  34.2 3.8 %collective-permute-done.7 = f32[4,32,128]{2,1,0:T(8,128)S(1)} collective-permute-done((f32[4,32,128]{2,1,0:T(8,128)S(1)}, f32[4,32,128]{2,1,0:T(8,128)S(1)}, u32[]{:S(2)}, u32[]{:S(2)}) %collective-permute-start.7) | collective-permute-done | bytes 65568 | tf_op jit(solution)/shard_map/ppermute | solution.py:427
  38.0 0.4 collective-permute-done.8
  38.4 2.4 %collective-permute-done.6 = f32[4,32,128]{2,1,0:T(8,128)S(1)} collective-permute-done((f32[4,32,128]{2,1,0:T(8,128)S(1)}, f32[4,32,128]{2,1,0:T(8,128)S(1)}, u32[]{:S(2)}, u32[]{:S(2)}) %collective-permute-start.6) | collective-permute-done | bytes 65568 | tf_op jit(solution)/shard_map/ppermute | solution.py:427
  40.8 0.7 %pad_maximum_fusion = f32[4,32,256]{2,1,0:T(8,128)} fusion(f32[1,32,256]{2,1,0:T(8,128)S(1)} %fusion.6, f32[3,32,256]{2,1,0:T(8,128)S(1)} %fusion), kind=kLoop, calls=%fused_computation.2 | loop fusion | flops 32768 | bytes 262144 | tf_op jit(solution)/shard_map/concatenate | solution.py:440
  (23 shorter events, 0.2 us)
Async XLA Ops:
  0.0 1.0 %copy-start = (bf16[4,8,32,256]{3,2,1,0:T(8,128)(2,1)S(1)}, bf16[4,8,32,256]{3,2,1,0:T(8,128)(2,1)}, u32[]{:S(2)}) copy-start(bf16[4,8,32,256]{3,2,1,0:T(8,128)(2,1)} %fields.1) | copy-start | bytes 1572868
  1.0 5.3 %copy-start.4 = (f32[32,12]{0,1:T(8,128)S(1)}, f32[32,12]{0,1:T(8,128)}, u32[]{:S(2)}) copy-start(f32[32,12]{0,1:T(8,128)} %param.6) | copy-start | bytes 4612
  1.4 15.7 %collective-permute-start = (bf16[1056,128]{1,0:T(8,128)(2,1)S(1)}, bf16[1056,128]{1,0:T(8,128)(2,1)S(1)}, u32[]{:S(2)}, u32[]{:S(2)}) collective-permute-start(bf16[1056,128]{1,0:T(8,128)(2,1)S(1)} %get-tuple-element.28), channel_id=1, source_target_pairs={{0,4},{4,0},{8,12},{12,8},{16,20},{20,16},{24,28},{28,24},{1,5},{5... | collective-permute-start | bytes 811016 | tf_op jit(solution)/shard_map/ppermute | solution.py:376
  4.4 3.4 %collective-permute-start.1 = (bf16[800,128]{1,0:T(8,128)(2,1)S(1)}, bf16[800,128]{1,0:T(8,128)(2,1)S(1)}, u32[]{:S(2)}, u32[]{:S(2)}) collective-permute-start(bf16[800,128]{1,0:T(8,128)(2,1)S(1)} %get-tuple-element.29), channel_id=1, source_target_pairs={{4,8},{12,16},{20,24},{8,4},{16,12},{24,20},{5,9},{13,17},{21,25},... | collective-permute-start | bytes 614408 | tf_op jit(solution)/shard_map/ppermute | solution.py:377
  5.0 12.0 %collective-permute-start.2 = (bf16[800,128]{1,0:T(8,128)(2,1)S(1)}, bf16[800,128]{1,0:T(8,128)(2,1)S(1)}, u32[]{:S(2)}, u32[]{:S(2)}) collective-permute-start(bf16[800,128]{1,0:T(8,128)(2,1)S(1)} %get-tuple-element.30), channel_id=1, source_target_pairs={{4,12},{12,20},{20,28},{8,0},{16,8},{24,16},{5,13},{13,21},{21,29}... | collective-permute-start | bytes 614408 | tf_op jit(solution)/shard_map/ppermute | solution.py:378
  6.4 0.7 %copy-start.1 = (f32[4,32]{1,0:T(4,128)S(1)}, f32[4,32]{1,0:T(4,128)}, u32[]{:S(2)}) copy-start(f32[4,32]{1,0:T(4,128)} %w_out.1) | copy-start | bytes 1540
  6.4 0.7 %copy-start.2 = (f32[32]{0:T(128)S(1)}, f32[32]{0:T(128)}, u32[]{:S(2)}) copy-start(f32[32]{0:T(128)} %param.7) | copy-start | bytes 388
  6.4 0.7 %copy-start.3 = (f32[4]{0:T(128)S(1)}, f32[4]{0:T(128)}, u32[]{:S(2)}) copy-start(f32[4]{0:T(128)} %param.9) | copy-start | bytes 52
  17.1 1.5 %collective-permute-start.4 = (bf16[800,128]{1,0:T(8,128)(2,1)S(1)}, bf16[800,128]{1,0:T(8,128)(2,1)S(1)}, u32[]{:S(2)}, u32[]{:S(2)}) collective-permute-start(bf16[800,128]{1,0:T(8,128)(2,1)S(1)} %get-tuple-element.38), channel_id=1, source_target_pairs={{0,1},{1,0},{2,3},{3,2},{4,5},{5,4},{6,7},{7,6},{8,9},{9,8},{10,11... | collective-permute-start | bytes 614408 | tf_op jit(solution)/shard_map/ppermute | solution.py:399
  17.2 6.7 %collective-permute-start.3 = (bf16[800,128]{1,0:T(8,128)(2,1)S(1)}, bf16[800,128]{1,0:T(8,128)(2,1)S(1)}, u32[]{:S(2)}, u32[]{:S(2)}) collective-permute-start(bf16[800,128]{1,0:T(8,128)(2,1)S(1)} %get-tuple-element.34), channel_id=1, source_target_pairs={{1,2},{2,1},{5,6},{6,5},{9,10},{10,9},{13,14},{14,13},{17,18},{18,... | collective-permute-start | bytes 614408 | tf_op jit(solution)/shard_map/ppermute | solution.py:398
  25.4 4.3 %collective-permute-start.5 = (f32[4,32,128]{2,1,0:T(8,128)S(1)}, f32[4,32,128]{2,1,0:T(8,128)S(1)}, u32[]{:S(2)}, u32[]{:S(2)}) collective-permute-start(f32[4,32,128]{2,1,0:T(8,128)S(1)} %shade_rest.1), channel_id=1, source_target_pairs={{0,8},{4,12},{8,0},{12,4},{16,24},{20,28},{24,16},{28,20},{1,9},{5... | collective-permute-start | bytes 196616 | tf_op jit(solution)/shard_map/ppermute | solution.py:427
  29.8 8.2 %collective-permute-start.7 = (f32[4,32,128]{2,1,0:T(8,128)S(1)}, f32[4,32,128]{2,1,0:T(8,128)S(1)}, u32[]{:S(2)}, u32[]{:S(2)}) collective-permute-start(f32[4,32,128]{2,1,0:T(8,128)S(1)} %pad_maximum_fusion.1), channel_id=1, source_target_pairs={{0,20},{4,16},{8,28},{12,24},{16,4},{20,0},{24,12},{28,8},{1,21},{... | collective-permute-start | bytes 196616 | tf_op jit(solution)/shard_map/ppermute | solution.py:427
  33.5 4.9 %collective-permute-start.8 = (f32[4,32,128]{2,1,0:T(8,128)S(1)}, f32[4,32,128]{2,1,0:T(8,128)S(1)}, u32[]{:S(2)}, u32[]{:S(2)}) collective-permute-start(f32[4,32,128]{2,1,0:T(8,128)S(1)} %pad_maximum_fusion.1), channel_id=1, source_target_pairs={{0,4},{4,0},{8,12},{12,8},{16,20},{20,16},{24,28},{28,24},{1,5},{5... | collective-permute-start | bytes 196616 | tf_op jit(solution)/shard_map/ppermute | solution.py:427
  34.0 6.7 %collective-permute-start.6 = (f32[4,32,128]{2,1,0:T(8,128)S(1)}, f32[4,32,128]{2,1,0:T(8,128)S(1)}, u32[]{:S(2)}, u32[]{:S(2)}) collective-permute-start(f32[4,32,128]{2,1,0:T(8,128)S(1)} %pad_maximum_fusion.1), channel_id=1, source_target_pairs={{0,16},{4,20},{8,24},{12,28},{16,0},{20,4},{24,8},{28,12},{1,17},{... | collective-permute-start | bytes 196616 | tf_op jit(solution)/shard_map/ppermute | solution.py:427

commit v8 on v7

--- a/solution.py
+++ b/solution.py
@@ -270,28 +270,32 @@
             out[c, target(y + 1), :] = line[:, LANES:]
 
 
-def most_kernel(mine, swap, straight, diagonal, halo, w1, w2, filters, out, state, grid, edge, kept, *, layers, rows):
+def filter_kernel(mine, swap, straight, diagonal, filters, grid, edge, *, layers, rows):
+    side = lax.axis_index("depth") & 1
+    flipped = (lax.axis_index("row") & 1) == 0
+    for source, (at, width) in zip((mine, swap, straight, diagonal), places(side, layers)):
+        at = pl.ds(pl.multiple_of(at, 8), width)
+        filtered = dot(source[0 : rows * width, :], filters[0])
+        for row in range(rows):
+            grid[jnp.where(flipped, rows - 1 - row, row), at, :] = filtered[row * width : (row + 1) * width]
+        edge[at, :] = dot(source[rows * width : rows * width + 32, :], filters[1])[:width]
+
+
+def most_kernel(own_grid, own_edge, halo, w1, w2, filters, out, state, grid, edge, kept, *, layers, rows):
     side = lax.axis_index("depth") & 1
     flipped = (lax.axis_index("row") & 1) == 0
     kk = 2 * (layers + HALO) * FIELDS
-    taps, own_border = filters[0], filters[1]
-    place_halo(halo, grid, edge.at[1], layers, side, flipped, taps, filters[2])
-    for source, (at, width) in zip((mine, swap, straight, diagonal), places(side, layers)):
-        at = pl.ds(pl.multiple_of(at, 8), width)
-        filtered = dot(source[0 : rows * width, :], taps)
-        for row in range(rows):
-            place = jnp.where(flipped, rows + HALO - 1 - row, row + HALO)
-            grid[place, at, :] = filtered[row * width : (row + 1) * width]
-        edge[0, at, :] = dot(source[rows * width : rows * width + 32, :], own_border)[:width]
+    place_halo(halo, grid, edge, layers, side, flipped, filters[0], filters[2])
     near = near_cut(side)
 
     def filter_rows(group, carry):
         at = pl.ds(pl.multiple_of(group * 16, 16), 16)
-        edges = edge[1, at, :], edge[0, at, :]
+        halo_edge, edges = edge[at, :], own_edge[at, :]
         chain, ring = [None] * 6, []
         for r in range(rows + HALO):
-            turned = pltpu.roll(edges[r >= HALO], (-3 * r) % LANES, 1)
-            given = next_row(grid[r, at, :] + jnp.where(near, turned, 0.0), chain, ring)
+            turned = pltpu.roll(halo_edge if r < HALO else edges, (-3 * r) % LANES, 1)
+            value = grid[r, at, :] if r < HALO else own_grid[r - HALO, at, :]
+            given = next_row(value + jnp.where(near, turned, 0.0), chain, ring)
             if given is not None:
                 keep(kept, r - 2 * HALO, at, *given)
         for index, value in enumerate(chain + ring):
@@ -398,14 +402,21 @@
     second = lax.ppermute(second, "row", across)
     first = lax.ppermute(first, "row", within)
 
+    own_grid, own_edge = call(
+        functools.partial(filter_kernel, layers=layers, rows=rows),
+        [shape((rows, kk, LANES), F32), shape((kk, LANES), F32)],
+        (mine, swap, straight, diagonal, filters),
+        flops=10**9,
+        name="filter",
+    )
     image = shape((4, rows, LANES), F32)
     current, state = call(
         functools.partial(most_kernel, layers=layers, rows=rows),
         [image, shape((12, kk, LANES), F32)],
-        (mine, swap, straight, diagonal, first, w1, w2, filters),
+        (own_grid, own_edge, first, w1, w2, filters),
         [
-            pltpu.VMEM((rows + HALO, kk, LANES), F32),
-            pltpu.VMEM((2, kk, LANES), F32),
+            pltpu.VMEM((HALO, kk, LANES), F32),
+            pltpu.VMEM((kk, LANES), F32),
             pltpu.VMEM((4, rows - HALO, kk, LANES), BF16),
         ],
         flops=10**10,

time: 41.7 us -> 41.5 us (level)
  waiting for transfers between devices: 19.1 us -> 16.6 us
  local copies, waits for them, and re-layouts: 1.82 us -> 3.81 us
    unnamed x11 -> x9, local copies, waits for them, and re-layouts: 1.82 us -> 3.81 us
    ppermute x1, waiting for transfers between devices: 9.28 us -> 7.29 us  [local(): straight = lax.ppermute(own_halo, 'depth', straight_pairs)]
    ppermute x1, waiting for transfers between devices: 0.76 us -> 0.31 us  [local(): first = lax.ppermute(first, 'row', within)]
    pallas_call x5 -> x6, Pallas kernels: 7.7 us -> 7.97 us  [call(): pl.pallas_call(kernel, out_shape=out_shape, in_specs=[vmem] * len(operand...]
  transfers between devices with their start and end apart: 9 -> 9, of which waited for: 6 -> 5; matrix products, arithmetic and copies ran while one was open for 0% -> 2% of each run, Pallas kernels for 14% -> 15%
where the time goes in v8:
time: 41.5 us; the launch traced here: 41.3 us
  waiting for transfers between devices  16.6 us (40%)
  starting transfers between devices  11.9 us (29%)
  Pallas kernels  7.97 us (19%)
  local copies, waits for them, and re-layouts  3.81 us (9%)
  other arithmetic  0.79 us (2%)
    ppermute x4, waiting for transfers between devices, exchanged(): lax.ppermute(current, 'depth', [(i, i ^ distance) for i in range(slabs)])  8.97 us
    pallas_call x6, Pallas kernels, call(): pl.pallas_call(kernel, out_shape=out_shape, in_specs=[vmem] * len(operand...  7.97 us
    ppermute x1, waiting for transfers between devices, local(): straight = lax.ppermute(own_halo, 'depth', straight_pairs)  7.29 us
    ppermute x4, starting transfers between devices, exchanged(): lax.ppermute(current, 'depth', [(i, i ^ distance) for i in range(slabs)])  6.23 us
    unnamed x9, local copies, waits for them, and re-layouts  3.81 us
    ppermute x1, starting transfers between devices, local(): swap = lax.ppermute(theirs, 'depth', swap_pairs)  3 us
    ppermute x1, starting transfers between devices, local(): straight = lax.ppermute(own_halo, 'depth', straight_pairs)  1.29 us
  transfers between devices with their start and end apart: 9, of which 5 were waited for; matrix products, arithmetic and copies ran while one was open for 2% of the time, Pallas kernels for 15%

profile of v8, /device:TPU:0, one launch (start us, length us, event | category | flops | bytes accessed | tf_op | source)
XLA Modules:
  0.0 41.3 jit_solution(10043667565309629979)
XLA Ops:
  0.0 1.0 %copy-done = bf16[4,8,32,256]{3,2,1,0:T(8,128)(2,1)S(1)} copy-done((bf16[4,8,32,256]{3,2,1,0:T(8,128)(2,1)S(1)}, bf16[4,8,32,256]{3,2,1,0:T(8,128)(2,1)}, u32[]{:S(2)}) %copy-start) | copy-done | bytes 524312
  1.0 0.3 pack.1
  1.4 3.0 %collective-permute-start = (bf16[1056,128]{1,0:T(8,128)(2,1)S(1)}, bf16[1056,128]{1,0:T(8,128)(2,1)S(1)}, u32[]{:S(2)}, u32[]{:S(2)}) collective-permute-start(bf16[1056,128]{1,0:T(8,128)(2,1)S(1)} %get-tuple-element.30), channel_id=1, source_target_pairs={{0,4},{4,0},{8,12},{12,8},{16,20},{20,16},{24,28},{28,24},{1,5},{5... | collective-permute-start | bytes 811016 | tf_op jit(solution)/shard_map/ppermute | solution.py:380
  4.4 0.7 %collective-permute-start.1 = (bf16[800,128]{1,0:T(8,128)(2,1)S(1)}, bf16[800,128]{1,0:T(8,128)(2,1)S(1)}, u32[]{:S(2)}, u32[]{:S(2)}) collective-permute-start(bf16[800,128]{1,0:T(8,128)(2,1)S(1)} %get-tuple-element.31), channel_id=1, source_target_pairs={{4,8},{12,16},{20,24},{8,4},{16,12},{24,20},{5,9},{13,17},{21,25},... | collective-permute-start | bytes 614408 | tf_op jit(solution)/shard_map/ppermute | solution.py:381
  5.0 1.3 %collective-permute-start.2 = (bf16[800,128]{1,0:T(8,128)(2,1)S(1)}, bf16[800,128]{1,0:T(8,128)(2,1)S(1)}, u32[]{:S(2)}, u32[]{:S(2)}) collective-permute-start(bf16[800,128]{1,0:T(8,128)(2,1)S(1)} %get-tuple-element.32), channel_id=1, source_target_pairs={{4,12},{12,20},{20,28},{8,0},{16,8},{24,16},{5,13},{13,21},{21,29}... | collective-permute-start | bytes 614408 | tf_op jit(solution)/shard_map/ppermute | solution.py:382
  6.3 0.8 %copy.6.w_in = f32[32,12]{1,0:T(8,128)S(1)} copy(f32[32,12]{0,1:T(8,128)} %param.6) | data formatting | bytes 3072 | tf_op args[1]
  7.1 0.7 %copy-done.1 = f32[4,32]{1,0:T(4,128)S(1)} copy-done((f32[4,32]{1,0:T(4,128)S(1)}, f32[4,32]{1,0:T(4,128)}, u32[]{:S(2)}) %copy-start.1) | copy-done | bytes 536
  7.8 0.7 %copy-done.2 = f32[32]{0:T(128)S(1)} copy-done((f32[32]{0:T(128)S(1)}, f32[32]{0:T(128)}, u32[]{:S(2)}) %copy-start.2) | copy-done | bytes 152
  8.5 0.7 %copy-done.3 = f32[4]{0:T(128)S(1)} copy-done((f32[4]{0:T(128)S(1)}, f32[4]{0:T(128)}, u32[]{:S(2)}) %copy-start.3) | copy-done | bytes 40
  9.1 0.6 %weights.1 = (bf16[2,256,512]{2,1,0:T(8,128)(2,1)S(1)}, f32[136,128]{1,0:T(8,128)S(1)}, bf16[4,128,128]{2,1,0:T(8,128)(2,1)S(1)}) custom-call(f32[32,12]{1,0:T(8,128)S(1)} %copy.6.w_in, f32[1,32]{1,0:T(1,128)S(1)} %bitcast.8, f32[4,32]{1,0:T(4,128)S(1)} %copy-done.1, f32[1,4]{1,0:T(1,128)S(1)} %bitcast.9), custom_call_target="tpu_custom_call" | custom-call | flops 100000000 | bytes 1048576 | tf_op jit(solution)/shard_map/weights/pallas_call | solution.py:337
  9.8 7.3 %collective-permute-done.2.straight = bf16[800,128]{1,0:T(8,128)(2,1)S(1)} collective-permute-done((bf16[800,128]{1,0:T(8,128)(2,1)S(1)}, bf16[800,128]{1,0:T(8,128)(2,1)S(1)}, u32[]{:S(2)}, u32[]{:S(2)}) %collective-permute-start.2) | collective-permute-done | bytes 204832 | tf_op jit(solution)/shard_map/ppermute | solution.py:382
  17.2 0.7 %collective-permute-start.3 = (bf16[800,128]{1,0:T(8,128)(2,1)S(1)}, bf16[800,128]{1,0:T(8,128)(2,1)S(1)}, u32[]{:S(2)}, u32[]{:S(2)}) collective-permute-start(bf16[800,128]{1,0:T(8,128)(2,1)S(1)} %get-tuple-element.36), channel_id=1, source_target_pairs={{1,2},{2,1},{5,6},{6,5},{9,10},{10,9},{13,14},{14,13},{17,18},{18,... | collective-permute-start | bytes 614408 | tf_op jit(solution)/shard_map/ppermute | solution.py:402
  17.9 0.4 %filter.1 = (f32[32,112,128]{2,1,0:T(8,128)S(1)}, f32[112,128]{1,0:T(8,128)S(1)}) custom-call(bf16[1056,128]{1,0:T(8,128)(2,1)S(1)} %get-tuple-element.29.mine, bf16[1056,128]{1,0:T(8,128)(2,1)S(1)} %collective-permute-done.swap, bf16[800,128]{1,0:T(8,128)(2,1)S(1)} %collective-permute-done.2.straight, bf16[800,128]{1,0:T(8,128)(2,1)S(1)} %collective-permute-done.1.diagonal, ...), custom_call_target="tpu_custom_call" | custom-call | flops 1000000000 | bytes 1048576 | tf_op jit(solution)/shard_map/filter/pallas_call | solution.py:337
  18.3 0.3 collective-permute-done.4.halo
  18.6 5.1 %shade_most.1 = (f32[4,32,128]{2,1,0:T(8,128)S(1)}, f32[12,112,128]{2,1,0:T(8,128)S(1)}) custom-call(f32[32,112,128]{2,1,0:T(8,128)S(1)} %get-tuple-element.40.own_grid, f32[112,128]{1,0:T(8,128)S(1)} %get-tuple-element.41.own_edge, bf16[800,128]{1,0:T(8,128)(2,1)S(1)} %collective-permute-done.4.halo, bf16[2,256,512]{2,1,0:T(8,128)(2,1)S(1)} %get-tuple-element.37.w1, ...), custom_call_target="tpu_custom_call" | custom-call | flops 10000000000 | bytes 1048576 | tf_op jit(solution)/shard_map/shade_most/pallas_call | solution.py:337
  23.7 1.4 %shade_rest.1 = f32[4,32,128]{2,1,0:T(8,128)S(1)} custom-call(bf16[800,128]{1,0:T(8,128)(2,1)S(1)} %collective-permute-done.3.halo, bf16[2,256,512]{2,1,0:T(8,128)(2,1)S(1)} %get-tuple-element.37.w1, f32[136,128]{1,0:T(8,128)S(1)} %get-tuple-element.38.w2, bf16[4,128,128]{2,1,0:T(8,128)(2,1)S(1)} %get-tuple-element.39.filters, ...), custom_call_target="tpu_custom_call" | custom-call | flops 1000000000 | bytes 1048576 | tf_op jit(solution)/shard_map/shade_rest/pallas_call | solution.py:337
  25.2 1.8 %collective-permute-start.5 = (f32[4,32,128]{2,1,0:T(8,128)S(1)}, f32[4,32,128]{2,1,0:T(8,128)S(1)}, u32[]{:S(2)}, u32[]{:S(2)}) collective-permute-start(f32[4,32,128]{2,1,0:T(8,128)S(1)} %shade_rest.1), channel_id=1, source_target_pairs={{0,8},{4,12},{8,0},{12,4},{16,24},{20,28},{24,16},{28,20},{1,9},{5... | collective-permute-start | bytes 196616 | tf_op jit(solution)/shard_map/ppermute | solution.py:438
  27.0 2.6 %collective-permute-done.5 = f32[4,32,128]{2,1,0:T(8,128)S(1)} collective-permute-done((f32[4,32,128]{2,1,0:T(8,128)S(1)}, f32[4,32,128]{2,1,0:T(8,128)S(1)}, u32[]{:S(2)}, u32[]{:S(2)}) %collective-permute-start.5) | collective-permute-done | bytes 65568 | tf_op jit(solution)/shard_map/ppermute | solution.py:438
  29.6 2.8 %collective-permute-start.6 = (f32[4,32,128]{2,1,0:T(8,128)S(1)}, f32[4,32,128]{2,1,0:T(8,128)S(1)}, u32[]{:S(2)}, u32[]{:S(2)}) collective-permute-start(f32[4,32,128]{2,1,0:T(8,128)S(1)} %pad_maximum_fusion.1), channel_id=1, source_target_pairs={{0,16},{4,20},{8,24},{12,28},{16,0},{20,4},{24,8},{28,12},{1,17},{... | collective-permute-start | bytes 196616 | tf_op jit(solution)/shard_map/ppermute | solution.py:438
  32.4 1.0 %collective-permute-start.7 = (f32[4,32,128]{2,1,0:T(8,128)S(1)}, f32[4,32,128]{2,1,0:T(8,128)S(1)}, u32[]{:S(2)}, u32[]{:S(2)}) collective-permute-start(f32[4,32,128]{2,1,0:T(8,128)S(1)} %pad_maximum_fusion.1), channel_id=1, source_target_pairs={{0,20},{4,16},{8,28},{12,24},{16,4},{20,0},{24,12},{28,8},{1,21},{... | collective-permute-start | bytes 196616 | tf_op jit(solution)/shard_map/ppermute | solution.py:438
  33.4 0.6 %collective-permute-start.8 = (f32[4,32,128]{2,1,0:T(8,128)S(1)}, f32[4,32,128]{2,1,0:T(8,128)S(1)}, u32[]{:S(2)}, u32[]{:S(2)}) collective-permute-start(f32[4,32,128]{2,1,0:T(8,128)S(1)} %pad_maximum_fusion.1), channel_id=1, source_target_pairs={{0,4},{4,0},{8,12},{12,8},{16,20},{20,16},{24,28},{28,24},{1,5},{5... | collective-permute-start | bytes 196616 | tf_op jit(solution)/shard_map/ppermute | solution.py:438
  34.0 0.9 %collective-permute-done.6 = f32[4,32,128]{2,1,0:T(8,128)S(1)} collective-permute-done((f32[4,32,128]{2,1,0:T(8,128)S(1)}, f32[4,32,128]{2,1,0:T(8,128)S(1)}, u32[]{:S(2)}, u32[]{:S(2)}) %collective-permute-start.6) | collective-permute-done | bytes 65568 | tf_op jit(solution)/shard_map/ppermute | solution.py:438
  35.0 5.5 %collective-permute-done.7 = f32[4,32,128]{2,1,0:T(8,128)S(1)} collective-permute-done((f32[4,32,128]{2,1,0:T(8,128)S(1)}, f32[4,32,128]{2,1,0:T(8,128)S(1)}, u32[]{:S(2)}, u32[]{:S(2)}) %collective-permute-start.7) | collective-permute-done | bytes 65568 | tf_op jit(solution)/shard_map/ppermute | solution.py:438
  40.6 0.7 %pad_maximum_fusion = f32[4,32,256]{2,1,0:T(8,128)} fusion(f32[1,32,256]{2,1,0:T(8,128)S(1)} %fusion.6, f32[3,32,256]{2,1,0:T(8,128)S(1)} %fusion), kind=kLoop, calls=%fused_computation.2 | loop fusion | flops 32768 | bytes 262144 | tf_op jit(solution)/shard_map/concatenate | solution.py:451
  (22 shorter events, 0.2 us)
Async XLA Ops:
  0.0 1.0 %copy-start = (bf16[4,8,32,256]{3,2,1,0:T(8,128)(2,1)S(1)}, bf16[4,8,32,256]{3,2,1,0:T(8,128)(2,1)}, u32[]{:S(2)}) copy-start(bf16[4,8,32,256]{3,2,1,0:T(8,128)(2,1)} %fields.1) | copy-start | bytes 1572868
  1.4 15.7 %collective-permute-start = (bf16[1056,128]{1,0:T(8,128)(2,1)S(1)}, bf16[1056,128]{1,0:T(8,128)(2,1)S(1)}, u32[]{:S(2)}, u32[]{:S(2)}) collective-permute-start(bf16[1056,128]{1,0:T(8,128)(2,1)S(1)} %get-tuple-element.30), channel_id=1, source_target_pairs={{0,4},{4,0},{8,12},{12,8},{16,20},{20,16},{24,28},{28,24},{1,5},{5... | collective-permute-start | bytes 811016 | tf_op jit(solution)/shard_map/ppermute | solution.py:380
  4.4 5.4 %collective-permute-start.1 = (bf16[800,128]{1,0:T(8,128)(2,1)S(1)}, bf16[800,128]{1,0:T(8,128)(2,1)S(1)}, u32[]{:S(2)}, u32[]{:S(2)}) collective-permute-start(bf16[800,128]{1,0:T(8,128)(2,1)S(1)} %get-tuple-element.31), channel_id=1, source_target_pairs={{4,8},{12,16},{20,24},{8,4},{16,12},{24,20},{5,9},{13,17},{21,25},... | collective-permute-start | bytes 614408 | tf_op jit(solution)/shard_map/ppermute | solution.py:381
  5.0 12.0 %collective-permute-start.2 = (bf16[800,128]{1,0:T(8,128)(2,1)S(1)}, bf16[800,128]{1,0:T(8,128)(2,1)S(1)}, u32[]{:S(2)}, u32[]{:S(2)}) collective-permute-start(bf16[800,128]{1,0:T(8,128)(2,1)S(1)} %get-tuple-element.32), channel_id=1, source_target_pairs={{4,12},{12,20},{20,28},{8,0},{16,8},{24,16},{5,13},{13,21},{21,29}... | collective-permute-start | bytes 614408 | tf_op jit(solution)/shard_map/ppermute | solution.py:382
  7.1 0.7 %copy-start.1 = (f32[4,32]{1,0:T(4,128)S(1)}, f32[4,32]{1,0:T(4,128)}, u32[]{:S(2)}) copy-start(f32[4,32]{1,0:T(4,128)} %w_out.1) | copy-start | bytes 1540
  7.8 0.7 %copy-start.2 = (f32[32]{0:T(128)S(1)}, f32[32]{0:T(128)}, u32[]{:S(2)}) copy-start(f32[32]{0:T(128)} %param.7) | copy-start | bytes 388
  8.5 0.7 %copy-start.3 = (f32[4]{0:T(128)S(1)}, f32[4]{0:T(128)}, u32[]{:S(2)}) copy-start(f32[4]{0:T(128)} %param.9) | copy-start | bytes 52
  17.1 1.5 %collective-permute-start.4 = (bf16[800,128]{1,0:T(8,128)(2,1)S(1)}, bf16[800,128]{1,0:T(8,128)(2,1)S(1)}, u32[]{:S(2)}, u32[]{:S(2)}) collective-permute-start(bf16[800,128]{1,0:T(8,128)(2,1)S(1)} %get-tuple-element.42), channel_id=1, source_target_pairs={{0,1},{1,0},{2,3},{3,2},{4,5},{5,4},{6,7},{7,6},{8,9},{9,8},{10,11... | collective-permute-start | bytes 614408 | tf_op jit(solution)/shard_map/ppermute | solution.py:403
  17.2 6.5 %collective-permute-start.3 = (bf16[800,128]{1,0:T(8,128)(2,1)S(1)}, bf16[800,128]{1,0:T(8,128)(2,1)S(1)}, u32[]{:S(2)}, u32[]{:S(2)}) collective-permute-start(bf16[800,128]{1,0:T(8,128)(2,1)S(1)} %get-tuple-element.36), channel_id=1, source_target_pairs={{1,2},{2,1},{5,6},{6,5},{9,10},{10,9},{13,14},{14,13},{17,18},{18,... | collective-permute-start | bytes 614408 | tf_op jit(solution)/shard_map/ppermute | solution.py:402
  25.2 4.3 %collective-permute-start.5 = (f32[4,32,128]{2,1,0:T(8,128)S(1)}, f32[4,32,128]{2,1,0:T(8,128)S(1)}, u32[]{:S(2)}, u32[]{:S(2)}) collective-permute-start(f32[4,32,128]{2,1,0:T(8,128)S(1)} %shade_rest.1), channel_id=1, source_target_pairs={{0,8},{4,12},{8,0},{12,4},{16,24},{20,28},{24,16},{28,20},{1,9},{5... | collective-permute-start | bytes 196616 | tf_op jit(solution)/shard_map/ppermute | solution.py:438
  29.6 5.4 %collective-permute-start.6 = (f32[4,32,128]{2,1,0:T(8,128)S(1)}, f32[4,32,128]{2,1,0:T(8,128)S(1)}, u32[]{:S(2)}, u32[]{:S(2)}) collective-permute-start(f32[4,32,128]{2,1,0:T(8,128)S(1)} %pad_maximum_fusion.1), channel_id=1, source_target_pairs={{0,16},{4,20},{8,24},{12,28},{16,0},{20,4},{24,8},{28,12},{1,17},{... | collective-permute-start | bytes 196616 | tf_op jit(solution)/shard_map/ppermute | solution.py:438
  32.4 8.1 %collective-permute-start.7 = (f32[4,32,128]{2,1,0:T(8,128)S(1)}, f32[4,32,128]{2,1,0:T(8,128)S(1)}, u32[]{:S(2)}, u32[]{:S(2)}) collective-permute-start(f32[4,32,128]{2,1,0:T(8,128)S(1)} %pad_maximum_fusion.1), channel_id=1, source_target_pairs={{0,20},{4,16},{8,28},{12,24},{16,4},{20,0},{24,12},{28,8},{1,21},{... | collective-permute-start | bytes 196616 | tf_op jit(solution)/shard_map/ppermute | solution.py:438
  33.4 7.1 %collective-permute-start.8 = (f32[4,32,128]{2,1,0:T(8,128)S(1)}, f32[4,32,128]{2,1,0:T(8,128)S(1)}, u32[]{:S(2)}, u32[]{:S(2)}) collective-permute-start(f32[4,32,128]{2,1,0:T(8,128)S(1)} %pad_maximum_fusion.1), channel_id=1, source_target_pairs={{0,4},{4,0},{8,12},{12,8},{16,20},{20,16},{24,28},{28,24},{1,5},{5... | collective-permute-start | bytes 196616 | tf_op jit(solution)/shard_map/ppermute | solution.py:438

commit v9 on v8

--- a/solution.py
+++ b/solution.py
@@ -380,7 +380,7 @@
     swap = lax.ppermute(theirs, "depth", swap_pairs)
     diagonal = lax.ppermute(other_halo, "depth", diagonal_pairs)
     straight = lax.ppermute(own_halo, "depth", straight_pairs)
-    swap, diagonal, straight = lax.optimization_barrier((swap, diagonal, straight))
+    swap, straight, diagonal = lax.optimization_barrier((swap, straight, diagonal))
 
     width = -(-(6 * (kw + 2 * kh) + 2) // 256) * 256
     w1, w2, filters = call(
@@ -434,21 +434,17 @@
         flops=10**9,
         name="shade_rest",
     )
-    def exchanged(distance):
-        return lax.ppermute(current, "depth", [(i, i ^ distance) for i in range(slabs)])
-
-    def composed(own, received, step):
+    step = 2
+    while step < slabs:
+        received = lax.ppermute(current, "depth", [(i, i ^ step) for i in range(slabs)])
         behind = (me & step) != 0
-        return combine(jnp.where(behind, received, own), jnp.where(behind, own, received))
-
-    step = 2
-    while 2 * step < slabs:
-        current = composed(current, exchanged(step), step)
+        current = combine(jnp.where(behind, received, current), jnp.where(behind, current, received))
         step *= 2
-    across_x, across_z, across_both = exchanged(1), exchanged(step), exchanged(1 ^ step)
-    own, other = composed(current, across_z, step), composed(across_x, across_both, step)
-    whole = jnp.concatenate([jnp.where(side == 0, own, other), jnp.where(side == 0, other, own)], 2)
-    return jnp.concatenate([whole[0:3], 1.0 - whole[3:4]], 0)
+    current = jnp.concatenate([current[0:3], 1.0 - current[3:4]], 0)
+    other = lax.ppermute(current, "depth", swap_pairs)
+    first_half = jnp.where(side == 0, current, other)
+    second_half = jnp.where(side == 0, other, current)
+    return jnp.concatenate([first_half, second_half], 2)
 
 
 def solution(mesh):

time: 41.5 us -> 40.9 us (0.986)
  the two profiles are of different devices: /device:TPU:0 before, /device:TPU:28 now
where the time goes in v9:
time: 40.9 us; the launch traced here: 40.7 us
  waiting for transfers between devices  17 us (42%)
  starting transfers between devices  10.9 us (27%)
  Pallas kernels  7.98 us (20%)
  local copies, waits for them, and re-layouts  3.81 us (9%)
  other arithmetic  0.75 us (2%)
    ppermute x2, waiting for transfers between devices, local(): lax.ppermute(current, 'depth', [(i, i ^ step) for i in range(slabs)])  9.23 us
    pallas_call x6, Pallas kernels, call(): pl.pallas_call(kernel, out_shape=out_shape, in_specs=[vmem] * len(operand...  7.98 us
    ppermute x1, waiting for transfers between devices, local(): other = lax.ppermute(current, 'depth', swap_pairs)  4.25 us
    unnamed x9, local copies, waits for them, and re-layouts  3.81 us
    ppermute x1, waiting for transfers between devices, local(): diagonal = lax.ppermute(other_halo, 'depth', diagonal_pairs)  3.53 us
    ppermute x1, starting transfers between devices, local(): diagonal = lax.ppermute(other_halo, 'depth', diagonal_pairs)  3.45 us
    ppermute x1, starting transfers between devices, local(): second = lax.ppermute(second, 'row', across)  2.5 us
    ppermute x1, starting transfers between devices, local(): straight = lax.ppermute(own_halo, 'depth', straight_pairs)  2.35 us
  transfers between devices with their start and end apart: 8, of which 4 were waited for; matrix products, arithmetic and copies ran while one was open for 2% of the time, Pallas kernels for 15%

profile of v9, /device:TPU:28, one launch (start us, length us, event | category | flops | bytes accessed | tf_op | source)
XLA Modules:
  0.0 40.7 jit_solution(12685304352431129174)
XLA Ops:
  0.0 1.0 %copy-done = bf16[4,8,32,256]{3,2,1,0:T(8,128)(2,1)S(1)} copy-done((bf16[4,8,32,256]{3,2,1,0:T(8,128)(2,1)S(1)}, bf16[4,8,32,256]{3,2,1,0:T(8,128)(2,1)}, u32[]{:S(2)}) %copy-start) | copy-done | bytes 524312
  1.0 0.3 pack.1
  1.4 1.6 %collective-permute-start = (bf16[1056,128]{1,0:T(8,128)(2,1)S(1)}, bf16[1056,128]{1,0:T(8,128)(2,1)S(1)}, u32[]{:S(2)}, u32[]{:S(2)}) collective-permute-start(bf16[1056,128]{1,0:T(8,128)(2,1)S(1)} %get-tuple-element.30), channel_id=1, source_target_pairs={{0,4},{4,0},{8,12},{12,8},{16,20},{20,16},{24,28},{28,24},{1,5},{5... | collective-permute-start | bytes 811016 | tf_op jit(solution)/shard_map/ppermute | solution.py:380
  2.9 2.4 %collective-permute-start.1 = (bf16[800,128]{1,0:T(8,128)(2,1)S(1)}, bf16[800,128]{1,0:T(8,128)(2,1)S(1)}, u32[]{:S(2)}, u32[]{:S(2)}) collective-permute-start(bf16[800,128]{1,0:T(8,128)(2,1)S(1)} %get-tuple-element.31), channel_id=1, source_target_pairs={{4,12},{12,20},{20,28},{8,0},{16,8},{24,16},{5,13},{13,21},{21,29}... | collective-permute-start | bytes 614408 | tf_op jit(solution)/shard_map/ppermute | solution.py:382
  5.3 3.5 %collective-permute-start.2 = (bf16[800,128]{1,0:T(8,128)(2,1)S(1)}, bf16[800,128]{1,0:T(8,128)(2,1)S(1)}, u32[]{:S(2)}, u32[]{:S(2)}) collective-permute-start(bf16[800,128]{1,0:T(8,128)(2,1)S(1)} %get-tuple-element.32), channel_id=1, source_target_pairs={{4,8},{12,16},{20,24},{8,4},{16,12},{24,20},{5,9},{13,17},{21,25},... | collective-permute-start | bytes 614408 | tf_op jit(solution)/shard_map/ppermute | solution.py:381
  8.7 0.8 %copy.6.w_in = f32[32,12]{1,0:T(8,128)S(1)} copy(f32[32,12]{0,1:T(8,128)} %param.6) | data formatting | bytes 3072 | tf_op args[1]
  9.5 0.7 %copy-done.1 = f32[4,32]{1,0:T(4,128)S(1)} copy-done((f32[4,32]{1,0:T(4,128)S(1)}, f32[4,32]{1,0:T(4,128)}, u32[]{:S(2)}) %copy-start.1) | copy-done | bytes 536
  10.2 0.7 %copy-done.2 = f32[32]{0:T(128)S(1)} copy-done((f32[32]{0:T(128)S(1)}, f32[32]{0:T(128)}, u32[]{:S(2)}) %copy-start.2) | copy-done | bytes 152
  10.9 0.7 %copy-done.3 = f32[4]{0:T(128)S(1)} copy-done((f32[4]{0:T(128)S(1)}, f32[4]{0:T(128)}, u32[]{:S(2)}) %copy-start.3) | copy-done | bytes 40
  11.5 0.6 %weights.1 = (bf16[2,256,512]{2,1,0:T(8,128)(2,1)S(1)}, f32[136,128]{1,0:T(8,128)S(1)}, bf16[4,128,128]{2,1,0:T(8,128)(2,1)S(1)}) custom-call(f32[32,12]{1,0:T(8,128)S(1)} %copy.6.w_in, f32[1,32]{1,0:T(1,128)S(1)} %bitcast.6, f32[4,32]{1,0:T(4,128)S(1)} %copy-done.1, f32[1,4]{1,0:T(1,128)S(1)} %bitcast.7), custom_call_target="tpu_custom_call" | custom-call | flops 100000000 | bytes 1048576 | tf_op jit(solution)/shard_map/weights/pallas_call | solution.py:337
  12.2 3.5 %collective-permute-done.2.diagonal = bf16[800,128]{1,0:T(8,128)(2,1)S(1)} collective-permute-done((bf16[800,128]{1,0:T(8,128)(2,1)S(1)}, bf16[800,128]{1,0:T(8,128)(2,1)S(1)}, u32[]{:S(2)}, u32[]{:S(2)}) %collective-permute-start.2) | collective-permute-done | bytes 204832 | tf_op jit(solution)/shard_map/ppermute | solution.py:381
  15.8 0.1 collective-permute-start.4
  15.8 2.5 %collective-permute-start.3 = (bf16[800,128]{1,0:T(8,128)(2,1)S(1)}, bf16[800,128]{1,0:T(8,128)(2,1)S(1)}, u32[]{:S(2)}, u32[]{:S(2)}) collective-permute-start(bf16[800,128]{1,0:T(8,128)(2,1)S(1)} %get-tuple-element.36), channel_id=1, source_target_pairs={{1,2},{2,1},{5,6},{6,5},{9,10},{10,9},{13,14},{14,13},{17,18},{18,... | collective-permute-start | bytes 614408 | tf_op jit(solution)/shard_map/ppermute | solution.py:402
  18.3 0.4 %filter.1 = (f32[32,112,128]{2,1,0:T(8,128)S(1)}, f32[112,128]{1,0:T(8,128)S(1)}) custom-call(bf16[1056,128]{1,0:T(8,128)(2,1)S(1)} %get-tuple-element.29.mine, bf16[1056,128]{1,0:T(8,128)(2,1)S(1)} %collective-permute-done.swap, bf16[800,128]{1,0:T(8,128)(2,1)S(1)} %collective-permute-done.1.straight, bf16[800,128]{1,0:T(8,128)(2,1)S(1)} %collective-permute-done.2.diagonal, ...), custom_call_target="tpu_custom_call" | custom-call | flops 1000000000 | bytes 1048576 | tf_op jit(solution)/shard_map/filter/pallas_call | solution.py:337
  18.8 0.0 collective-permute-done.4.halo
  18.8 5.1 %shade_most.1 = (f32[4,32,128]{2,1,0:T(8,128)S(1)}, f32[12,112,128]{2,1,0:T(8,128)S(1)}) custom-call(f32[32,112,128]{2,1,0:T(8,128)S(1)} %get-tuple-element.40.own_grid, f32[112,128]{1,0:T(8,128)S(1)} %get-tuple-element.41.own_edge, bf16[800,128]{1,0:T(8,128)(2,1)S(1)} %collective-permute-done.4.halo, bf16[2,256,512]{2,1,0:T(8,128)(2,1)S(1)} %get-tuple-element.37.w1, ...), custom_call_target="tpu_custom_call" | custom-call | flops 10000000000 | bytes 1048576 | tf_op jit(solution)/shard_map/shade_most/pallas_call | solution.py:337
  23.9 1.4 %shade_rest.1 = f32[4,32,128]{2,1,0:T(8,128)S(1)} custom-call(bf16[800,128]{1,0:T(8,128)(2,1)S(1)} %collective-permute-done.3.halo, bf16[2,256,512]{2,1,0:T(8,128)(2,1)S(1)} %get-tuple-element.37.w1, f32[136,128]{1,0:T(8,128)S(1)} %get-tuple-element.38.w2, bf16[4,128,128]{2,1,0:T(8,128)(2,1)S(1)} %get-tuple-element.39.filters, ...), custom_call_target="tpu_custom_call" | custom-call | flops 1000000000 | bytes 1048576 | tf_op jit(solution)/shard_map/shade_rest/pallas_call | solution.py:337
  25.4 0.5 %collective-permute-start.5 = (f32[4,32,128]{2,1,0:T(8,128)S(1)}, f32[4,32,128]{2,1,0:T(8,128)S(1)}, u32[]{:S(2)}, u32[]{:S(2)}) collective-permute-start(f32[4,32,128]{2,1,0:T(8,128)S(1)} %shade_rest.1), channel_id=1, source_target_pairs={{0,8},{4,12},{8,0},{12,4},{16,24},{20,28},{24,16},{28,20},{1,9},{5... | collective-permute-start | bytes 196616 | tf_op jit(solution)/shard_map/ppermute | solution.py:439
  25.9 3.8 %collective-permute-done.5 = f32[4,32,128]{2,1,0:T(8,128)S(1)} collective-permute-done((f32[4,32,128]{2,1,0:T(8,128)S(1)}, f32[4,32,128]{2,1,0:T(8,128)S(1)}, u32[]{:S(2)}, u32[]{:S(2)}) %collective-permute-start.5) | collective-permute-done | bytes 65568 | tf_op jit(solution)/shard_map/ppermute | solution.py:439
  29.8 0.4 %collective-permute-start.6 = (f32[4,32,128]{2,1,0:T(8,128)S(1)}, f32[4,32,128]{2,1,0:T(8,128)S(1)}, u32[]{:S(2)}, u32[]{:S(2)}) collective-permute-start(f32[4,32,128]{2,1,0:T(8,128)S(1)} %pad_maximum_fusion.1), channel_id=1, source_target_pairs={{0,16},{4,20},{8,24},{12,28},{16,0},{20,4},{24,8},{28,12},{1,17},{... | collective-permute-start | bytes 196616 | tf_op jit(solution)/shard_map/ppermute | solution.py:439
  30.2 5.4 %collective-permute-done.6 = f32[4,32,128]{2,1,0:T(8,128)S(1)} collective-permute-done((f32[4,32,128]{2,1,0:T(8,128)S(1)}, f32[4,32,128]{2,1,0:T(8,128)S(1)}, u32[]{:S(2)}, u32[]{:S(2)}) %collective-permute-start.6) | collective-permute-done | bytes 65568 | tf_op jit(solution)/shard_map/ppermute | solution.py:439
  35.6 0.1 collective-permute-start.7
  35.7 4.2 %collective-permute-done.7 = f32[4,32,128]{2,1,0:T(8,128)S(1)} collective-permute-done((f32[4,32,128]{2,1,0:T(8,128)S(1)}, f32[4,32,128]{2,1,0:T(8,128)S(1)}, u32[]{:S(2)}, u32[]{:S(2)}) %collective-permute-start.7) | collective-permute-done | bytes 65568 | tf_op jit(solution)/shard_map/ppermute | solution.py:444
  40.0 0.7 %pad_maximum_fusion = f32[4,32,256]{2,1,0:T(8,128)} fusion(f32[4,32,128]{2,1,0:T(8,128)S(1)} %get-tuple-element.46, f32[4,32,128]{2,1,0:T(8,128)S(1)} %get-tuple-element.45), kind=kLoop, calls=%fused_computation | loop fusion | flops 32768 | bytes 262144 | tf_op jit(solution)/shard_map/concatenate | solution.py:447
  (17 shorter events, 0.1 us)
Async XLA Ops:
  0.0 1.0 %copy-start = (bf16[4,8,32,256]{3,2,1,0:T(8,128)(2,1)S(1)}, bf16[4,8,32,256]{3,2,1,0:T(8,128)(2,1)}, u32[]{:S(2)}) copy-start(bf16[4,8,32,256]{3,2,1,0:T(8,128)(2,1)} %fields.1) | copy-start | bytes 1572868
  1.4 14.3 %collective-permute-start = (bf16[1056,128]{1,0:T(8,128)(2,1)S(1)}, bf16[1056,128]{1,0:T(8,128)(2,1)S(1)}, u32[]{:S(2)}, u32[]{:S(2)}) collective-permute-start(bf16[1056,128]{1,0:T(8,128)(2,1)S(1)} %get-tuple-element.30), channel_id=1, source_target_pairs={{0,4},{4,0},{8,12},{12,8},{16,20},{20,16},{24,28},{28,24},{1,5},{5... | collective-permute-start | bytes 811016 | tf_op jit(solution)/shard_map/ppermute | solution.py:380
  2.9 9.2 %collective-permute-start.1 = (bf16[800,128]{1,0:T(8,128)(2,1)S(1)}, bf16[800,128]{1,0:T(8,128)(2,1)S(1)}, u32[]{:S(2)}, u32[]{:S(2)}) collective-permute-start(bf16[800,128]{1,0:T(8,128)(2,1)S(1)} %get-tuple-element.31), channel_id=1, source_target_pairs={{4,12},{12,20},{20,28},{8,0},{16,8},{24,16},{5,13},{13,21},{21,29}... | collective-permute-start | bytes 614408 | tf_op jit(solution)/shard_map/ppermute | solution.py:382
  5.3 10.4 %collective-permute-start.2 = (bf16[800,128]{1,0:T(8,128)(2,1)S(1)}, bf16[800,128]{1,0:T(8,128)(2,1)S(1)}, u32[]{:S(2)}, u32[]{:S(2)}) collective-permute-start(bf16[800,128]{1,0:T(8,128)(2,1)S(1)} %get-tuple-element.32), channel_id=1, source_target_pairs={{4,8},{12,16},{20,24},{8,4},{16,12},{24,20},{5,9},{13,17},{21,25},... | collective-permute-start | bytes 614408 | tf_op jit(solution)/shard_map/ppermute | solution.py:381
  9.5 0.7 %copy-start.1 = (f32[4,32]{1,0:T(4,128)S(1)}, f32[4,32]{1,0:T(4,128)}, u32[]{:S(2)}) copy-start(f32[4,32]{1,0:T(4,128)} %w_out.1) | copy-start | bytes 1540
  10.2 0.7 %copy-start.2 = (f32[32]{0:T(128)S(1)}, f32[32]{0:T(128)}, u32[]{:S(2)}) copy-start(f32[32]{0:T(128)} %param.7) | copy-start | bytes 388
  10.9 0.7 %copy-start.3 = (f32[4]{0:T(128)S(1)}, f32[4]{0:T(128)}, u32[]{:S(2)}) copy-start(f32[4]{0:T(128)} %param.9) | copy-start | bytes 52
  15.8 3.0 %collective-permute-start.4 = (bf16[800,128]{1,0:T(8,128)(2,1)S(1)}, bf16[800,128]{1,0:T(8,128)(2,1)S(1)}, u32[]{:S(2)}, u32[]{:S(2)}) collective-permute-start(bf16[800,128]{1,0:T(8,128)(2,1)S(1)} %get-tuple-element.42), channel_id=1, source_target_pairs={{0,1},{1,0},{2,3},{3,2},{4,5},{5,4},{6,7},{7,6},{8,9},{9,8},{10,11... | collective-permute-start | bytes 614408 | tf_op jit(solution)/shard_map/ppermute | solution.py:403
  15.8 8.1 %collective-permute-start.3 = (bf16[800,128]{1,0:T(8,128)(2,1)S(1)}, bf16[800,128]{1,0:T(8,128)(2,1)S(1)}, u32[]{:S(2)}, u32[]{:S(2)}) collective-permute-start(bf16[800,128]{1,0:T(8,128)(2,1)S(1)} %get-tuple-element.36), channel_id=1, source_target_pairs={{1,2},{2,1},{5,6},{6,5},{9,10},{10,9},{13,14},{14,13},{17,18},{18,... | collective-permute-start | bytes 614408 | tf_op jit(solution)/shard_map/ppermute | solution.py:402
  25.4 4.3 %collective-permute-start.5 = (f32[4,32,128]{2,1,0:T(8,128)S(1)}, f32[4,32,128]{2,1,0:T(8,128)S(1)}, u32[]{:S(2)}, u32[]{:S(2)}) collective-permute-start(f32[4,32,128]{2,1,0:T(8,128)S(1)} %shade_rest.1), channel_id=1, source_target_pairs={{0,8},{4,12},{8,0},{12,4},{16,24},{20,28},{24,16},{28,20},{1,9},{5... | collective-permute-start | bytes 196616 | tf_op jit(solution)/shard_map/ppermute | solution.py:439
  29.8 5.8 %collective-permute-start.6 = (f32[4,32,128]{2,1,0:T(8,128)S(1)}, f32[4,32,128]{2,1,0:T(8,128)S(1)}, u32[]{:S(2)}, u32[]{:S(2)}) collective-permute-start(f32[4,32,128]{2,1,0:T(8,128)S(1)} %pad_maximum_fusion.1), channel_id=1, source_target_pairs={{0,16},{4,20},{8,24},{12,28},{16,0},{20,4},{24,8},{28,12},{1,17},{... | collective-permute-start | bytes 196616 | tf_op jit(solution)/shard_map/ppermute | solution.py:439
  35.6 4.3 %collective-permute-start.7 = (f32[4,32,128]{2,1,0:T(8,128)S(1)}, f32[4,32,128]{2,1,0:T(8,128)S(1)}, u32[]{:S(2)}, u32[]{:S(2)}) collective-permute-start(f32[4,32,128]{2,1,0:T(8,128)S(1)} %pad_maximum_fusion.2), channel_id=1, source_target_pairs={{0,4},{4,0},{8,12},{12,8},{16,20},{20,16},{24,28},{28,24},{1,5},{5... | collective-permute-start | bytes 196616 | tf_op jit(solution)/shard_map/ppermute | solution.py:444

commit v10 on v9

--- a/solution.py
+++ b/solution.py
@@ -347,8 +347,8 @@
 
 
 def combine(front, back):
-    color = front[0:3] + front[3:4] * back[0:3]
-    return jnp.concatenate([color, front[3:4] * back[3:4]], 0)
+    is_color = lax.broadcasted_iota(jnp.int32, front.shape, 0) < 3
+    return jnp.where(is_color, front, 0.0) + front[3:4] * back
 
 
 def local(fields, w_in, b_in, w_out, b_out):
@@ -440,11 +440,12 @@
         behind = (me & step) != 0
         current = combine(jnp.where(behind, received, current), jnp.where(behind, current, received))
         step *= 2
-    current = jnp.concatenate([current[0:3], 1.0 - current[3:4]], 0)
     other = lax.ppermute(current, "depth", swap_pairs)
     first_half = jnp.where(side == 0, current, other)
     second_half = jnp.where(side == 0, other, current)
-    return jnp.concatenate([first_half, second_half], 2)
+    whole = jnp.concatenate([first_half, second_half], 2)
+    is_color = lax.broadcasted_iota(jnp.int32, whole.shape, 0) < 3
+    return jnp.where(is_color, whole, 1.0 - whole)
 
 
 def solution(mesh):

time: 40.9 us -> 40.7 us (level)
    select_n x0 -> x1, other arithmetic: none -> 0.73 us  [local(): return jnp.where(is_color, whole, 1.0 - whole)]
    concatenate x3 -> x0, other arithmetic: 0.68 us -> none  [the longest x1 0.67 us: local(): return jnp.concatenate([first_half, second_half], 2)]
where the time goes in v10:
time: 40.7 us; the launch traced here: 40.4 us
  waiting for transfers between devices  17 us (42%)
  starting transfers between devices  10.8 us (27%)
  Pallas kernels  7.68 us (19%)
  local copies, waits for them, and re-layouts  3.82 us (9%)
  other arithmetic  0.93 us (2%)
    ppermute x2, waiting for transfers between devices, local(): lax.ppermute(current, 'depth', [(i, i ^ step) for i in range(slabs)])  9.23 us
    pallas_call x6, Pallas kernels, call(): pl.pallas_call(kernel, out_shape=out_shape, in_specs=[vmem] * len(operand...  7.68 us
    ppermute x1, waiting for transfers between devices, local(): other = lax.ppermute(current, 'depth', swap_pairs)  4.25 us
    unnamed x9, local copies, waits for them, and re-layouts  3.81 us
    ppermute x1, waiting for transfers between devices, local(): diagonal = lax.ppermute(other_halo, 'depth', diagonal_pairs)  3.53 us
    ppermute x1, starting transfers between devices, local(): diagonal = lax.ppermute(other_halo, 'depth', diagonal_pairs)  3.45 us
    ppermute x1, starting transfers between devices, local(): second = lax.ppermute(second, 'row', across)  2.5 us
    ppermute x1, starting transfers between devices, local(): straight = lax.ppermute(own_halo, 'depth', straight_pairs)  2.35 us
  transfers between devices with their start and end apart: 8, of which 4 were waited for; matrix products, arithmetic and copies ran while one was open for 2% of the time, Pallas kernels for 15%

profile of v10, /device:TPU:28, one launch (start us, length us, event | category | flops | bytes accessed | tf_op | source)
XLA Modules:
  0.0 40.4 jit_solution(614149226905998961)
XLA Ops:
  0.0 1.0 %copy-done = bf16[4,8,32,256]{3,2,1,0:T(8,128)(2,1)S(1)} copy-done((bf16[4,8,32,256]{3,2,1,0:T(8,128)(2,1)S(1)}, bf16[4,8,32,256]{3,2,1,0:T(8,128)(2,1)}, u32[]{:S(2)}) %copy-start) | copy-done | bytes 524312
  1.0 0.3 pack.1
  1.4 1.6 %collective-permute-start = (bf16[1056,128]{1,0:T(8,128)(2,1)S(1)}, bf16[1056,128]{1,0:T(8,128)(2,1)S(1)}, u32[]{:S(2)}, u32[]{:S(2)}) collective-permute-start(bf16[1056,128]{1,0:T(8,128)(2,1)S(1)} %get-tuple-element.30), channel_id=1, source_target_pairs={{0,4},{4,0},{8,12},{12,8},{16,20},{20,16},{24,28},{28,24},{1,5},{5... | collective-permute-start | bytes 811016 | tf_op jit(solution)/shard_map/ppermute | solution.py:380
  2.9 2.4 %collective-permute-start.1 = (bf16[800,128]{1,0:T(8,128)(2,1)S(1)}, bf16[800,128]{1,0:T(8,128)(2,1)S(1)}, u32[]{:S(2)}, u32[]{:S(2)}) collective-permute-start(bf16[800,128]{1,0:T(8,128)(2,1)S(1)} %get-tuple-element.31), channel_id=1, source_target_pairs={{4,12},{12,20},{20,28},{8,0},{16,8},{24,16},{5,13},{13,21},{21,29}... | collective-permute-start | bytes 614408 | tf_op jit(solution)/shard_map/ppermute | solution.py:382
  5.3 3.5 %collective-permute-start.2 = (bf16[800,128]{1,0:T(8,128)(2,1)S(1)}, bf16[800,128]{1,0:T(8,128)(2,1)S(1)}, u32[]{:S(2)}, u32[]{:S(2)}) collective-permute-start(bf16[800,128]{1,0:T(8,128)(2,1)S(1)} %get-tuple-element.32), channel_id=1, source_target_pairs={{4,8},{12,16},{20,24},{8,4},{16,12},{24,20},{5,9},{13,17},{21,25},... | collective-permute-start | bytes 614408 | tf_op jit(solution)/shard_map/ppermute | solution.py:381
  8.7 0.8 %copy.6.w_in = f32[32,12]{1,0:T(8,128)S(1)} copy(f32[32,12]{0,1:T(8,128)} %param.6) | data formatting | bytes 3072 | tf_op args[1]
  9.5 0.7 %copy-done.1 = f32[4,32]{1,0:T(4,128)S(1)} copy-done((f32[4,32]{1,0:T(4,128)S(1)}, f32[4,32]{1,0:T(4,128)}, u32[]{:S(2)}) %copy-start.1) | copy-done | bytes 536
  10.2 0.7 %copy-done.2 = f32[32]{0:T(128)S(1)} copy-done((f32[32]{0:T(128)S(1)}, f32[32]{0:T(128)}, u32[]{:S(2)}) %copy-start.2) | copy-done | bytes 152
  10.9 0.7 %copy-done.3 = f32[4]{0:T(128)S(1)} copy-done((f32[4]{0:T(128)S(1)}, f32[4]{0:T(128)}, u32[]{:S(2)}) %copy-start.3) | copy-done | bytes 40
  11.5 0.6 %weights.1 = (bf16[2,256,512]{2,1,0:T(8,128)(2,1)S(1)}, f32[136,128]{1,0:T(8,128)S(1)}, bf16[4,128,128]{2,1,0:T(8,128)(2,1)S(1)}) custom-call(f32[32,12]{1,0:T(8,128)S(1)} %copy.6.w_in, f32[1,32]{1,0:T(1,128)S(1)} %bitcast.6, f32[4,32]{1,0:T(4,128)S(1)} %copy-done.1, f32[1,4]{1,0:T(1,128)S(1)} %bitcast.7), custom_call_target="tpu_custom_call" | custom-call | flops 100000000 | bytes 1048576 | tf_op jit(solution)/shard_map/weights/pallas_call | solution.py:337
  12.2 3.5 %collective-permute-done.2.diagonal = bf16[800,128]{1,0:T(8,128)(2,1)S(1)} collective-permute-done((bf16[800,128]{1,0:T(8,128)(2,1)S(1)}, bf16[800,128]{1,0:T(8,128)(2,1)S(1)}, u32[]{:S(2)}, u32[]{:S(2)}) %collective-permute-start.2) | collective-permute-done | bytes 204832 | tf_op jit(solution)/shard_map/ppermute | solution.py:381
  15.8 0.1 collective-permute-start.4
  15.8 2.5 %collective-permute-start.3 = (bf16[800,128]{1,0:T(8,128)(2,1)S(1)}, bf16[800,128]{1,0:T(8,128)(2,1)S(1)}, u32[]{:S(2)}, u32[]{:S(2)}) collective-permute-start(bf16[800,128]{1,0:T(8,128)(2,1)S(1)} %get-tuple-element.36), channel_id=1, source_target_pairs={{1,2},{2,1},{5,6},{6,5},{9,10},{10,9},{13,14},{14,13},{17,18},{18,... | collective-permute-start | bytes 614408 | tf_op jit(solution)/shard_map/ppermute | solution.py:402
  18.3 0.4 %filter.1 = (f32[32,112,128]{2,1,0:T(8,128)S(1)}, f32[112,128]{1,0:T(8,128)S(1)}) custom-call(bf16[1056,128]{1,0:T(8,128)(2,1)S(1)} %get-tuple-element.29.mine, bf16[1056,128]{1,0:T(8,128)(2,1)S(1)} %collective-permute-done.swap, bf16[800,128]{1,0:T(8,128)(2,1)S(1)} %collective-permute-done.1.straight, bf16[800,128]{1,0:T(8,128)(2,1)S(1)} %collective-permute-done.2.diagonal, ...), custom_call_target="tpu_custom_call" | custom-call | flops 1000000000 | bytes 1048576 | tf_op jit(solution)/shard_map/filter/pallas_call | solution.py:337
  18.8 4.8 %shade_most.1 = (f32[4,32,128]{2,1,0:T(8,128)S(1)}, f32[12,112,128]{2,1,0:T(8,128)S(1)}) custom-call(f32[32,112,128]{2,1,0:T(8,128)S(1)} %get-tuple-element.40.own_grid, f32[112,128]{1,0:T(8,128)S(1)} %get-tuple-element.41.own_edge, bf16[800,128]{1,0:T(8,128)(2,1)S(1)} %collective-permute-done.4.halo, bf16[2,256,512]{2,1,0:T(8,128)(2,1)S(1)} %get-tuple-element.37.w1, ...), custom_call_target="tpu_custom_call" | custom-call | flops 10000000000 | bytes 1048576 | tf_op jit(solution)/shard_map/shade_most/pallas_call | solution.py:337
  23.6 1.4 %shade_rest.1 = f32[4,32,128]{2,1,0:T(8,128)S(1)} custom-call(bf16[800,128]{1,0:T(8,128)(2,1)S(1)} %collective-permute-done.3.halo, bf16[2,256,512]{2,1,0:T(8,128)(2,1)S(1)} %get-tuple-element.37.w1, f32[136,128]{1,0:T(8,128)S(1)} %get-tuple-element.38.w2, bf16[4,128,128]{2,1,0:T(8,128)(2,1)S(1)} %get-tuple-element.39.filters, ...), custom_call_target="tpu_custom_call" | custom-call | flops 1000000000 | bytes 1048576 | tf_op jit(solution)/shard_map/shade_rest/pallas_call | solution.py:337
  25.1 0.5 %collective-permute-start.5 = (f32[4,32,128]{2,1,0:T(8,128)S(1)}, f32[4,32,128]{2,1,0:T(8,128)S(1)}, u32[]{:S(2)}, u32[]{:S(2)}) collective-permute-start(f32[4,32,128]{2,1,0:T(8,128)S(1)} %shade_rest.1), channel_id=1, source_target_pairs={{0,8},{4,12},{8,0},{12,4},{16,24},{20,28},{24,16},{28,20},{1,9},{5... | collective-permute-start | bytes 196616 | tf_op jit(solution)/shard_map/ppermute | solution.py:439
  25.6 3.8 %collective-permute-done.5 = f32[4,32,128]{2,1,0:T(8,128)S(1)} collective-permute-done((f32[4,32,128]{2,1,0:T(8,128)S(1)}, f32[4,32,128]{2,1,0:T(8,128)S(1)}, u32[]{:S(2)}, u32[]{:S(2)}) %collective-permute-start.5) | collective-permute-done | bytes 65568 | tf_op jit(solution)/shard_map/ppermute | solution.py:439
  29.4 0.1 multiply_add_fusion.1
  29.5 0.3 collective-permute-start.6
  29.8 5.4 %collective-permute-done.6 = f32[4,32,128]{2,1,0:T(8,128)S(1)} collective-permute-done((f32[4,32,128]{2,1,0:T(8,128)S(1)}, f32[4,32,128]{2,1,0:T(8,128)S(1)}, u32[]{:S(2)}, u32[]{:S(2)}) %collective-permute-start.6) | collective-permute-done | bytes 65568 | tf_op jit(solution)/shard_map/ppermute | solution.py:439
  35.3 0.1 multiply_add_fusion
  35.4 4.2 %collective-permute-done.7 = f32[4,32,128]{2,1,0:T(8,128)S(1)} collective-permute-done((f32[4,32,128]{2,1,0:T(8,128)S(1)}, f32[4,32,128]{2,1,0:T(8,128)S(1)}, u32[]{:S(2)}, u32[]{:S(2)}) %collective-permute-start.7) | collective-permute-done | bytes 65568 | tf_op jit(solution)/shard_map/ppermute | solution.py:443
  39.7 0.7 %subtract_select_fusion = f32[4,32,256]{2,1,0:T(8,128)} fusion(f32[4,32,128]{2,1,0:T(8,128)S(1)} %get-tuple-element.46, f32[4,32,128]{2,1,0:T(8,128)S(1)} %get-tuple-element.45, pred[4]{0:T(512)(128)(4,1)S(1)} %iota_compare_fusion), kind=kLoop, calls=%fused_computation | loop fusion | flops 98304 | bytes 262148 | tf_op jit(solution)/shard_map/jit(_where)/select_n | solution.py:448
  (16 shorter events, 0.1 us)
Async XLA Ops:
  0.0 1.0 %copy-start = (bf16[4,8,32,256]{3,2,1,0:T(8,128)(2,1)S(1)}, bf16[4,8,32,256]{3,2,1,0:T(8,128)(2,1)}, u32[]{:S(2)}) copy-start(bf16[4,8,32,256]{3,2,1,0:T(8,128)(2,1)} %fields.1) | copy-start | bytes 1572868
  1.4 14.3 %collective-permute-start = (bf16[1056,128]{1,0:T(8,128)(2,1)S(1)}, bf16[1056,128]{1,0:T(8,128)(2,1)S(1)}, u32[]{:S(2)}, u32[]{:S(2)}) collective-permute-start(bf16[1056,128]{1,0:T(8,128)(2,1)S(1)} %get-tuple-element.30), channel_id=1, source_target_pairs={{0,4},{4,0},{8,12},{12,8},{16,20},{20,16},{24,28},{28,24},{1,5},{5... | collective-permute-start | bytes 811016 | tf_op jit(solution)/shard_map/ppermute | solution.py:380
  2.9 9.2 %collective-permute-start.1 = (bf16[800,128]{1,0:T(8,128)(2,1)S(1)}, bf16[800,128]{1,0:T(8,128)(2,1)S(1)}, u32[]{:S(2)}, u32[]{:S(2)}) collective-permute-start(bf16[800,128]{1,0:T(8,128)(2,1)S(1)} %get-tuple-element.31), channel_id=1, source_target_pairs={{4,12},{12,20},{20,28},{8,0},{16,8},{24,16},{5,13},{13,21},{21,29}... | collective-permute-start | bytes 614408 | tf_op jit(solution)/shard_map/ppermute | solution.py:382
  5.3 10.4 %collective-permute-start.2 = (bf16[800,128]{1,0:T(8,128)(2,1)S(1)}, bf16[800,128]{1,0:T(8,128)(2,1)S(1)}, u32[]{:S(2)}, u32[]{:S(2)}) collective-permute-start(bf16[800,128]{1,0:T(8,128)(2,1)S(1)} %get-tuple-element.32), channel_id=1, source_target_pairs={{4,8},{12,16},{20,24},{8,4},{16,12},{24,20},{5,9},{13,17},{21,25},... | collective-permute-start | bytes 614408 | tf_op jit(solution)/shard_map/ppermute | solution.py:381
  9.5 0.7 %copy-start.1 = (f32[4,32]{1,0:T(4,128)S(1)}, f32[4,32]{1,0:T(4,128)}, u32[]{:S(2)}) copy-start(f32[4,32]{1,0:T(4,128)} %w_out.1) | copy-start | bytes 1540
  10.2 0.7 %copy-start.2 = (f32[32]{0:T(128)S(1)}, f32[32]{0:T(128)}, u32[]{:S(2)}) copy-start(f32[32]{0:T(128)} %param.7) | copy-start | bytes 388
  10.9 0.7 %copy-start.3 = (f32[4]{0:T(128)S(1)}, f32[4]{0:T(128)}, u32[]{:S(2)}) copy-start(f32[4]{0:T(128)} %param.9) | copy-start | bytes 52
  15.8 3.0 %collective-permute-start.4 = (bf16[800,128]{1,0:T(8,128)(2,1)S(1)}, bf16[800,128]{1,0:T(8,128)(2,1)S(1)}, u32[]{:S(2)}, u32[]{:S(2)}) collective-permute-start(bf16[800,128]{1,0:T(8,128)(2,1)S(1)} %get-tuple-element.42), channel_id=1, source_target_pairs={{0,1},{1,0},{2,3},{3,2},{4,5},{5,4},{6,7},{7,6},{8,9},{9,8},{10,11... | collective-permute-start | bytes 614408 | tf_op jit(solution)/shard_map/ppermute | solution.py:403
  15.8 7.8 %collective-permute-start.3 = (bf16[800,128]{1,0:T(8,128)(2,1)S(1)}, bf16[800,128]{1,0:T(8,128)(2,1)S(1)}, u32[]{:S(2)}, u32[]{:S(2)}) collective-permute-start(bf16[800,128]{1,0:T(8,128)(2,1)S(1)} %get-tuple-element.36), channel_id=1, source_target_pairs={{1,2},{2,1},{5,6},{6,5},{9,10},{10,9},{13,14},{14,13},{17,18},{18,... | collective-permute-start | bytes 614408 | tf_op jit(solution)/shard_map/ppermute | solution.py:402
  25.1 4.3 %collective-permute-start.5 = (f32[4,32,128]{2,1,0:T(8,128)S(1)}, f32[4,32,128]{2,1,0:T(8,128)S(1)}, u32[]{:S(2)}, u32[]{:S(2)}) collective-permute-start(f32[4,32,128]{2,1,0:T(8,128)S(1)} %shade_rest.1), channel_id=1, source_target_pairs={{0,8},{4,12},{8,0},{12,4},{16,24},{20,28},{24,16},{28,20},{1,9},{5... | collective-permute-start | bytes 196616 | tf_op jit(solution)/shard_map/ppermute | solution.py:439
  29.5 5.8 %collective-permute-start.6 = (f32[4,32,128]{2,1,0:T(8,128)S(1)}, f32[4,32,128]{2,1,0:T(8,128)S(1)}, u32[]{:S(2)}, u32[]{:S(2)}) collective-permute-start(f32[4,32,128]{2,1,0:T(8,128)S(1)} %multiply_add_fusion.1), channel_id=1, source_target_pairs={{0,16},{4,20},{8,24},{12,28},{16,0},{20,4},{24,8},{28,12},{1,17},{... | collective-permute-start | bytes 196616 | tf_op jit(solution)/shard_map/ppermute | solution.py:439
  35.4 4.3 %collective-permute-start.7 = (f32[4,32,128]{2,1,0:T(8,128)S(1)}, f32[4,32,128]{2,1,0:T(8,128)S(1)}, u32[]{:S(2)}, u32[]{:S(2)}) collective-permute-start(f32[4,32,128]{2,1,0:T(8,128)S(1)} %multiply_add_fusion), channel_id=1, source_target_pairs={{0,4},{4,0},{8,12},{12,8},{16,20},{20,16},{24,28},{28,24},{1,5},{5... | collective-permute-start | bytes 196616 | tf_op jit(solution)/shard_map/ppermute | solution.py:443

commit v11 on v10

--- a/solution.py
+++ b/solution.py
@@ -252,11 +252,11 @@
                 for c in range(4):
                     o[c] = o[c] + splat(c * hidden + h) * unit
             x = o[3]
-            optical = (jnp.maximum(x, 0.0) + jnp.log(1.0 + jnp.exp(-jnp.abs(x)))) * scale
+            optical = jnp.log(1.0 + jnp.exp(x)) * scale
             through = optical
             for step in (1, 2, 4):
                 through = through + jnp.where(sub >= step, pltpu.roll(through, step, 0), 0.0)
-            through = through + total
+            through = through + total if half else through
             total = through[layers - 1 :]
             after = jnp.exp(-through)
             before = jnp.where(sub == 0, front, pltpu.roll(after, 1, 0))

time: 40.7 us -> 40.6 us (level)
  no operation moved by 1% of the time
where the time goes in v11:
time: 40.6 us; the launch traced here: 40.4 us
  waiting for transfers between devices  17 us (42%)
  starting transfers between devices  10.8 us (27%)
  Pallas kernels  7.64 us (19%)
  local copies, waits for them, and re-layouts  3.82 us (9%)
  other arithmetic  0.93 us (2%)
    ppermute x2, waiting for transfers between devices, local(): lax.ppermute(current, 'depth', [(i, i ^ step) for i in range(slabs)])  9.24 us
    pallas_call x6, Pallas kernels, call(): pl.pallas_call(kernel, out_shape=out_shape, in_specs=[vmem] * len(operand...  7.64 us
    ppermute x1, waiting for transfers between devices, local(): other = lax.ppermute(current, 'depth', swap_pairs)  4.25 us
    unnamed x9, local copies, waits for them, and re-layouts  3.81 us
    ppermute x1, waiting for transfers between devices, local(): diagonal = lax.ppermute(other_halo, 'depth', diagonal_pairs)  3.53 us
    ppermute x1, starting transfers between devices, local(): diagonal = lax.ppermute(other_halo, 'depth', diagonal_pairs)  3.45 us
    ppermute x1, starting transfers between devices, local(): second = lax.ppermute(second, 'row', across)  2.5 us
    ppermute x1, starting transfers between devices, local(): straight = lax.ppermute(own_halo, 'depth', straight_pairs)  2.35 us
  transfers between devices with their start and end apart: 8, of which 4 were waited for; matrix products, arithmetic and copies ran while one was open for 2% of the time, Pallas kernels for 15%

profile of v11, /device:TPU:28, one launch (start us, length us, event | category | flops | bytes accessed | tf_op | source)
XLA Modules:
  0.0 40.4 jit_solution(1585865554305988617)
XLA Ops:
  0.0 1.0 %copy-done = bf16[4,8,32,256]{3,2,1,0:T(8,128)(2,1)S(1)} copy-done((bf16[4,8,32,256]{3,2,1,0:T(8,128)(2,1)S(1)}, bf16[4,8,32,256]{3,2,1,0:T(8,128)(2,1)}, u32[]{:S(2)}) %copy-start) | copy-done | bytes 524312
  1.0 0.3 pack.1
  1.4 1.6 %collective-permute-start = (bf16[1056,128]{1,0:T(8,128)(2,1)S(1)}, bf16[1056,128]{1,0:T(8,128)(2,1)S(1)}, u32[]{:S(2)}, u32[]{:S(2)}) collective-permute-start(bf16[1056,128]{1,0:T(8,128)(2,1)S(1)} %get-tuple-element.30), channel_id=1, source_target_pairs={{0,4},{4,0},{8,12},{12,8},{16,20},{20,16},{24,28},{28,24},{1,5},{5... | collective-permute-start | bytes 811016 | tf_op jit(solution)/shard_map/ppermute | solution.py:380
  2.9 2.4 %collective-permute-start.1 = (bf16[800,128]{1,0:T(8,128)(2,1)S(1)}, bf16[800,128]{1,0:T(8,128)(2,1)S(1)}, u32[]{:S(2)}, u32[]{:S(2)}) collective-permute-start(bf16[800,128]{1,0:T(8,128)(2,1)S(1)} %get-tuple-element.31), channel_id=1, source_target_pairs={{4,12},{12,20},{20,28},{8,0},{16,8},{24,16},{5,13},{13,21},{21,29}... | collective-permute-start | bytes 614408 | tf_op jit(solution)/shard_map/ppermute | solution.py:382
  5.3 3.5 %collective-permute-start.2 = (bf16[800,128]{1,0:T(8,128)(2,1)S(1)}, bf16[800,128]{1,0:T(8,128)(2,1)S(1)}, u32[]{:S(2)}, u32[]{:S(2)}) collective-permute-start(bf16[800,128]{1,0:T(8,128)(2,1)S(1)} %get-tuple-element.32), channel_id=1, source_target_pairs={{4,8},{12,16},{20,24},{8,4},{16,12},{24,20},{5,9},{13,17},{21,25},... | collective-permute-start | bytes 614408 | tf_op jit(solution)/shard_map/ppermute | solution.py:381
  8.7 0.8 %copy.6.w_in = f32[32,12]{1,0:T(8,128)S(1)} copy(f32[32,12]{0,1:T(8,128)} %param.6) | data formatting | bytes 3072 | tf_op args[1]
  9.5 0.7 %copy-done.1 = f32[4,32]{1,0:T(4,128)S(1)} copy-done((f32[4,32]{1,0:T(4,128)S(1)}, f32[4,32]{1,0:T(4,128)}, u32[]{:S(2)}) %copy-start.1) | copy-done | bytes 536
  10.2 0.7 %copy-done.2 = f32[32]{0:T(128)S(1)} copy-done((f32[32]{0:T(128)S(1)}, f32[32]{0:T(128)}, u32[]{:S(2)}) %copy-start.2) | copy-done | bytes 152
  10.9 0.7 %copy-done.3 = f32[4]{0:T(128)S(1)} copy-done((f32[4]{0:T(128)S(1)}, f32[4]{0:T(128)}, u32[]{:S(2)}) %copy-start.3) | copy-done | bytes 40
  11.5 0.6 %weights.1 = (bf16[2,256,512]{2,1,0:T(8,128)(2,1)S(1)}, f32[136,128]{1,0:T(8,128)S(1)}, bf16[4,128,128]{2,1,0:T(8,128)(2,1)S(1)}) custom-call(f32[32,12]{1,0:T(8,128)S(1)} %copy.6.w_in, f32[1,32]{1,0:T(1,128)S(1)} %bitcast.6, f32[4,32]{1,0:T(4,128)S(1)} %copy-done.1, f32[1,4]{1,0:T(1,128)S(1)} %bitcast.7), custom_call_target="tpu_custom_call" | custom-call | flops 100000000 | bytes 1048576 | tf_op jit(solution)/shard_map/weights/pallas_call | solution.py:337
  12.2 3.5 %collective-permute-done.2.diagonal = bf16[800,128]{1,0:T(8,128)(2,1)S(1)} collective-permute-done((bf16[800,128]{1,0:T(8,128)(2,1)S(1)}, bf16[800,128]{1,0:T(8,128)(2,1)S(1)}, u32[]{:S(2)}, u32[]{:S(2)}) %collective-permute-start.2) | collective-permute-done | bytes 204832 | tf_op jit(solution)/shard_map/ppermute | solution.py:381
  15.8 0.1 collective-permute-start.4
  15.8 2.5 %collective-permute-start.3 = (bf16[800,128]{1,0:T(8,128)(2,1)S(1)}, bf16[800,128]{1,0:T(8,128)(2,1)S(1)}, u32[]{:S(2)}, u32[]{:S(2)}) collective-permute-start(bf16[800,128]{1,0:T(8,128)(2,1)S(1)} %get-tuple-element.36), channel_id=1, source_target_pairs={{1,2},{2,1},{5,6},{6,5},{9,10},{10,9},{13,14},{14,13},{17,18},{18,... | collective-permute-start | bytes 614408 | tf_op jit(solution)/shard_map/ppermute | solution.py:402
  18.3 0.4 %filter.1 = (f32[32,112,128]{2,1,0:T(8,128)S(1)}, f32[112,128]{1,0:T(8,128)S(1)}) custom-call(bf16[1056,128]{1,0:T(8,128)(2,1)S(1)} %get-tuple-element.29.mine, bf16[1056,128]{1,0:T(8,128)(2,1)S(1)} %collective-permute-done.swap, bf16[800,128]{1,0:T(8,128)(2,1)S(1)} %collective-permute-done.1.straight, bf16[800,128]{1,0:T(8,128)(2,1)S(1)} %collective-permute-done.2.diagonal, ...), custom_call_target="tpu_custom_call" | custom-call | flops 1000000000 | bytes 1048576 | tf_op jit(solution)/shard_map/filter/pallas_call | solution.py:337
  18.8 4.8 %shade_most.1 = (f32[4,32,128]{2,1,0:T(8,128)S(1)}, f32[12,112,128]{2,1,0:T(8,128)S(1)}) custom-call(f32[32,112,128]{2,1,0:T(8,128)S(1)} %get-tuple-element.40.own_grid, f32[112,128]{1,0:T(8,128)S(1)} %get-tuple-element.41.own_edge, bf16[800,128]{1,0:T(8,128)(2,1)S(1)} %collective-permute-done.4.halo, bf16[2,256,512]{2,1,0:T(8,128)(2,1)S(1)} %get-tuple-element.37.w1, ...), custom_call_target="tpu_custom_call" | custom-call | flops 10000000000 | bytes 1048576 | tf_op jit(solution)/shard_map/shade_most/pallas_call | solution.py:337
  23.6 1.4 %shade_rest.1 = f32[4,32,128]{2,1,0:T(8,128)S(1)} custom-call(bf16[800,128]{1,0:T(8,128)(2,1)S(1)} %collective-permute-done.3.halo, bf16[2,256,512]{2,1,0:T(8,128)(2,1)S(1)} %get-tuple-element.37.w1, f32[136,128]{1,0:T(8,128)S(1)} %get-tuple-element.38.w2, bf16[4,128,128]{2,1,0:T(8,128)(2,1)S(1)} %get-tuple-element.39.filters, ...), custom_call_target="tpu_custom_call" | custom-call | flops 1000000000 | bytes 1048576 | tf_op jit(solution)/shard_map/shade_rest/pallas_call | solution.py:337
  25.0 0.5 %collective-permute-start.5 = (f32[4,32,128]{2,1,0:T(8,128)S(1)}, f32[4,32,128]{2,1,0:T(8,128)S(1)}, u32[]{:S(2)}, u32[]{:S(2)}) collective-permute-start(f32[4,32,128]{2,1,0:T(8,128)S(1)} %shade_rest.1), channel_id=1, source_target_pairs={{0,8},{4,12},{8,0},{12,4},{16,24},{20,28},{24,16},{28,20},{1,9},{5... | collective-permute-start | bytes 196616 | tf_op jit(solution)/shard_map/ppermute | solution.py:439
  25.5 3.8 %collective-permute-done.5 = f32[4,32,128]{2,1,0:T(8,128)S(1)} collective-permute-done((f32[4,32,128]{2,1,0:T(8,128)S(1)}, f32[4,32,128]{2,1,0:T(8,128)S(1)}, u32[]{:S(2)}, u32[]{:S(2)}) %collective-permute-start.5) | collective-permute-done | bytes 65568 | tf_op jit(solution)/shard_map/ppermute | solution.py:439
  29.4 0.1 multiply_add_fusion.1
  29.5 0.3 collective-permute-start.6
  29.8 5.4 %collective-permute-done.6 = f32[4,32,128]{2,1,0:T(8,128)S(1)} collective-permute-done((f32[4,32,128]{2,1,0:T(8,128)S(1)}, f32[4,32,128]{2,1,0:T(8,128)S(1)}, u32[]{:S(2)}, u32[]{:S(2)}) %collective-permute-start.6) | collective-permute-done | bytes 65568 | tf_op jit(solution)/shard_map/ppermute | solution.py:439
  35.2 0.1 multiply_add_fusion
  35.4 4.2 %collective-permute-done.7 = f32[4,32,128]{2,1,0:T(8,128)S(1)} collective-permute-done((f32[4,32,128]{2,1,0:T(8,128)S(1)}, f32[4,32,128]{2,1,0:T(8,128)S(1)}, u32[]{:S(2)}, u32[]{:S(2)}) %collective-permute-start.7) | collective-permute-done | bytes 65568 | tf_op jit(solution)/shard_map/ppermute | solution.py:443
  39.6 0.7 %subtract_select_fusion = f32[4,32,256]{2,1,0:T(8,128)} fusion(f32[4,32,128]{2,1,0:T(8,128)S(1)} %get-tuple-element.46, f32[4,32,128]{2,1,0:T(8,128)S(1)} %get-tuple-element.45, pred[4]{0:T(512)(128)(4,1)S(1)} %iota_compare_fusion), kind=kLoop, calls=%fused_computation | loop fusion | flops 98304 | bytes 262148 | tf_op jit(solution)/shard_map/jit(_where)/select_n | solution.py:448
  (16 shorter events, 0.1 us)
Async XLA Ops:
  0.0 1.0 %copy-start = (bf16[4,8,32,256]{3,2,1,0:T(8,128)(2,1)S(1)}, bf16[4,8,32,256]{3,2,1,0:T(8,128)(2,1)}, u32[]{:S(2)}) copy-start(bf16[4,8,32,256]{3,2,1,0:T(8,128)(2,1)} %fields.1) | copy-start | bytes 1572868
  1.4 14.3 %collective-permute-start = (bf16[1056,128]{1,0:T(8,128)(2,1)S(1)}, bf16[1056,128]{1,0:T(8,128)(2,1)S(1)}, u32[]{:S(2)}, u32[]{:S(2)}) collective-permute-start(bf16[1056,128]{1,0:T(8,128)(2,1)S(1)} %get-tuple-element.30), channel_id=1, source_target_pairs={{0,4},{4,0},{8,12},{12,8},{16,20},{20,16},{24,28},{28,24},{1,5},{5... | collective-permute-start | bytes 811016 | tf_op jit(solution)/shard_map/ppermute | solution.py:380
  2.9 9.2 %collective-permute-start.1 = (bf16[800,128]{1,0:T(8,128)(2,1)S(1)}, bf16[800,128]{1,0:T(8,128)(2,1)S(1)}, u32[]{:S(2)}, u32[]{:S(2)}) collective-permute-start(bf16[800,128]{1,0:T(8,128)(2,1)S(1)} %get-tuple-element.31), channel_id=1, source_target_pairs={{4,12},{12,20},{20,28},{8,0},{16,8},{24,16},{5,13},{13,21},{21,29}... | collective-permute-start | bytes 614408 | tf_op jit(solution)/shard_map/ppermute | solution.py:382
  5.3 10.4 %collective-permute-start.2 = (bf16[800,128]{1,0:T(8,128)(2,1)S(1)}, bf16[800,128]{1,0:T(8,128)(2,1)S(1)}, u32[]{:S(2)}, u32[]{:S(2)}) collective-permute-start(bf16[800,128]{1,0:T(8,128)(2,1)S(1)} %get-tuple-element.32), channel_id=1, source_target_pairs={{4,8},{12,16},{20,24},{8,4},{16,12},{24,20},{5,9},{13,17},{21,25},... | collective-permute-start | bytes 614408 | tf_op jit(solution)/shard_map/ppermute | solution.py:381
  9.5 0.7 %copy-start.1 = (f32[4,32]{1,0:T(4,128)S(1)}, f32[4,32]{1,0:T(4,128)}, u32[]{:S(2)}) copy-start(f32[4,32]{1,0:T(4,128)} %w_out.1) | copy-start | bytes 1540
  10.2 0.7 %copy-start.2 = (f32[32]{0:T(128)S(1)}, f32[32]{0:T(128)}, u32[]{:S(2)}) copy-start(f32[32]{0:T(128)} %param.7) | copy-start | bytes 388
  10.9 0.7 %copy-start.3 = (f32[4]{0:T(128)S(1)}, f32[4]{0:T(128)}, u32[]{:S(2)}) copy-start(f32[4]{0:T(128)} %param.9) | copy-start | bytes 52
  15.8 3.0 %collective-permute-start.4 = (bf16[800,128]{1,0:T(8,128)(2,1)S(1)}, bf16[800,128]{1,0:T(8,128)(2,1)S(1)}, u32[]{:S(2)}, u32[]{:S(2)}) collective-permute-start(bf16[800,128]{1,0:T(8,128)(2,1)S(1)} %get-tuple-element.42), channel_id=1, source_target_pairs={{0,1},{1,0},{2,3},{3,2},{4,5},{5,4},{6,7},{7,6},{8,9},{9,8},{10,11... | collective-permute-start | bytes 614408 | tf_op jit(solution)/shard_map/ppermute | solution.py:403
  15.8 7.8 %collective-permute-start.3 = (bf16[800,128]{1,0:T(8,128)(2,1)S(1)}, bf16[800,128]{1,0:T(8,128)(2,1)S(1)}, u32[]{:S(2)}, u32[]{:S(2)}) collective-permute-start(bf16[800,128]{1,0:T(8,128)(2,1)S(1)} %get-tuple-element.36), channel_id=1, source_target_pairs={{1,2},{2,1},{5,6},{6,5},{9,10},{10,9},{13,14},{14,13},{17,18},{18,... | collective-permute-start | bytes 614408 | tf_op jit(solution)/shard_map/ppermute | solution.py:402
  25.0 4.3 %collective-permute-start.5 = (f32[4,32,128]{2,1,0:T(8,128)S(1)}, f32[4,32,128]{2,1,0:T(8,128)S(1)}, u32[]{:S(2)}, u32[]{:S(2)}) collective-permute-start(f32[4,32,128]{2,1,0:T(8,128)S(1)} %shade_rest.1), channel_id=1, source_target_pairs={{0,8},{4,12},{8,0},{12,4},{16,24},{20,28},{24,16},{28,20},{1,9},{5... | collective-permute-start | bytes 196616 | tf_op jit(solution)/shard_map/ppermute | solution.py:439
  29.5 5.8 %collective-permute-start.6 = (f32[4,32,128]{2,1,0:T(8,128)S(1)}, f32[4,32,128]{2,1,0:T(8,128)S(1)}, u32[]{:S(2)}, u32[]{:S(2)}) collective-permute-start(f32[4,32,128]{2,1,0:T(8,128)S(1)} %multiply_add_fusion.1), channel_id=1, source_target_pairs={{0,16},{4,20},{8,24},{12,28},{16,0},{20,4},{24,8},{28,12},{1,17},{... | collective-permute-start | bytes 196616 | tf_op jit(solution)/shard_map/ppermute | solution.py:439
  35.3 4.3 %collective-permute-start.7 = (f32[4,32,128]{2,1,0:T(8,128)S(1)}, f32[4,32,128]{2,1,0:T(8,128)S(1)}, u32[]{:S(2)}, u32[]{:S(2)}) collective-permute-start(f32[4,32,128]{2,1,0:T(8,128)S(1)} %multiply_add_fusion), channel_id=1, source_target_pairs={{0,4},{4,0},{8,12},{12,8},{16,20},{20,16},{24,28},{28,24},{1,5},{5... | collective-permute-start | bytes 196616 | tf_op jit(solution)/shard_map/ppermute | solution.py:443
